TPU v7x, 32 devices: a whole 2x2x4 slice. The times are simulated.
32 devices in a mesh: dp: 16 (over z, y, core), freq: 2 (over x).
Axes of the slice: x: 2, y: 2, z: 4, core: 2. Of those that a mesh axis runs over, the one named last changes fastest.
Arguments:
- pixels: bfloat16 [256, 256, 3328], P('dp', None, 'freq'), may hold values from -6 to 6
- band_group: int32 [256], P('dp'), may hold values from 0 to 1
- mask_order: int32 [256, 256], P('dp'), may hold values from 0 to 255, each once within a row
- visible_count: int32 [256], P('dp'), may hold values from 32 to 64, as said below
- scale_id: int32 [256], P('dp'), may hold values from 0 to 3
- patch_weight: bfloat16 [2, 3328, 1024], P(None, 'freq'), may hold values from -0.109375 to 0.109375
- enc_qkv: bfloat16 [1024, 3, 1024], P(None, None, 'freq'), may hold values from -0.1875 to 0.1875
- enc_out: bfloat16 [1024, 1024], P('freq'), may hold values from -0.375 to 0.375
- enc_up: bfloat16 [1024, 4096], P(None, 'freq'), may hold values from -0.1875 to 0.1875
- enc_down: bfloat16 [4096, 1024], P('freq'), may hold values from -0.09375 to 0.09375
- enc_gains: float32 [3, 1024], replicated, may hold values from 0.25 to 1.75
- enc_biases: float32 [3, 1024], replicated, may hold values from -3 to 3
- dec_embed: bfloat16 [1024, 512], replicated, may hold values from -0.1875 to 0.1875
- mask_token: float32 [512], replicated, may hold values from -5 to 5
- dec_qkv: bfloat16 [512, 3, 512], P(None, None, 'freq'), may hold values from -0.25 to 0.25
- dec_out: bfloat16 [512, 512], P('freq'), may hold values from -0.5 to 0.5
- dec_up: bfloat16 [512, 2048], P(None, 'freq'), may hold values from -0.25 to 0.25
- dec_down: bfloat16 [2048, 512], P('freq'), may hold values from -0.125 to 0.125
- dec_gains: float32 [3, 512], replicated, may hold values from 0.25 to 1.75
- dec_biases: float32 [3, 512], replicated, may hold values from -3 to 3
- head_weight: bfloat16 [512, 6656], P(None, 'freq'), may hold values from -0.25 to 0.25
- recon_cotangent: bfloat16 [256, 256, 6656], P('dp', None, 'freq'), may hold values from -6 to 6
Outputs:
- reconstructions: bfloat16 [256, 256, 6656], P('dp', None, 'freq')
- pixel_grad: float32 [256, 256, 3328], P('dp', None, 'freq')
- patch_weight_grad: float32 [2, 3328, 1024], P(None, 'freq')
- enc_qkv_grad: float32 [1024, 3, 1024], P(None, None, 'freq')
- enc_out_grad: float32 [1024, 1024], P('freq')
- enc_up_grad: float32 [1024, 4096], P(None, 'freq')
- enc_down_grad: float32 [4096, 1024], P('freq')
- enc_gains_grad: float32 [3, 1024], replicated
- enc_biases_grad: float32 [3, 1024], replicated
- dec_embed_grad: float32 [1024, 512], replicated
- mask_token_grad: float32 [512], replicated
- dec_qkv_grad: float32 [512, 3, 512], P(None, None, 'freq')
- dec_out_grad: float32 [512, 512], P('freq')
- dec_up_grad: float32 [512, 2048], P(None, 'freq')
- dec_down_grad: float32 [2048, 512], P('freq')
- dec_gains_grad: float32 [3, 512], replicated
- dec_biases_grad: float32 [3, 512], replicated
- head_weight_grad: float32 [512, 6656], P(None, 'freq')
Inputs may be any that keep to these rules, and one draw needn't show every extreme that they name: `visible_count`: every image has at least 32 and at most 64 visible patches, and in each aligned block of 16 images at least one image has 64.
All inputs are finite; a program needn't handle non-finite values.
Results may differ from a plain program's by a relative error of at most 0.035.
Values may be sent and summed in bfloat16 or wider, within the bound.
A program may use at most 512 MiB of HBM per device.

v0:
```python
import math

import jax
import jax.numpy as jnp
from jax import lax
from jax.sharding import PartitionSpec as P

D = 1024
HDIM = 64
DDEC = 512
DHDIM = 32
RGB_PIX = 768
SIDE = 16
NPATCH = 256
VIS = 64


HIGHEST = lax.Precision.HIGHEST
EPSILON = 1e-06
MASKED = -1e30


def layer_norm(values, scales, shifts):
    center = values - jnp.mean(values, -1, keepdims=True)
    spread = jnp.mean(center * center, -1, keepdims=True)
    return center * lax.rsqrt(spread + EPSILON) * scales + shifts


def position_code(patch_ids, ratios, features):
    quarter = features // 4
    index_f = jnp.arange(quarter, dtype=jnp.float32)
    frequencies = jnp.exp(index_f * (-math.log(10000.0) / quarter))
    row_angle = ((patch_ids // SIDE).astype(jnp.float32) * ratios)[..., None] * frequencies
    col_angle = ((patch_ids % SIDE).astype(jnp.float32) * ratios)[..., None] * frequencies
    return jnp.concatenate(
        [jnp.sin(row_angle), jnp.cos(row_angle), jnp.sin(col_angle), jnp.cos(col_angle)], -1
    )


def matmul(left, right):
    return jnp.dot(left, right, preferred_element_type=jnp.float32)


def matmul_tn(left, right):
    return lax.dot_general(
        left, right, (((0,), (0,)), ((), ())), preferred_element_type=jnp.float32
    )


def matmul_nt(left, right):
    return lax.dot_general(
        left, right, (((1,), (1,)), ((), ())), preferred_element_type=jnp.float32
    )


def gather_rows(values):
    return lax.all_gather(values, "freq", axis=0, tiled=True)


def gather_grads(values):
    return lax.all_gather(values, "freq", axis=0, tiled=True)


def reduce_rows(term_fn, row_total):
    return lax.psum_scatter(
        term_fn(jnp.int32(0), row_total * lax.axis_size("freq")),
        "freq",
        scatter_dimension=0,
        tiled=True,
    )


def reduce_grads(term_fn, row_total):
    return lax.psum_scatter(
        term_fn(jnp.int32(0), lax.axis_size("freq") * row_total).astype(jnp.bfloat16),
        "freq",
        scatter_dimension=0,
        tiled=True,
    ).astype(jnp.float32)


def attention_weights(queries, keys_all, valid_keys, shape4):
    scores = jnp.einsum(
        "bshd,bthd->bhst",
        queries.reshape(shape4),
        keys_all.reshape(shape4),
        preferred_element_type=jnp.float32,
    )
    scores = jnp.where(valid_keys[:, None, None, :], scores, MASKED)
    return jax.nn.softmax(scores, axis=-1)


def attend_forward(stream, scales, shifts, weight_qkv, weight_out, valid_keys, seq_len, head_size):
    normed = layer_norm(stream, scales, shifts).astype(jnp.bfloat16)
    gathered = gather_rows(normed)
    project = jnp.einsum("rw,wcn->rcn", gathered, weight_qkv, preferred_element_type=jnp.float32)
    local_width = weight_qkv.shape[2]
    shape4 = (gathered.shape[0] // seq_len, seq_len, local_width // head_size, head_size)
    queries = (project[:, 0] * head_size ** (-0.5)).astype(jnp.bfloat16)
    keys_all = project[:, 1].astype(jnp.bfloat16)
    values_all = project[:, 2].astype(jnp.bfloat16)
    weights = attention_weights(queries, keys_all, valid_keys, shape4)
    mixed_rows = jnp.einsum(
        "bhst,bthd->bshd",
        weights.astype(jnp.bfloat16),
        values_all.reshape(shape4),
        preferred_element_type=jnp.float32,
    )
    mixed_rows = mixed_rows.reshape(-1, local_width).astype(jnp.bfloat16)

    def attend_out_term(first_row, row_count):
        return matmul(mixed_rows, weight_out)

    row_total = stream.shape[0]
    branch = reduce_rows(attend_out_term, row_total)
    return (branch, (gathered, queries, keys_all, values_all, mixed_rows))


def attend_backward(
    grad_stream,
    stream,
    scales,
    shifts,
    weight_qkv,
    weight_out,
    valid_keys,
    seq_len,
    head_size,
    saved_parts,
):
    kept_rows, queries, keys_all, values_all, mixed_rows = saved_parts
    local_width = weight_qkv.shape[2]
    shape4 = (kept_rows.shape[0] // seq_len, seq_len, local_width // head_size, head_size)
    grad_low = grad_stream.astype(jnp.bfloat16)
    grad_out = gather_grads(grad_low)
    out_grad = matmul_tn(mixed_rows, grad_out)
    grad_mixed = matmul_nt(grad_out, weight_out).astype(jnp.bfloat16).reshape(shape4)
    weights = attention_weights(queries, keys_all, valid_keys, shape4)
    grad_values = jnp.einsum(
        "bhst,bshd->bthd",
        weights.astype(jnp.bfloat16),
        grad_mixed,
        preferred_element_type=jnp.float32,
    ).astype(jnp.bfloat16)
    grad_weights = jnp.einsum(
        "bshd,bthd->bhst",
        grad_mixed,
        values_all.reshape(shape4),
        preferred_element_type=jnp.float32,
    )
    grad_scores = (
        weights * (grad_weights - jnp.sum(weights * grad_weights, -1, keepdims=True))
    ).astype(jnp.bfloat16)
    grad_queries = jnp.einsum(
        "bhst,bthd->bshd", grad_scores, keys_all.reshape(shape4), preferred_element_type=jnp.float32
    )
    grad_queries = (grad_queries * head_size ** (-0.5)).astype(jnp.bfloat16)
    grad_keys = jnp.einsum(
        "bhst,bshd->bthd", grad_scores, queries.reshape(shape4), preferred_element_type=jnp.float32
    ).astype(jnp.bfloat16)
    grad_project = jnp.stack(
        [
            grad_queries.reshape(-1, local_width),
            grad_keys.reshape(-1, local_width),
            grad_values.reshape(-1, local_width),
        ],
        axis=1,
    )
    qkv_grad = jnp.einsum(
        "rw,rcn->wcn", kept_rows, grad_project, preferred_element_type=jnp.float32
    )

    def attend_input_term(first_row, row_count):
        return jnp.einsum(
            "rcn,wcn->rw", grad_project, weight_qkv, preferred_element_type=jnp.float32
        )

    row_total = stream.shape[0]
    grad_normed = reduce_grads(attend_input_term, row_total)
    _, pull_back = jax.vjp(layer_norm, stream, scales, shifts)
    grad_input, scale_grad, shift_grad = pull_back(grad_normed)
    return (grad_stream + grad_input, scale_grad, shift_grad, qkv_grad, out_grad)


def exact_gelu(pre_values):
    return jax.nn.gelu(pre_values, approximate=False)


def mlp_forward(stream, scales, shifts, weight_up, weight_down):
    normed = layer_norm(stream, scales, shifts).astype(jnp.bfloat16)
    gathered = gather_rows(normed)
    pre_act = matmul(gathered, weight_up)
    active = exact_gelu(pre_act).astype(jnp.bfloat16)

    def mlp_out_term(first_row, row_count):
        return matmul(active, weight_down)

    row_total = stream.shape[0]
    branch = reduce_rows(mlp_out_term, row_total)
    return (branch, (gathered, pre_act, active))


def mlp_backward(grad_stream, stream, scales, shifts, weight_up, weight_down, saved_parts):
    kept_rows, pre_act, active = saved_parts
    grad_low = grad_stream.astype(jnp.bfloat16)
    grad_out = gather_grads(grad_low)
    down_grad = matmul_tn(active, grad_out)
    grad_active = matmul_nt(grad_out, weight_down)
    _, pull_gelu = jax.vjp(exact_gelu, pre_act)
    grad_pre = pull_gelu(grad_active)[0].astype(jnp.bfloat16)
    up_grad = matmul_tn(kept_rows, grad_pre)

    def mlp_input_term(first_row, row_count):
        return matmul_nt(grad_pre, weight_up)

    row_total = stream.shape[0]
    grad_normed = reduce_grads(mlp_input_term, row_total)
    _, pull_back = jax.vjp(layer_norm, stream, scales, shifts)
    grad_input, scale_grad, shift_grad = pull_back(grad_normed)
    return (grad_stream + grad_input, scale_grad, shift_grad, up_grad, down_grad)


def block_forward(stream, scales, shifts, weights, valid_keys, seq_len, head_size):
    attn_out, attn_saved = attend_forward(
        stream, scales[0], shifts[0], weights[0], weights[1], valid_keys, seq_len, head_size
    )
    middle = stream + attn_out
    mlp_out, mlp_saved = mlp_forward(middle, scales[1], shifts[1], weights[2], weights[3])
    return (middle + mlp_out, (stream, middle, attn_saved, mlp_saved))


def block_backward(
    grad_stream, scales, shifts, weights, valid_keys, seq_len, head_size, saved_parts
):
    stream, middle, attn_saved, mlp_saved = saved_parts
    grad_middle, mlp_scale, mlp_shift, up_grad, down_grad = mlp_backward(
        grad_stream, middle, scales[1], shifts[1], weights[2], weights[3], mlp_saved
    )
    grad_input, attn_scale, attn_shift, qkv_grad, out_grad = attend_backward(
        grad_middle,
        stream,
        scales[0],
        shifts[0],
        weights[0],
        weights[1],
        valid_keys,
        seq_len,
        head_size,
        attn_saved,
    )
    return (
        grad_input,
        (attn_scale, mlp_scale),
        (attn_shift, mlp_shift),
        (qkv_grad, out_grad, up_grad, down_grad),
    )


def local(
    pixels,
    band_group,
    mask_order,
    visible_count,
    scale_id,
    patch_weight,
    enc_qkv,
    enc_out,
    enc_up,
    enc_down,
    enc_gains,
    enc_biases,
    dec_embed,
    mask_token,
    dec_qkv,
    dec_out,
    dec_up,
    dec_down,
    dec_gains,
    dec_biases,
    head_weight,
    recon_cotangent,
):
    shards = lax.axis_size("freq")
    position = lax.axis_index("freq")
    images = pixels.shape[0]
    local_images = images // shards
    pixel_width = pixels.shape[2]
    start_image = position * local_images
    local_rows = local_images * VIS
    dec_weights = (dec_qkv, dec_out, dec_up, dec_down)
    valid_dec = jnp.ones((images, NPATCH), dtype=bool)
    slot_ids = mask_order[:, :VIS]
    picked = jnp.take_along_axis(pixels, slot_ids[:, :, None], axis=1)
    columns = position * pixel_width + jnp.arange(pixel_width)
    multi_band = band_group == 0
    keep_band = multi_band[:, None] | (columns[None, :] < RGB_PIX)
    zero_value = jnp.zeros((), jnp.bfloat16)
    picked_multi = jnp.where(
        (keep_band & multi_band[:, None])[:, None, :], picked, zero_value
    ).reshape(images * VIS, pixel_width)
    picked_rgb = jnp.where(
        (keep_band & ~multi_band[:, None])[:, None, :], picked, zero_value
    ).reshape(images * VIS, pixel_width)
    embedded = lax.psum_scatter(
        matmul(picked_multi, patch_weight[0]) + matmul(picked_rgb, patch_weight[1]),
        "freq",
        scatter_dimension=0,
        tiled=True,
    )
    my_slots = lax.dynamic_slice_in_dim(slot_ids, start_image, local_images, 0)
    my_count = lax.dynamic_slice_in_dim(visible_count, start_image, local_images, 0)
    my_scale = lax.dynamic_slice_in_dim(scale_id, start_image, local_images, 0)
    ratios = jnp.exp2(my_scale.astype(jnp.float32) - 1.0)[:, None]
    stream = embedded + position_code(my_slots, ratios, D).reshape(local_rows, D)
    valid_enc = jnp.arange(VIS)[None, :] < visible_count[:, None]
    enc_weights = (enc_qkv, enc_out, enc_up, enc_down)
    stream, enc_saved = block_forward(
        stream, enc_gains, enc_biases, enc_weights, valid_enc, VIS, HDIM
    )
    latent = layer_norm(stream, enc_gains[2], enc_biases[2]).astype(jnp.bfloat16)
    lifted = matmul(latent, dec_embed)
    live_mask = (jnp.arange(VIS)[None, :] < my_count[:, None]).astype(jnp.float32)
    select = (my_slots[:, :, None] == jnp.arange(NPATCH)[None, None, :]).astype(
        jnp.float32
    ) * live_mask[:, :, None]
    shown_mask = jnp.sum(select, axis=1)[:, :, None]
    decoded = (
        jnp.einsum(
            "bsp,bse->bpe", select, lifted.reshape(local_images, VIS, DDEC), precision=HIGHEST
        )
        + (1.0 - shown_mask) * mask_token
    )
    decoded = decoded + position_code(jnp.arange(NPATCH)[None, :], ratios, DDEC)
    decoded = decoded.reshape(local_images * NPATCH, DDEC)
    decoded, dec_saved = block_forward(
        decoded, dec_gains, dec_biases, dec_weights, valid_dec, NPATCH, DHDIM
    )
    final_rows = layer_norm(decoded, dec_gains[2], dec_biases[2]).astype(jnp.bfloat16)
    final_all = gather_rows(final_rows)
    reconstructions = (
        matmul(final_all, head_weight).astype(jnp.bfloat16).reshape(images, NPATCH, -1)
    )
    cotangent = recon_cotangent.reshape(images * NPATCH, -1)
    head_grad = matmul_tn(final_all, cotangent)

    def head_term(first_row, row_count):
        return matmul_nt(cotangent, head_weight)

    grad_final = reduce_grads(head_term, local_images * NPATCH)
    _, pull_final = jax.vjp(layer_norm, decoded, dec_gains[2], dec_biases[2])
    grad_decoded, dec_last_scale, dec_last_shift = pull_final(grad_final)
    grad_decoded, dec_scales, dec_shifts, dec_grads = block_backward(
        grad_decoded, dec_gains, dec_biases, dec_weights, valid_dec, NPATCH, DHDIM, dec_saved
    )
    grad_grid = grad_decoded.reshape(local_images, NPATCH, DDEC)
    mask_grad = jnp.sum((1.0 - shown_mask) * grad_grid, axis=(0, 1))
    grad_lifted = (
        jnp.einsum("bsp,bpe->bse", select, grad_grid, precision=HIGHEST)
        .reshape(local_rows, DDEC)
        .astype(jnp.bfloat16)
    )
    embed_grad = matmul_tn(latent, grad_lifted)
    grad_latent = matmul_nt(grad_lifted, dec_embed)
    dec_gain_grad = jnp.stack([dec_scales[0], dec_scales[1], dec_last_scale])
    dec_bias_grad = jnp.stack([dec_shifts[0], dec_shifts[1], dec_last_shift])
    _, pull_latent = jax.vjp(layer_norm, stream, enc_gains[2], enc_biases[2])
    grad_stream, enc_last_scale, enc_last_shift = pull_latent(grad_latent)
    grad_stream, enc_scales, enc_shifts, enc_grads = block_backward(
        grad_stream, enc_gains, enc_biases, enc_weights, valid_enc, VIS, HDIM, enc_saved
    )
    grad_embedded = gather_grads(grad_stream.astype(jnp.bfloat16))
    patch_grad = jnp.stack(
        [matmul_tn(picked_multi, grad_embedded), matmul_tn(picked_rgb, grad_embedded)]
    )
    back_multi = matmul_nt(grad_embedded, patch_weight[0]).reshape(images, VIS, pixel_width)
    back_rgb = matmul_nt(grad_embedded, patch_weight[1]).reshape(images, VIS, pixel_width)
    grad_picked = jnp.where(multi_band[:, None, None], back_multi, back_rgb) * keep_band[
        :, None, :
    ].astype(jnp.float32)
    pixel_grad = (
        jnp.zeros((images, NPATCH, pixel_width), jnp.float32)
        .at[jnp.arange(images)[:, None], slot_ids]
        .set(grad_picked)
    )
    enc_gain_grad = jnp.stack([enc_scales[0], enc_scales[1], enc_last_scale])
    enc_bias_grad = jnp.stack([enc_shifts[0], enc_shifts[1], enc_last_shift])
    summed_all = (
        lax.psum(patch_grad.astype(jnp.bfloat16), "dp").astype(jnp.float32),
        lax.psum(enc_grads[0].astype(jnp.bfloat16), "dp").astype(jnp.float32),
        lax.psum(enc_grads[1].astype(jnp.bfloat16), "dp").astype(jnp.float32),
        lax.psum(enc_grads[2].astype(jnp.bfloat16), "dp").astype(jnp.float32),
        lax.psum(enc_grads[3].astype(jnp.bfloat16), "dp").astype(jnp.float32),
        lax.psum(dec_grads[0].astype(jnp.bfloat16), "dp").astype(jnp.float32),
        lax.psum(dec_grads[1].astype(jnp.bfloat16), "dp").astype(jnp.float32),
        lax.psum(dec_grads[2].astype(jnp.bfloat16), "dp").astype(jnp.float32),
        lax.psum(dec_grads[3].astype(jnp.bfloat16), "dp").astype(jnp.float32),
        lax.psum(head_grad.astype(jnp.bfloat16), "dp").astype(jnp.float32),
    )
    shared_all = lax.psum(
        (enc_gain_grad, enc_bias_grad, embed_grad, mask_grad, dec_gain_grad, dec_bias_grad),
        ("dp", "freq"),
    )
    enc_summed = summed_all[:5]
    dec_summed = summed_all[5:]
    enc_shared = shared_all[:2]
    dec_shared = shared_all[2:]
    return (
        reconstructions,
        pixel_grad,
        enc_summed[0],
        enc_summed[1],
        enc_summed[2],
        enc_summed[3],
        enc_summed[4],
        enc_shared[0],
        enc_shared[1],
        dec_shared[0],
        dec_shared[1],
        dec_summed[0],
        dec_summed[1],
        dec_summed[2],
        dec_summed[3],
        dec_shared[2],
        dec_shared[3],
        dec_summed[4],
    )


def solution(mesh):
    return jax.shard_map(
        local,
        mesh=mesh,
        in_specs=(
            P("dp", None, "freq"),
            P("dp"),
            P("dp", None),
            P("dp"),
            P("dp"),
            P(None, "freq", None),
            P(None, None, "freq"),
            P("freq", None),
            P(None, "freq"),
            P("freq", None),
            P(),
            P(),
            P(),
            P(),
            P(None, None, "freq"),
            P("freq", None),
            P(None, "freq"),
            P("freq", None),
            P(),
            P(),
            P(None, "freq"),
            P("dp", None, "freq"),
        ),
        out_specs=(
            P("dp", None, "freq"),
            P("dp", None, "freq"),
            P(None, "freq", None),
            P(None, None, "freq"),
            P("freq", None),
            P(None, "freq"),
            P("freq", None),
            P(),
            P(),
            P(),
            P(),
            P(None, None, "freq"),
            P("freq", None),
            P(None, "freq"),
            P("freq", None),
            P(),
            P(),
            P(None, "freq"),
        ),
        check_vma=False,
    )
```

profile of v0, /device:TPU:0, one launch (start us, length us, event | category | flops | bytes accessed | tf_op | source)
XLA Modules:
  0.0 2295.8 jit_solution(11122833873274805604)
XLA Ops:
  9.7 23.8 %gather_fusion = bf16[1024,1664]{1,0:T(8,128)(2,1)} fusion(bf16[16,256,1664]{2,1,0:T(8,128)(2,1)} %param.22, s32[1024]{0:T(1024)S(1)} %reshape.713), kind=kCustom, calls=%fused_computation | custom fusion | bytes 6823936 | tf_op jit(solution)/shard_map/jit(take_along_axis)/gather | solution.py:293
  42.2 5.5 fusion.69
  49.4 5.4 multiply_sine_fusion.3
  54.8 50.1 %reduce-scatter.11.cloned.1.call-done = f32[512,1024]{1,0:T(8,128)} async-done(((f32[1024,1024]{1,0:T(8,128)}), f32[512,1024]{1,0:T(8,128)}) %reduce-scatter.11.cloned.1.call-update) | async-done | bytes 2097168 | tf_op jit(solution)/shard_map/reduce_scatter | solution.py:304
  110.4 32.8 %all-gather.11.cloned.1.call-done = bf16[1024,1024]{1,0:T(8,128)(2,1)} async-done(((bf16[512,1024]{1,0:T(8,128)(2,1)}), bf16[1024,1024]{1,0:T(8,128)(2,1)}) %all-gather.11.cloned.1.call-update) | async-done | bytes 2097168 | tf_op jit(solution)/shard_map/all_gather | solution.py:57
  143.3 8.6 fusion.159
  176.1 6.3 fusion.160
  182.4 5.0 convert_bitcast_fusion.5
  201.0 53.9 %reduce-scatter.13.cloned.1.call-done = f32[512,1024]{1,0:T(8,128)} async-done(((f32[1024,1024]{1,0:T(8,128)}), f32[512,1024]{1,0:T(8,128)}) %reduce-scatter.13.cloned.1.call-update) | async-done | bytes 2097168 | tf_op jit(solution)/shard_map/reduce_scatter | solution.py:65
  260.2 33.2 %all-gather.13.cloned.1.call-done = bf16[1024,1024]{1,0:T(8,128)(2,1)} async-done(((bf16[512,1024]{1,0:T(8,128)(2,1)}), bf16[1024,1024]{1,0:T(8,128)(2,1)}) %all-gather.13.cloned.1.call-update) | async-done | bytes 2097168 | tf_op jit(solution)/shard_map/all_gather | solution.py:57
  293.4 25.7 %multiply_convert_fusion.2 = (bf16[1024,2048]{1,0:T(8,128)(2,1)S(1)}, f32[1024,2048]{1,0:T(8,128)}, f32[1024,2048]{1,0:T(8,128)}) fusion(bf16[1024,1024]{1,0:T(8,128)(2,1)} %all-gather.13.cloned.1.call-done, bf16[1024,2048]{1,0:T(8,128)(2,1)} %param.30), kind=kOutput, calls=%fused_computation.36 | convolution fusion | flops 4431282176 | bytes 27262976 | tf_op jit(solution)/shard_map/dot_general | solution.py:41
  321.3 6.0 fusion.169
  329.8 8.7 multiply_sine_fusion.1
  338.5 43.3 %reduce-scatter.15.cloned.1.call-done = f32[512,1024]{1,0:T(8,128)} async-done(((f32[1024,1024]{1,0:T(8,128)}), f32[512,1024]{1,0:T(8,128)}) %reduce-scatter.15.cloned.1.call-update) | async-done | bytes 2097168 | tf_op jit(solution)/shard_map/reduce_scatter | solution.py:65
  397.6 56.6 %all-gather.15.cloned.1.call-done = bf16[4096,512]{1,0:T(8,128)(2,1)} async-done(((bf16[2048,512]{1,0:T(8,128)(2,1)}), bf16[4096,512]{1,0:T(8,128)(2,1)}) %all-gather.15.cloned.1.call-update) | async-done | bytes 4194320 | tf_op jit(solution)/shard_map/all_gather | solution.py:57
  454.2 10.6 fusion.162
  494.0 17.9 fusion.163
  511.9 15.7 convert_bitcast_fusion.4
  537.6 99.3 %reduce-scatter.17.cloned.1.call-done = f32[2048,512]{1,0:T(8,128)} async-done(((f32[4096,512]{1,0:T(8,128)}), f32[2048,512]{1,0:T(8,128)}) %reduce-scatter.17.cloned.1.call-update) | async-done | bytes 4194320 | tf_op jit(solution)/shard_map/reduce_scatter | solution.py:65
  645.3 56.9 %all-gather.17.cloned.1.call-done = bf16[4096,512]{1,0:T(8,128)(2,1)} async-done(((bf16[2048,512]{1,0:T(8,128)(2,1)}), bf16[4096,512]{1,0:T(8,128)(2,1)}) %all-gather.17.cloned.1.call-update) | async-done | bytes 4194320 | tf_op jit(solution)/shard_map/all_gather | solution.py:57
  702.2 43.1 %multiply_convert_fusion.1 = (bf16[4096,1024]{1,0:T(8,128)(2,1)S(1)}, f32[4096,1024]{1,0:T(8,128)}, f32[4096,1024]{1,0:T(8,128)}) fusion(bf16[4096,512]{1,0:T(8,128)(2,1)} %all-gather.17.cloned.1.call-done, bf16[512,1024]{1,0:T(8,128)(2,1)} %param.38), kind=kOutput, calls=%fused_computation.11 | convolution fusion | flops 4567597056 | bytes 47185920 | tf_op jit(solution)/shard_map/dot_general | solution.py:41
  748.6 6.9 fusion.172
  755.5 21.0 convolution_convert_fusion.2
  776.5 78.3 %reduce-scatter.19.cloned.1.call-done = f32[2048,512]{1,0:T(8,128)} async-done(((f32[4096,512]{1,0:T(8,128)}), f32[2048,512]{1,0:T(8,128)}) %reduce-scatter.19.cloned.1.call-update) | async-done | bytes 4194320 | tf_op jit(solution)/shard_map/reduce_scatter | solution.py:65
  861.7 50.3 %reduce-scatter.21.cloned.1.call-done = bf16[2048,512]{1,0:T(8,128)(2,1)} async-done(((bf16[4096,512]{1,0:T(8,128)(2,1)}), bf16[2048,512]{1,0:T(8,128)(2,1)}) %reduce-scatter.21.cloned.1.call-update) | async-done | bytes 2097168 | tf_op jit(solution)/shard_map/reduce_scatter | solution.py:74
  923.7 56.9 %all-gather.21.cloned.1.call-done = bf16[4096,512]{1,0:T(8,128)(2,1)} async-done(((bf16[2048,512]{1,0:T(8,128)(2,1)}), bf16[4096,512]{1,0:T(8,128)(2,1)}) %all-gather.21.cloned.1.call-update) | async-done | bytes 4194320 | tf_op jit(solution)/shard_map/all_gather | solution.py:61
  980.6 20.5 add_convert_fusion
  1001.1 10.2 convolution_convert_fusion.1
  1011.4 54.4 %reduce-scatter.23.cloned.1.call-done = bf16[2048,512]{1,0:T(8,128)(2,1)} async-done(((bf16[4096,512]{1,0:T(8,128)(2,1)}), bf16[2048,512]{1,0:T(8,128)(2,1)}) %reduce-scatter.23.cloned.1.call-update) | async-done | bytes 2097168 | tf_op jit(solution)/shard_map/reduce_scatter | solution.py:74
  1065.8 5.1 fusion.30
  1076.5 56.9 %all-gather.23.cloned.1.call-done = bf16[4096,512]{1,0:T(8,128)(2,1)} async-done(((bf16[2048,512]{1,0:T(8,128)(2,1)}), bf16[4096,512]{1,0:T(8,128)(2,1)}) %all-gather.23.cloned.1.call-update) | async-done | bytes 4194320 | tf_op jit(solution)/shard_map/all_gather | solution.py:61
  1145.0 23.8 %multiply_reduce_fusion = (f32[16,8,256]{2,1,0:T(8,128)}, f32[16,8,256,256]{2,3,1,0:T(8,128)}) fusion(f32[16,8,256,256]{2,3,1,0:T(8,128)} %get-tuple-element.135, f32[16,8,256]{2,1,0:T(8,128)S(1)} %copy-done.59, bf16[16,256,8,32]{1,0,3,2:T(8,128)(2,1)S(1)} %bitcast.276, bf16[16,256,8,32]{1,0,3,2:T(8,128)(2,1)S(1)} %bitcast.277), kind=kOutput, calls=%fused_computation.5 | convolution fusion | flops 562003968 | bytes 71565312 | tf_op jit(solution)/shard_map/bshd,bthd->bhst/dot_general | solution.py:145
  1168.8 27.8 %multiply_convert_fusion = bf16[16,8,256,256]{2,3,1,0:T(8,128)(2,1)} fusion(f32[16,8,256,256]{2,3,1,0:T(8,128)} %get-tuple-element.138, f32[16,8,256]{2,1,0:T(8,128)} %get-tuple-element.137, f32[16,8,256,256]{2,3,1,0:T(8,128)} %get-tuple-element.135, f32[16,8,256]{2,1,0:T(8,128)S(1)} %copy-done.59), kind=kLoop, calls=%fused_computation.4 | loop fusion | flops 33554432 | bytes 84148224 | tf_op jit(solution)/shard_map/convert_element_type | solution.py:153
  1196.6 10.7 fusion.84
  1207.3 12.7 convert_bitcast_fusion.3
  1220.0 15.7 convert_bitcast_fusion.2
  1273.0 8.5 bitcast_convert_fusion
  1282.2 53.8 %reduce-scatter.25.cloned.1.call-done = bf16[2048,512]{1,0:T(8,128)(2,1)} async-done(((bf16[4096,512]{1,0:T(8,128)(2,1)}), bf16[2048,512]{1,0:T(8,128)(2,1)}) %reduce-scatter.25.cloned.1.call-update) | async-done | bytes 2097168 | tf_op jit(solution)/shard_map/reduce_scatter | solution.py:74
  1336.0 5.3 convert_reduce_fusion
  1345.8 5.4 multiply_reduce_fusion.1
  1358.8 33.2 %all-gather.25.cloned.1.call-done = bf16[1024,1024]{1,0:T(8,128)(2,1)} async-done(((bf16[512,1024]{1,0:T(8,128)(2,1)}), bf16[1024,1024]{1,0:T(8,128)(2,1)}) %all-gather.25.cloned.1.call-update) | async-done | bytes 2097168 | tf_op jit(solution)/shard_map/all_gather | solution.py:61
  1392.0 12.8 add_convert_fusion.1
  1406.9 5.7 convolution_convert_fusion.10
  1413.4 5.5 bitcast_select_fusion.1
  1418.9 25.7 %reduce-scatter.27.cloned.1.call-done = bf16[512,1024]{1,0:T(8,128)(2,1)} async-done(((bf16[1024,1024]{1,0:T(8,128)(2,1)}), bf16[512,1024]{1,0:T(8,128)(2,1)}) %reduce-scatter.27.cloned.1.call-update) | async-done | bytes 1048592 | tf_op jit(solution)/shard_map/reduce_scatter | solution.py:74
  1452.8 11.4 convolution_convert_fusion.11
  1464.2 38.6 %all-gather.19.cloned.1.call-done = bf16[4096,512]{1,0:T(8,128)(2,1)} async-done(((bf16[2048,512]{1,0:T(8,128)(2,1)}), bf16[4096,512]{1,0:T(8,128)(2,1)}) %all-gather.19.cloned.1.call-update) | async-done | bytes 4194320 | tf_op jit(solution)/shard_map/all_gather | solution.py:57
  1502.9 23.4 %convolution_convert_fusion.3 = bf16[512,3328]{1,0:T(8,128)(2,1)} fusion(bf16[4096,512]{1,0:T(8,128)(2,1)} %all-gather.19.cloned.1.call-done, bf16[4096,3328]{1,0:T(8,128)(2,1)} %bitcast.324), kind=kOutput, calls=%fused_computation.69 | convolution fusion | flops 13960347648 | bytes 34865152 | tf_op jit(solution)/shard_map/dot_general | solution.py:45
  1526.2 11.8 all-gather.27.cloned.1.call-done
  1550.5 5.5 convert_bitcast_fusion
  1597.6 10.3 convolution_convert_fusion.12
  1615.3 6.1 convolution_convert_fusion.7
  1621.4 7.7 reduce-scatter.29.cloned.1.call-done
  1637.5 9.6 convolution_convert_fusion.8
  1654.3 16.2 all-gather.29.cloned.1.call-done
  1670.5 6.5 fusion.45
  1685.5 22.6 convolution_convert_fusion
  1710.5 42.5 %all-reduce = (f32[3,1024]{1,0:T(4,128)}, f32[3,1024]{1,0:T(4,128)}, f32[512]{0:T(512)}, f32[3,512]{1,0:T(4,128)}, f32[3,512]{1,0:T(4,128)}) all-reduce(f32[3,1024]{1,0:T(4,128)S(1)} %pad_maximum_fusion.6, f32[3,1024]{1,0:T(4,128)S(1)} %pad_maximum_fusion.7, ...), channel_id=1, replica_groups=mesh['dp'=16,'freq'=2] {'dp','freq'}, use_global_device_ids=true, to_apply=%region_50.51 | all-reduce | flops 9728 | bytes 77824 | tf_op jit(solution)/shard_map/psum | solution.py:399
  1753.0 6.8 fusion.39
  1759.9 8.0 select_multiply_fusion
  1767.9 19.1 scatter_custom_fusion
  1787.0 358.7 %all-reduce.7.cloned.1.call-done = (bf16[2,1664,1024]{2,1,0:T(8,128)(2,1)}, bf16[1024,3,512]{2,0,1:T(8,128)(2,1)}, bf16[512,1024]{1,0:T(8,128)(2,1)}, bf16[1024,...) async-done(((bf16[2,1664,1024]{2,1,0:T(8,128)(2,1)}, ...) | async-done | bytes 25952272 | tf_op jit(solution)/shard_map/psum | solution.py:388
  2145.8 9.9 convert_element_type.358
  2178.5 107.3 %all-reduce.5.cloned.1.call-done = f32[1024,512]{1,0:T(8,128)} async-done(((f32[1024,512]{1,0:T(8,128)}), f32[1024,512]{1,0:T(8,128)}) %all-reduce.5.cloned.1.call-update) | async-done | bytes 2097168 | tf_op jit(solution)/shard_map/psum | solution.py:399
  (530 shorter events, 342.2 us)
Async XLA Ops:
  7.2 748.3 %copy-start = (bf16[512,3328]{1,0:T(8,128)(2,1)S(1)}, bf16[512,3328]{1,0:T(8,128)(2,1)}, u32[]{:S(2)}) copy-start(bf16[512,3328]{1,0:T(8,128)(2,1)} %param.42) | copy-start | bytes 10223620
  7.2 97.6 %reduce-scatter.11.cloned.1.call-start = ((), (), s32[]{:S(2)}) async-start(), calls=%async_computation.10 | async-start | bytes 6291456 | tf_op jit(solution)/shard_map/reduce_scatter | solution.py:304
  8.9 25.3 %copy-start.119 = (pred[16,64]{1,0:T(8,128)(4,1)}, pred[16,64]{1,0:T(8,128)(4,1)S(1)}, u32[]{:S(2)}) copy-start(pred[16,64]{1,0:T(8,128)(4,1)S(1)} %compare_and_fusion) | copy-start | bytes 3076
  9.6 23.9 %copy-start.137 = (pred[16]{0:T(512)(128)(4,1)}, pred[16]{0:T(512)(128)(4,1)S(1)}, u32[]{:S(2)}) copy-start(pred[16]{0:T(512)(128)(4,1)S(1)} %get-tuple-element.119) | copy-start | bytes 52
  47.7 95.6 %all-gather.11.cloned.1.call-start = ((), (), s32[]{:S(2)}) async-start(), calls=%async_computation.11 | async-start | bytes 3145728 | tf_op jit(solution)/shard_map/all_gather | solution.py:57
  49.1 338.2 %copy-start.86 = (s32[8,64]{1,0:T(8,128)}, s32[8,64]{1,0:T(8,128)S(1)}, u32[]{:S(2)}) copy-start(s32[8,64]{1,0:T(8,128)S(1)} %get-tuple-element.78) | copy-start | bytes 6148
  49.3 58.4 %copy-start.77 = (f32[1,1024]{1,0:T(1,128)}, f32[1,1024]{1,0:T(1,128)S(1)}, u32[]{:S(2)}) copy-start(f32[1,1024]{1,0:T(1,128)S(1)} %get-tuple-element.91) | copy-start | bytes 12292
  49.3 208.5 %copy-start.90 = (f32[1,1024]{1,0:T(1,128)}, f32[1,1024]{1,0:T(1,128)S(1)}, u32[]{:S(2)}) copy-start(f32[1,1024]{1,0:T(1,128)S(1)} %get-tuple-element.92) | copy-start | bytes 12292
  49.3 335.4 %copy-start.99 = (f32[1,1024]{1,0:T(1,128)}, f32[1,1024]{1,0:T(1,128)S(1)}, u32[]{:S(2)}) copy-start(f32[1,1024]{1,0:T(1,128)S(1)} %get-tuple-element.90) | copy-start | bytes 12292
  107.7 44.2 %copy-start.113 = (f32[512]{0:T(512)}, f32[512]{0:T(512)S(1)}, u32[]{:S(2)}) copy-start(f32[512]{0:T(512)S(1)} %multiply_reduce_fusion.10) | copy-start | bytes 6148
  107.7 44.2 %copy-start.108 = (f32[512]{0:T(512)}, f32[512]{0:T(512)S(1)}, u32[]{:S(2)}) copy-start(f32[512]{0:T(512)S(1)} %fusion.121) | copy-start | bytes 6148
  110.0 144.9 %reduce-scatter.13.cloned.1.call-start = ((), (), s32[]{:S(2)}) async-start(), calls=%async_computation.12 | async-start | bytes 6291456 | tf_op jit(solution)/shard_map/reduce_scatter | solution.py:65
  200.4 93.0 %all-gather.13.cloned.1.call-start = ((), (), s32[]{:S(2)}) async-start(), calls=%async_computation.13 | async-start | bytes 3145728 | tf_op jit(solution)/shard_map/all_gather | solution.py:57
  257.4 61.7 %copy-start.94 = (f32[512]{0:T(512)}, f32[512]{0:T(512)S(1)}, u32[]{:S(2)}) copy-start(f32[512]{0:T(512)S(1)} %broadcast_multiply_fusion.6) | copy-start | bytes 6148
  257.8 61.4 %copy-start.115 = (f32[512]{0:T(512)}, f32[512]{0:T(512)S(1)}, u32[]{:S(2)}) copy-start(f32[512]{0:T(512)S(1)} %multiply_reduce_fusion.9) | copy-start | bytes 6148
  257.8 61.4 %copy-start.102 = (f32[512]{0:T(512)}, f32[512]{0:T(512)S(1)}, u32[]{:S(2)}) copy-start(f32[512]{0:T(512)S(1)} %fusion.122) | copy-start | bytes 6148
  260.1 121.6 %reduce-scatter.15.cloned.1.call-start = ((), (), s32[]{:S(2)}) async-start(), calls=%async_computation.14 | async-start | bytes 6291456 | tf_op jit(solution)/shard_map/reduce_scatter | solution.py:65
  293.4 27.9 %copy-start.143 = (bf16[2048,1024]{1,0:T(8,128)(2,1)S(1)}, bf16[2048,1024]{1,0:T(8,128)(2,1)}, u32[]{:S(2)}) copy-start(bf16[2048,1024]{1,0:T(8,128)(2,1)} %param.31) | copy-start | bytes 12582916
  327.3 126.9 %all-gather.15.cloned.1.call-start = ((), (), s32[]{:S(2)}) async-start(), calls=%async_computation.15 | async-start | bytes 6291456 | tf_op jit(solution)/shard_map/all_gather | solution.py:57
  327.7 59.6 %copy-start.96 = (f32[8,64]{1,0:T(8,128)}, f32[8,64]{1,0:T(8,128)S(1)}, u32[]{:S(2)}) copy-start(f32[8,64]{1,0:T(8,128)S(1)} %fusion.118) | copy-start | bytes 6148
  328.6 66.1 %copy-start.92 = (f32[1,512]{1,0:T(1,128)}, f32[1,512]{1,0:T(1,128)S(1)}, u32[]{:S(2)}) copy-start(f32[1,512]{1,0:T(1,128)S(1)} %get-tuple-element.103) | copy-start | bytes 6148
  328.6 314.3 %copy-start.106 = (f32[1,512]{1,0:T(1,128)}, f32[1,512]{1,0:T(1,128)S(1)}, u32[]{:S(2)}) copy-start(f32[1,512]{1,0:T(1,128)S(1)} %get-tuple-element.104) | copy-start | bytes 6148
  397.3 239.6 %reduce-scatter.17.cloned.1.call-start = ((), (), s32[]{:S(2)}) async-start(), calls=%async_computation.16 | async-start | bytes 12582912 | tf_op jit(solution)/shard_map/reduce_scatter | solution.py:65
  511.9 15.7 copy-start.58
  537.5 164.6 %all-gather.17.cloned.1.call-start = ((), (), s32[]{:S(2)}) async-start(), calls=%async_computation.17 | async-start | bytes 6291456 | tf_op jit(solution)/shard_map/all_gather | solution.py:57
  645.3 209.6 %reduce-scatter.19.cloned.1.call-start = ((), (), s32[]{:S(2)}) async-start(), calls=%async_computation.18 | async-start | bytes 12582912 | tf_op jit(solution)/shard_map/reduce_scatter | solution.py:65
  702.2 46.4 %copy-start.151 = (bf16[1024,512]{1,0:T(8,128)(2,1)S(1)}, bf16[1024,512]{1,0:T(8,128)(2,1)}, u32[]{:S(2)}) copy-start(bf16[1024,512]{1,0:T(8,128)(2,1)} %param.39) | copy-start | bytes 3145732
  755.5 156.6 %reduce-scatter.21.cloned.1.call-start = ((), (), s32[]{:S(2)}) async-start(), calls=%async_computation.20 | async-start | bytes 6291456 | tf_op jit(solution)/shard_map/reduce_scatter | solution.py:74
  776.5 204.1 %all-gather.21.cloned.1.call-start = ((), (), s32[]{:S(2)}) async-start(), calls=%async_computation.21 | async-start | bytes 6291456 | tf_op jit(solution)/shard_map/all_gather | solution.py:61
  858.8 53.2 %copy-start.110 = (f32[1,512]{1,0:T(1,128)S(1)}, f32[1,512]{1,0:T(1,128)}, u32[]{:S(2)}) copy-start(f32[1,512]{1,0:T(1,128)} %get-tuple-element.102) | copy-start | bytes 6148
  861.7 55.3 %copy-start.132 = (f32[1,512]{1,0:T(1,128)S(1)}, f32[1,512]{1,0:T(1,128)}, u32[]{:S(2)}) copy-start(f32[1,512]{1,0:T(1,128)} %get-tuple-element.105) | copy-start | bytes 6148
  923.7 142.1 %reduce-scatter.23.cloned.1.call-start = ((), (), s32[]{:S(2)}) async-start(), calls=%async_computation.22 | async-start | bytes 6291456 | tf_op jit(solution)/shard_map/reduce_scatter | solution.py:74
  1011.3 54.5 %copy-start.71 = (f32[2048]{0:T(1024)S(1)}, f32[2048]{0:T(1024)}, u32[]{:S(2)}) copy-start(f32[2048]{0:T(1024)} %copy-done.70) | copy-start | bytes 24580
  1011.3 54.5 %copy-start.75 = (f32[2048]{0:T(1024)S(1)}, f32[2048]{0:T(1024)}, u32[]{:S(2)}) copy-start(f32[2048]{0:T(1024)} %copy-done.74) | copy-start | bytes 24580
  1011.3 54.5 %copy-start.107 = (f32[1,512]{1,0:T(1,128)S(1)}, f32[1,512]{1,0:T(1,128)}, u32[]{:S(2)}) copy-start(f32[1,512]{1,0:T(1,128)} %copy-done.106) | copy-start | bytes 6148
  1011.3 59.5 %copy-start.80 = (f32[2048]{0:T(1024)S(1)}, f32[2048]{0:T(1024)}, u32[]{:S(2)}) copy-start(f32[2048]{0:T(1024)} %copy-done.79) | copy-start | bytes 24580
  1011.3 122.0 %all-gather.23.cloned.1.call-start = ((), (), s32[]{:S(2)}) async-start(), calls=%async_computation.23 | async-start | bytes 6291456 | tf_op jit(solution)/shard_map/all_gather | solution.py:61
  1076.4 259.6 %reduce-scatter.25.cloned.1.call-start = ((), (), s32[]{:S(2)}) async-start(), calls=%async_computation.24 | async-start | bytes 6291456 | tf_op jit(solution)/shard_map/reduce_scatter | solution.py:74
  1145.0 23.8 %copy-start.48 = (bf16[32,8,16,256]{3,2,1,0:T(8,128)(2,1)}, bf16[32,8,16,256]{3,2,1,0:T(8,128)(2,1)S(1)}, u32[]{:S(2)}) copy-start(bf16[32,8,16,256]{3,2,1,0:T(8,128)(2,1)S(1)} %copy.125) | copy-start | bytes 6291460
  1281.5 54.5 %copy-start.69 = (f32[1,2,8,128]{3,1,2,0:T(2,128)S(1)}, f32[1,2,8,128]{3,1,2,0:T(2,128)}, u32[]{:S(2)}) copy-start(f32[1,2,8,128]{3,1,2,0:T(2,128)} %copy-done.68) | copy-start | bytes 24580
  1281.5 54.5 %copy-start.93 = (f32[1,512]{1,0:T(1,128)S(1)}, f32[1,512]{1,0:T(1,128)}, u32[]{:S(2)}) copy-start(f32[1,512]{1,0:T(1,128)} %copy-done.92) | copy-start | bytes 6148
  1281.5 59.8 %copy-start.83 = (f32[1,2,8,128]{3,1,2,0:T(2,128)S(1)}, f32[1,2,8,128]{3,1,2,0:T(2,128)}, u32[]{:S(2)}) copy-start(f32[1,2,8,128]{3,1,2,0:T(2,128)} %copy-done.82) | copy-start | bytes 24580
  1281.6 59.8 %copy-start.73 = (f32[2048]{0:T(1024)S(1)}, f32[2048]{0:T(1024)}, u32[]{:S(2)}) copy-start(f32[2048]{0:T(1024)} %copy-done.72) | copy-start | bytes 24580
  1281.6 110.5 %all-gather.25.cloned.1.call-start = ((), (), s32[]{:S(2)}) async-start(), calls=%async_computation.25 | async-start | bytes 3145728 | tf_op jit(solution)/shard_map/all_gather | solution.py:61
  1358.8 85.8 %reduce-scatter.27.cloned.1.call-start = ((), (), s32[]{:S(2)}) async-start(), calls=%async_computation.26 | async-start | bytes 3145728 | tf_op jit(solution)/shard_map/reduce_scatter | solution.py:74
  1392.0 14.9 copy-start.144
  1412.6 90.2 %all-gather.19.cloned.1.call-start = ((), (), s32[]{:S(2)}) async-start(), calls=%async_computation.19 | async-start | bytes 6291456 | tf_op jit(solution)/shard_map/all_gather | solution.py:57
  1413.2 124.8 %all-gather.27.cloned.1.call-start = ((), (), s32[]{:S(2)}) async-start(), calls=%async_computation.27 | async-start | bytes 3145728 | tf_op jit(solution)/shard_map/all_gather | solution.py:61
  1413.4 31.2 %copy-start.91 = (f32[1,1024]{1,0:T(1,128)S(1)}, f32[1,1024]{1,0:T(1,128)}, u32[]{:S(2)}) copy-start(f32[1,1024]{1,0:T(1,128)} %copy-done.90) | copy-start | bytes 12292
  1413.4 31.2 %copy-start.95 = (f32[512]{0:T(512)S(1)}, f32[512]{0:T(512)}, u32[]{:S(2)}) copy-start(f32[512]{0:T(512)} %copy-done.94) | copy-start | bytes 6148
  1413.4 31.2 %copy-start.103 = (f32[512]{0:T(512)S(1)}, f32[512]{0:T(512)}, u32[]{:S(2)}) copy-start(f32[512]{0:T(512)} %copy-done.102) | copy-start | bytes 6148
  1413.4 34.7 %copy-start.116 = (f32[512]{0:T(512)S(1)}, f32[512]{0:T(512)}, u32[]{:S(2)}) copy-start(f32[512]{0:T(512)} %copy-done.115) | copy-start | bytes 6148
  1452.8 176.3 %reduce-scatter.29.cloned.1.call-start = ((), (), s32[]{:S(2)}) async-start(), calls=%async_computation.28 | async-start | bytes 3145728 | tf_op jit(solution)/shard_map/reduce_scatter | solution.py:74
  1597.1 73.4 %all-gather.29.cloned.1.call-start = ((), (), s32[]{:S(2)}) async-start(), calls=%async_computation.29 | async-start | bytes 3145728 | tf_op jit(solution)/shard_map/all_gather | solution.py:61
  1597.6 12.2 copy-start.44
  1597.6 12.2 copy-start.45
  1615.2 13.8 copy-start.78
  1615.2 13.8 copy-start.85
  1615.3 16.6 copy-start.114
  1615.3 16.6 copy-start.109
  1637.3 508.5 %all-reduce.7.cloned.1.call-start = ((), (), s32[]{:S(2)}) async-start(), calls=%async_computation.31 | async-start | bytes 51904512 | tf_op jit(solution)/shard_map/psum | solution.py:388
  1684.6 601.2 %all-reduce.5.cloned.1.call-start = ((), (), s32[]{:S(2)}) async-start(), calls=%async_computation.30 | async-start | bytes 4194304 | tf_op jit(solution)/shard_map/psum | solution.py:399
  1685.5 22.6 copy-start.32
  1685.5 22.6 copy-start.41
  (118 other events, 418.2 us)
Sparse Core Ops, SparseCore 0:
  47.8 56.9 reduce-scatter.10
  110.1 33.0 all-gather.10
  200.5 54.3 reduce-scatter.12
  260.3 33.1 all-gather.12
  327.4 54.2 reduce-scatter.14
  397.5 56.7 all-gather.14
  537.6 99.2 reduce-scatter.16
  645.4 56.7 all-gather.16
  755.6 99.2 reduce-scatter.18
  857.7 54.3 reduce-scatter.20
  923.8 56.7 all-gather.20
  1011.4 54.2 reduce-scatter.22
  1076.5 56.7 all-gather.22
  1281.7 54.3 reduce-scatter.24
  1358.9 33.0 all-gather.24
  1412.8 31.8 reduce-scatter.26
  1446.1 56.7 all-gather.18
  1504.9 33.1 all-gather.26
  1597.2 31.8 reduce-scatter.28
  1637.4 33.1 all-gather.28
  1684.7 461.0 all-reduce.6
  2151.7 134.0 all-reduce.4
where the time goes:
time: 2300 us
  waiting for transfers between devices  1380 us (60%)
  matrix products  465 us (20%)
  local copies, waits for them, and re-layouts  217 us (9%)
  other arithmetic  176 us (8%)
  blocking collectives  42.5 us (2%)
    psum x1, waiting for transfers between devices, local(): lax.psum(patch_grad.astype(jnp.bfloat16), 'dp').astype(jnp.float32)  359 us
    reduce_scatter x4, waiting for transfers between devices, reduce_rows(): lax.psum_scatter(term_fn(jnp.int32(0), row_total * lax.axis_size('freq'))...  275 us
    all_gather x5, waiting for transfers between devices, gather_rows(): return lax.all_gather(values, 'freq', axis=0, tiled=True)  218 us
    reduce_scatter x5, waiting for transfers between devices, reduce_grads(): lax.psum_scatter(term_fn(jnp.int32(0), lax.axis_size('freq') * row_total)...  192 us
    all_gather x5, waiting for transfers between devices, gather_grads(): return lax.all_gather(values, 'freq', axis=0, tiled=True)  175 us
    dot_general x10, matrix products, matmul(): return jnp.dot(left, right, preferred_element_type=jnp.float32)  124 us
    psum x1, waiting for transfers between devices, local(): lax.psum((enc_gain_grad, enc_bias_grad, embed_grad, mask_grad, dec_gain_g...  107 us
    dot_general x10, matrix products, matmul_nt(): lax.dot_general(left, right, (((1,), (1,)), ((), ())), preferred_element_...  95.6 us
  transfers between devices with their start and end apart: 22, of which 22 were waited for; matrix products, arithmetic and copies ran while one was open for 10% of the time, Pallas kernels for 0%

commit v1 on v0

v1 whole, which is shorter than its diff:
```python
import math

import jax
import jax.numpy as jnp
from jax import lax
from jax.experimental import pallas as pl
from jax.experimental.pallas import tpu as pltpu
from jax.sharding import PartitionSpec as P

D = 1024
HDIM = 64
DDEC = 512
DHDIM = 32
RGB_PIX = 768
SIDE = 16
NPATCH = 256
VIS = 64

HIGHEST = lax.Precision.HIGHEST
EPSILON = 1e-06
MASKED = -1e30
BF16 = jnp.bfloat16
F32 = jnp.float32
LANES = 128
VMEM_LIMIT = 48 * 1024 * 1024
MESH = pl.DeviceIdType.MESH


def dot(left, right):
    return jnp.dot(left, right, preferred_element_type=F32)


def dot_tn(left, right):
    return lax.dot_general(left, right, (((0,), (0,)), ((), ())), preferred_element_type=F32)


def dot_nt(left, right):
    return lax.dot_general(left, right, (((1,), (1,)), ((), ())), preferred_element_type=F32)


def normalize(values):
    center = values - jnp.mean(values, -1, keepdims=True)
    rstd = lax.rsqrt(jnp.mean(center * center, -1, keepdims=True) + EPSILON)
    return center * rstd, rstd


def layer_norm(values, scales, shifts):
    return (normalize(values)[0] * scales + shifts).astype(BF16)


def layer_norm_back(grad, values, scales):
    unit, rstd = normalize(values)
    scaled = grad * scales
    mean_grad = jnp.mean(scaled, -1, keepdims=True)
    mean_along = jnp.mean(scaled * unit, -1, keepdims=True)
    grad_in = rstd * (scaled - mean_grad - unit * mean_along)
    return grad_in, jnp.sum(grad * unit, 0), jnp.sum(grad, 0)


def code_tables(ratios, features):
    quarter = features // 4
    index_f = jnp.arange(quarter, dtype=F32)
    frequencies = jnp.exp(index_f * (-math.log(10000.0) / quarter))
    places = jnp.arange(SIDE).astype(F32)
    angle = (places[None, :] * ratios[:, None])[..., None] * frequencies
    return jnp.concatenate([jnp.sin(angle), jnp.cos(angle)], -1)


def slot_codes(slot_ids, ratios, features):
    table = code_tables(ratios, features)
    places = jnp.arange(SIDE)
    row = (slot_ids[..., None] // SIDE == places).astype(F32)
    col = (slot_ids[..., None] % SIDE == places).astype(F32)
    pick = lambda one_hot: jnp.einsum("bsp,bpf->bsf", one_hot, table, precision=HIGHEST)
    return jnp.concatenate([pick(row), pick(col)], -1)


def grid_codes(ratios, features):
    table = code_tables(ratios, features)
    images, _, half = table.shape
    row = jnp.broadcast_to(table[:, :, None, :], (images, SIDE, SIDE, half))
    col = jnp.broadcast_to(table[:, None, :, :], (images, SIDE, SIDE, half))
    return jnp.concatenate([row, col], -1).reshape(images, NPATCH, features)


def head_masks(group, head_size):
    lane = lax.broadcasted_iota(jnp.int32, (1, group), 1)
    return [(lane // head_size == h) for h in range(group // head_size)]


def masked_scores(keys, queries, valid):
    scores = dot_nt(keys, queries)
    if valid is not None:
        scores = jnp.where(valid, scores, MASKED)
    return scores


def attend_kernel(head_size, masked, count_ref, q_ref, k_ref, v_ref, o_ref):
    seq, width = q_ref.shape
    group = LANES
    valid = None
    if masked:
        valid = lax.broadcasted_iota(jnp.int32, (seq, seq), 0) < count_ref[pl.program_id(0)]
    masks = head_masks(group, head_size)
    for g in range(width // group):
        lanes = slice(g * group, (g + 1) * group)
        queries, keys, values = q_ref[:, lanes], k_ref[:, lanes], v_ref[:, lanes]
        values_t = jnp.transpose(values)
        parts = []
        for h, mask in enumerate(masks):
            scores = masked_scores(keys, jnp.where(mask, queries, 0).astype(BF16), valid)
            top = jnp.max(scores, 0, keepdims=True)
            power = jnp.exp(scores - top)
            total = jnp.sum(power, 0, keepdims=True)
            rows = slice(h * head_size, (h + 1) * head_size)
            parts.append(dot(values_t[rows], power.astype(BF16)) * (1.0 / total))
        mixed = jnp.concatenate(parts, 0)
        o_ref[:, lanes] = jnp.transpose(mixed).astype(BF16)


def attend_back_kernel(
    head_size, masked, count_ref, q_ref, k_ref, v_ref, g_ref, dq_ref, dk_ref, dv_ref
):
    seq, width = q_ref.shape
    group = LANES
    factor = head_size ** (-0.5)
    valid = None
    if masked:
        valid = lax.broadcasted_iota(jnp.int32, (seq, seq), 0) < count_ref[pl.program_id(0)]
    masks = head_masks(group, head_size)
    for g in range(width // group):
        lanes = slice(g * group, (g + 1) * group)
        queries, keys, values, grads = (
            q_ref[:, lanes],
            k_ref[:, lanes],
            v_ref[:, lanes],
            g_ref[:, lanes],
        )
        keys_t = jnp.transpose(keys)
        dq_parts = []
        dk_sum = jnp.zeros((seq, group), F32)
        dv_sum = jnp.zeros((seq, group), F32)
        for h, mask in enumerate(masks):
            own_q = jnp.where(mask, queries, 0).astype(BF16)
            own_g = jnp.where(mask, grads, 0).astype(BF16)
            scores = masked_scores(keys, own_q, valid)
            top = jnp.max(scores, 0, keepdims=True)
            power = jnp.exp(scores - top)
            weights = power * (1.0 / jnp.sum(power, 0, keepdims=True))
            dv_sum += dot(weights.astype(BF16), own_g)
            grad_weights = dot_nt(values, own_g)
            along = jnp.sum(weights * grad_weights, 0, keepdims=True)
            grad_scores = (weights * (grad_weights - along)).astype(BF16)
            dk_sum += dot(grad_scores, own_q)
            rows = slice(h * head_size, (h + 1) * head_size)
            dq_parts.append(dot(keys_t[rows], grad_scores) * factor)
        dq_ref[:, lanes] = jnp.transpose(jnp.concatenate(dq_parts, 0)).astype(BF16)
        dk_ref[:, lanes] = dk_sum.astype(BF16)
        dv_ref[:, lanes] = dv_sum.astype(BF16)


def attention_call(kernel, counts, arrays, seq, n_out, head_size, flop_factor):
    rows, width = arrays[0].shape
    images = rows // seq
    block = pl.BlockSpec((seq, width), lambda i, counts: (i, 0))
    out = jax.ShapeDtypeStruct((rows, width), BF16)
    return pl.pallas_call(
        kernel,
        grid_spec=pltpu.PrefetchScalarGridSpec(
            num_scalar_prefetch=1,
            grid=(images,),
            in_specs=[block] * len(arrays),
            out_specs=[block] * n_out,
        ),
        out_shape=[out] * n_out,
        compiler_params=pltpu.CompilerParams(vmem_limit_bytes=VMEM_LIMIT),
        cost_estimate=pl.CostEstimate(
            flops=flop_factor * rows * seq * width * (LANES // head_size),
            bytes_accessed=(len(arrays) + n_out) * rows * width * 2,
            transcendentals=rows * seq * width // head_size,
        ),
    )(counts, *arrays)


def attend(queries, keys, values, counts, seq, head_size, masked):
    kernel = lambda *refs: attend_kernel(head_size, masked, *refs)
    return attention_call(kernel, counts, [queries, keys, values], seq, 1, head_size, 4)[0]


def attend_back(queries, keys, values, grads, counts, seq, head_size, masked):
    kernel = lambda *refs: attend_back_kernel(head_size, masked, *refs)
    return attention_call(kernel, counts, [queries, keys, values, grads], seq, 3, head_size, 10)


def up_kernel(x_ref, w_ref, active_ref, slope_ref):
    pre = dot(x_ref[...], w_ref[...])
    cdf = 0.5 + 0.5 * lax.erf(pre * math.sqrt(0.5))
    density = jnp.exp(-0.5 * pre * pre) * (1.0 / math.sqrt(2.0 * math.pi))
    active_ref[...] = (pre * cdf).astype(BF16)
    slope_ref[...] = (cdf + pre * density).astype(BF16)


def up_projection(rows_in, weight):
    rows, depth = rows_in.shape
    width = weight.shape[1]
    row_block = math.gcd(rows, 512)
    col_block = math.gcd(width, 512)
    out = jax.ShapeDtypeStruct((rows, width), BF16)
    spec = pl.BlockSpec((row_block, col_block), lambda i, j: (i, j))
    return pl.pallas_call(
        up_kernel,
        grid=(rows // row_block, width // col_block),
        in_specs=[
            pl.BlockSpec((row_block, depth), lambda i, j: (i, 0)),
            pl.BlockSpec((depth, col_block), lambda i, j: (0, j)),
        ],
        out_specs=[spec, spec],
        out_shape=[out, out],
        compiler_params=pltpu.CompilerParams(vmem_limit_bytes=VMEM_LIMIT),
        cost_estimate=pl.CostEstimate(
            flops=2 * rows * depth * width,
            bytes_accessed=2 * (rows * depth + depth * width + 2 * rows * width),
            transcendentals=2 * rows * width,
        ),
    )(rows_in, weight)


class Links:
    def __init__(self):
        self.shards = lax.axis_size("freq")
        self.fast = self.shards == 2 and lax.axis_size("dp") == 16
        self.place = lax.axis_index("freq")
        index = lax.axis_index("dp")
        self.last = None
        self.core = index % 2
        self.row = (index // 2) % 2
        depth = index // 4
        along = jnp.where(self.row == 0, depth, 7 - depth)
        self.rank = jnp.where(self.core == 0, along, (8 - along) % 8)
        cycle = [z * 4 for z in range(4)] + [z * 4 + 2 for z in range(3, -1, -1)]
        self.ring = []
        for i in range(8):
            self.ring.append((cycle[i], cycle[(i + 1) % 8]))
            self.ring.append((cycle[i] + 1, cycle[(i + 7) % 8] + 1))

    def over_x(self, values):
        return lax.ppermute(values, "freq", [(0, 1), (1, 0)])

    def over_x_in_turn(self, values):
        if self.last is not None:
            values, _ = lax.optimization_barrier((values, self.last))
        self.last = self.over_x(values)
        return self.last

    def over(self, bit, values):
        return lax.ppermute(values, "dp", [(i, i ^ bit) for i in range(16)])

    def over_core(self, values):
        return self.over(1, values)

    def over_ring(self, values):
        return lax.ppermute(values, "dp", self.ring)


def halves(values, which, axis):
    size = values.shape[axis] // 2
    return (
        lax.dynamic_slice_in_dim(values, which * size, size, axis),
        lax.dynamic_slice_in_dim(values, (1 - which) * size, size, axis),
    )


def ordered(which, own, other, axis):
    return jnp.where(
        which == 0,
        jnp.concatenate([own, other], axis),
        jnp.concatenate([other, own], axis),
    )


def fetch_other(links, weight, axis):
    half = halves(weight, links.core, axis)[0]
    quarter = halves(half, links.row, axis)[0]
    quarter = links.over_x_in_turn(quarter)
    half = ordered(links.row, quarter, links.over(2, quarter), axis)
    return jnp.concatenate([half, links.over_core(half)], axis)


def weight_shards(links, weight, axis):
    if links.fast:
        return [weight, fetch_other(links, weight, axis)]
    return [lax.all_gather(weight, "freq", axis=axis, tiled=True)]


def core_sum(links, values, axis):
    keep, send = halves(values, links.core, axis)
    return keep + links.over_core(send)


def quad_sum(links, grads, axis):
    own, across = grads
    size = across.shape[axis] // 2
    keep = lax.slice_in_dim(across, 0, size, axis=axis)
    send = lax.slice_in_dim(across, size, 2 * size, axis=axis)
    across = keep + links.over_core(send)
    return core_sum(links, own, axis) + links.over_x(across)


def ring_kernel(count, *refs):
    parts, sums, others, held = (refs[i * count : (i + 1) * count] for i in range(4))
    out_send, out_recv, back_send, back_recv, core_send, core_recv = refs[4 * count :]
    index, across = lax.axis_index("dp"), lax.axis_index("freq")
    core, row, depth = index % 2, (index // 2) % 2, index // 4
    along = depth * (1 - row) + (7 - depth) * row
    rank = (along * (1 - core) + (8 - along) * core) % 8

    def device(spot):
        spot = spot % 8
        side = spot // 4
        return (spot * (1 - side) + (7 - spot) * side) * 4 + side * 2 + core

    way = 1 - 2 * core
    after, before = (device(along + way + 8), across), (device(along - way + 8), across)
    twin = (index + 1 - 2 * core, across)
    barrier = pltpu.get_barrier_semaphore()
    for partner in (after, before, twin):
        pl.semaphore_signal(barrier, inc=1, device_id=partner, device_id_type=MESH)
    pl.semaphore_wait(barrier, 3)

    def copy(src, dst, send, recv, partner):
        return pltpu.make_async_remote_copy(
            src_ref=src,
            dst_ref=dst,
            send_sem=send,
            recv_sem=recv,
            device_id=partner,
            device_id_type=MESH,
        )

    def outward(i, step, src):
        return copy(src, held[i].at[step], out_send.at[step, i], out_recv.at[step, i], after)

    def backward(i, step, place):
        ref = sums[i].at[place]
        return copy(ref, ref, back_send.at[step, i], back_recv.at[step, i], after)

    def sideward(i, step, place):
        return copy(
            sums[i].at[place],
            others[i].at[place],
            core_send.at[step, i],
            core_recv.at[step, i],
            twin,
        )

    for i in range(count):
        outward(i, 0, parts[i].at[rank]).start()

    def out_step(step, carry):
        place = (rank + 7 - step) % 8
        for i in range(count):
            outward(i, step, held[i].at[step]).wait_recv()
            held[i][step] = held[i][step] + parts[i][place]
            outward(i, step + 1, held[i].at[step]).start()
        return carry

    lax.fori_loop(0, 6, out_step, 0)
    place = (rank + 1) % 8
    for i in range(count):
        outward(i, 6, held[i].at[6]).wait_recv()
        sums[i][place] = held[i][6] + parts[i][place]
        backward(i, 0, place).start()
        sideward(i, 0, place).start()

    def back_step(step, carry):
        place = (rank + 8 - step) % 8
        for i in range(count):
            backward(i, step, place).wait_recv()
            backward(i, step + 1, place).start()
            sideward(i, step + 1, place).start()
        return carry

    lax.fori_loop(0, 6, back_step, 0)
    place = (rank + 2) % 8
    for i in range(count):
        backward(i, 6, place).wait_recv()
        sideward(i, 7, place).start()

    def end_step(step, carry):
        for i in range(count):
            outward(i, step, held[i].at[step]).wait_send()
            backward(i, step, step).wait_send()
            sideward(i, step, step).wait_send()
            sideward(i, step, step).wait_recv()
        return carry

    lax.fori_loop(0, 7, end_step, 0)
    for i in range(count):
        sideward(i, 7, 7).wait_send()
        sideward(i, 7, 7).wait_recv()


def ring_sums(parts, collective_id):
    count = len(parts)
    chunked = [p.reshape((8, p.shape[0] // 8, p.shape[1])) for p in parts]
    shapes = [jax.ShapeDtypeStruct(c.shape, c.dtype) for c in chunked]
    whole = pl.BlockSpec(memory_space=pltpu.VMEM)
    sem = pltpu.SemaphoreType.DMA
    outs = pl.pallas_call(
        lambda *refs: ring_kernel(count, *refs),
        out_shape=shapes * 2,
        in_specs=[whole] * count,
        out_specs=[whole] * (2 * count),
        scratch_shapes=[pltpu.VMEM((7,) + c.shape[1:], c.dtype) for c in chunked]
        + [sem((7, count))] * 4
        + [sem((8, count))] * 2,
        compiler_params=pltpu.CompilerParams(
            collective_id=collective_id, has_side_effects=True, vmem_limit_bytes=VMEM_LIMIT
        ),
        cost_estimate=pl.CostEstimate(
            flops=2 * sum(p.size for p in parts),
            bytes_accessed=6 * sum(p.size for p in parts),
            transcendentals=0,
        ),
    )(*chunked)
    flat = [o.reshape(p.shape) for o, p in zip(outs, parts + parts)]
    return list(zip(flat[:count], flat[count:]))


def column_kernel(sum_rows, core_ref, own_ref, other_ref, out_ref):
    is_own = pl.program_id(1) == core_ref[0]
    filled = pl.program_id(0) < sum_rows

    @pl.when(filled & is_own)
    def _():
        out_ref[...] = own_ref[...].astype(F32)

    @pl.when(filled & ~is_own)
    def _():
        out_ref[...] = other_ref[...].astype(F32)

    @pl.when(~filled)
    def _():
        out_ref[...] = jnp.zeros(out_ref.shape, F32)


def join_columns(links, own, other, rows):
    have, half = own.shape
    block = math.gcd(have, rows)
    block = math.gcd(block, 128)
    have_blocks = have // block
    spec = pl.BlockSpec((block, half), lambda i, j, core: (jnp.minimum(i, have_blocks - 1), 0))
    return pl.pallas_call(
        lambda *refs: column_kernel(have_blocks, *refs),
        grid_spec=pltpu.PrefetchScalarGridSpec(
            num_scalar_prefetch=1,
            grid=(rows // block, 2),
            in_specs=[spec, spec],
            out_specs=pl.BlockSpec((block, half), lambda i, j, core: (i, j)),
        ),
        out_shape=jax.ShapeDtypeStruct((rows, 2 * half), F32),
        compiler_params=pltpu.CompilerParams(vmem_limit_bytes=VMEM_LIMIT),
        cost_estimate=pl.CostEstimate(
            flops=0, bytes_accessed=4 * have * half + 8 * rows * half, transcendentals=0
        ),
    )(links.core.reshape(1), own, other)


def row_kernel(blocks, core_ref, own_ref, other_ref, out_ref):
    is_own = pl.program_id(0) // blocks == core_ref[0]

    @pl.when(is_own)
    def _():
        out_ref[...] = own_ref[...].astype(F32)

    @pl.when(~is_own)
    def _():
        out_ref[...] = other_ref[...].astype(F32)


def join_rows(links, own, other):
    half, width = own.shape
    block = math.gcd(half, 256)
    blocks = half // block

    def spec(mine):
        def place(i, core):
            here = (i // blocks == core[0]) == mine
            return (jnp.where(here, i % blocks, 0), 0)

        return pl.BlockSpec((block, width), place)

    return pl.pallas_call(
        lambda *refs: row_kernel(blocks, *refs),
        grid_spec=pltpu.PrefetchScalarGridSpec(
            num_scalar_prefetch=1,
            grid=(2 * blocks,),
            in_specs=[spec(True), spec(False)],
            out_specs=pl.BlockSpec((block, width), lambda i, core: (i, 0)),
        ),
        out_shape=jax.ShapeDtypeStruct((2 * half, width), F32),
        compiler_params=pltpu.CompilerParams(vmem_limit_bytes=VMEM_LIMIT),
        cost_estimate=pl.CostEstimate(
            flops=0, bytes_accessed=12 * half * width, transcendentals=0
        ),
    )(links.core.reshape(1), own, other)


def join_qkv(links, own, other):
    total = ordered(links.core, own, other, 1)
    depth = own.shape[0] // 3
    return jnp.stack([total[i * depth : (i + 1) * depth] for i in range(3)], axis=1).astype(F32)


def sum_small(links, values):
    if links.fast:
        values = values + links.over_x(values)
        for bit in (1, 2, 4, 8):
            values = values + links.over(bit, values)
        return values
    return lax.psum(values, ("dp", "freq"))


def own_images(links, values):
    count = values.shape[0] // links.shards
    return lax.dynamic_slice_in_dim(values, links.place * count, count, 0)


def reduce_rows(links, partial):
    if links.fast:
        keep, send = halves(partial, links.place, 0)
        return keep + links.over_x_in_turn(send.astype(BF16)).astype(F32)
    return lax.psum_scatter(
        partial.astype(BF16), "freq", scatter_dimension=0, tiled=True
    ).astype(F32)


def gather_rows(links, values):
    if links.fast:
        return ordered(links.place, values, links.over_x(values), 0)
    return lax.all_gather(values, "freq", axis=0, tiled=True)


def block_forward(stream, gains, biases, shards, counts, seq, head_size, masked):
    normed = layer_norm(stream, gains[0], biases[0])
    middle = stream
    heads = []
    for weight_qkv, weight_out, _, _ in shards:
        queries = (dot(normed, weight_qkv[0]) * head_size ** (-0.5)).astype(BF16)
        keys = dot(normed, weight_qkv[1]).astype(BF16)
        values = dot(normed, weight_qkv[2]).astype(BF16)
        mixed = attend(queries, keys, values, counts, seq, head_size, masked)
        middle = middle + dot(mixed, weight_out)
        heads.append((queries, keys, values, mixed))
    normed_mid = layer_norm(middle, gains[1], biases[1])
    result = middle
    units = []
    for _, _, weight_up, weight_down in shards:
        active, slope = up_projection(normed_mid, weight_up)
        result = result + dot(active, weight_down)
        units.append((active, slope))
    return result, (stream, normed, heads, middle, normed_mid, units)


def block_backward(grad, gains, shards, counts, seq, head_size, masked, saved):
    stream, normed, heads, middle, normed_mid, units = saved
    low = grad.astype(BF16)
    down_grads, up_grads, grad_normed = [], [], 0.0
    for (_, _, weight_up, weight_down), (active, slope) in zip(shards, units):
        grad_pre = (dot_nt(low, weight_down) * slope.astype(F32)).astype(BF16)
        grad_normed = grad_normed + dot_nt(grad_pre, weight_up)
        down_grads.append(dot_tn(active, low).astype(BF16))
        up_grads.append(dot_tn(normed_mid, grad_pre).astype(BF16))
    grad_in, mid_gain, mid_bias = layer_norm_back(grad_normed, middle, gains[1])
    grad = grad + grad_in
    low = grad.astype(BF16)
    out_grads, qkv_grads, grad_normed = [], [], 0.0
    for (weight_qkv, weight_out, _, _), (queries, keys, values, mixed) in zip(shards, heads):
        grad_mixed = dot_nt(low, weight_out).astype(BF16)
        grads = attend_back(queries, keys, values, grad_mixed, counts, seq, head_size, masked)
        for i in range(3):
            grad_normed = grad_normed + dot_nt(grads[i], weight_qkv[i])
        out_grads.append(dot_tn(mixed, low).astype(BF16))
        qkv_grads.append([dot_tn(normed, grads[i]).astype(BF16) for i in range(3)])
    grad_in, first_gain, first_bias = layer_norm_back(grad_normed, stream, gains[0])
    return (
        grad + grad_in,
        (first_gain, mid_gain),
        (first_bias, mid_bias),
        (qkv_grads, out_grads, up_grads, down_grads),
    )


def local(
    pixels,
    band_group,
    mask_order,
    visible_count,
    scale_id,
    patch_weight,
    enc_qkv,
    enc_out,
    enc_up,
    enc_down,
    enc_gains,
    enc_biases,
    dec_embed,
    mask_token,
    dec_qkv,
    dec_out,
    dec_up,
    dec_down,
    dec_gains,
    dec_biases,
    head_weight,
    recon_cotangent,
):
    links = Links()
    images, _, pixel_width = pixels.shape
    own = images // links.shards
    own_slots = own * VIS
    rgb_width = min(RGB_PIX, pixel_width)

    stacked = lambda weight: jnp.stack([weight[:, i] for i in range(3)])
    enc_parts = [weight_shards(links, stacked(enc_qkv), 2), weight_shards(links, enc_out, 0)]

    slot_ids = mask_order[:, :VIS]
    one_hot = slot_ids[:, :, None] == jnp.arange(NPATCH)[None, None, :]
    picked = jnp.einsum(
        "bsp,bpc->bsc", one_hot.astype(BF16), pixels, preferred_element_type=F32
    ).astype(BF16)
    multi = (band_group == 0)[:, None, None]
    zero = jnp.zeros((), BF16)
    rgb_valid = links.place * pixel_width + jnp.arange(rgb_width) < RGB_PIX
    picked_multi = jnp.where(multi, picked, zero).reshape(images * VIS, pixel_width)
    picked_rgb = jnp.where(~multi & rgb_valid, picked[:, :, :rgb_width], zero)
    picked_rgb = picked_rgb.reshape(images * VIS, rgb_width)
    patch_rgb = patch_weight[1, :rgb_width]
    partial = dot(picked_multi, patch_weight[0]) + dot(picked_rgb, patch_rgb)
    embedded = reduce_rows(links, partial)
    enc_parts += [weight_shards(links, enc_up, 1), weight_shards(links, enc_down, 0)]
    enc_shards = list(zip(*enc_parts))
    dec_parts = [
        weight_shards(links, stacked(dec_qkv), 2),
        weight_shards(links, dec_out, 0),
        weight_shards(links, dec_up, 1),
        weight_shards(links, dec_down, 0),
    ]
    dec_shards = list(zip(*dec_parts))
    cotangent = recon_cotangent.reshape(images * NPATCH, -1)
    grad_final = reduce_rows(links, dot_nt(cotangent, head_weight))

    my_slots = own_images(links, slot_ids)
    my_count = own_images(links, visible_count)
    ratios = jnp.exp2(own_images(links, scale_id).astype(F32) - 1.0)
    stream = embedded + slot_codes(my_slots, ratios, D).reshape(own_slots, D)

    stream, enc_saved = block_forward(
        stream, enc_gains, enc_biases, enc_shards, my_count, VIS, HDIM, True
    )
    latent = layer_norm(stream, enc_gains[2], enc_biases[2])
    lifted = dot(latent, dec_embed)

    live = jnp.arange(VIS)[None, :] < my_count[:, None]
    select = (my_slots[:, :, None] == jnp.arange(NPATCH)[None, None, :]) & live[:, :, None]
    hidden = 1.0 - jnp.sum(select.astype(F32), axis=1)[:, :, None]
    decoded = (
        jnp.einsum(
            "bsp,bse->bpe",
            select.astype(F32),
            lifted.reshape(own, VIS, DDEC),
            precision=HIGHEST,
        )
        + hidden * mask_token
        + grid_codes(ratios, DDEC)
    ).reshape(own * NPATCH, DDEC)
    decoded, dec_saved = block_forward(
        decoded, dec_gains, dec_biases, dec_shards, my_count, NPATCH, DHDIM, False
    )
    final_own = layer_norm(decoded, dec_gains[2], dec_biases[2])

    final_all = gather_rows(links, final_own)
    reconstructions = dot(final_all, head_weight).astype(BF16).reshape(images, NPATCH, -1)
    head_grad = dot_tn(final_all, cotangent).astype(BF16)

    grad_in, dec_gain_2, dec_bias_2 = layer_norm_back(grad_final, decoded, dec_gains[2])
    grad_decoded, dec_gain_01, dec_bias_01, dec_grads = block_backward(
        grad_in, dec_gains, dec_shards, my_count, NPATCH, DHDIM, False, dec_saved
    )
    grad_grid = grad_decoded.reshape(own, NPATCH, DDEC)
    mask_grad = jnp.sum(hidden * grad_grid, axis=(0, 1))
    grad_lifted = (
        jnp.einsum(
            "bsp,bpe->bse",
            select.astype(BF16),
            grad_grid.astype(BF16),
            preferred_element_type=F32,
        )
        .astype(BF16)
        .reshape(own_slots, DDEC)
    )
    embed_grad = dot_tn(latent, grad_lifted).astype(BF16)
    grad_latent = dot_nt(grad_lifted, dec_embed)

    grad_in, enc_gain_2, enc_bias_2 = layer_norm_back(grad_latent, stream, enc_gains[2])
    grad_stream, enc_gain_01, enc_bias_01, enc_grads = block_backward(
        grad_in, enc_gains, enc_shards, my_count, VIS, HDIM, True, enc_saved
    )

    grad_embedded = gather_rows(links, grad_stream.astype(BF16))
    patch_grads = [
        dot_tn(picked_multi, grad_embedded).astype(BF16),
        dot_tn(picked_rgb, grad_embedded).astype(BF16),
    ]
    multi_rows = jnp.repeat(band_group == 0, VIS)[:, None]
    back_multi = dot_nt(jnp.where(multi_rows, grad_embedded, zero), patch_weight[0])
    back_rgb = dot_nt(jnp.where(multi_rows, zero, grad_embedded), patch_rgb)
    back_rgb = jnp.where(rgb_valid, back_rgb, 0.0)
    back = back_multi + jnp.pad(back_rgb, ((0, 0), (0, pixel_width - rgb_width)))
    pixel_grad = jnp.einsum(
        "bsp,bsc->bpc",
        one_hot.astype(BF16),
        back.astype(BF16).reshape(images, VIS, pixel_width),
        preferred_element_type=F32,
    )

    dec_qkv_grads, dec_out_grads, dec_up_grads, dec_down_grads = dec_grads
    enc_qkv_grads, enc_out_grads, enc_up_grads, enc_down_grads = enc_grads
    stacked_qkv = lambda grads: [jnp.concatenate(g, 0) for g in grads]
    enc_stack = [
        (stacked_qkv(enc_qkv_grads), 1),
        (enc_out_grads, 0),
        (enc_up_grads, 1),
        (enc_down_grads, 0),
    ]
    dec_stack = [
        (stacked_qkv(dec_qkv_grads), 1),
        (dec_out_grads, 0),
        (dec_up_grads, 1),
        (dec_down_grads, 0),
    ]
    patch_grad = jnp.concatenate(patch_grads, 0)
    if links.fast:
        early = [quad_sum(links, g, axis) for g, axis in dec_stack]
        embed_part = core_sum(links, embed_grad, 0)
        early += [embed_part + links.over_x(embed_part), core_sum(links, head_grad, 1)]
        late = [quad_sum(links, g, axis) for g, axis in enc_stack]
        late += [core_sum(links, patch_grad, 1)]
        early = ring_sums(early, 1)
        late = ring_sums(late, 2)
        totals = []
        for group in (early, late):
            totals.append(
                [
                    join_qkv(links, *group[0]),
                    join_rows(links, *group[1]),
                    join_columns(links, *group[2], group[2][0].shape[0]),
                    join_rows(links, *group[3]),
                ]
            )
        dec_totals, enc_totals = totals
        embed_total = join_rows(links, *early[4])
        head_total = join_columns(links, *early[5], DDEC)
        patch_total = join_columns(links, *late[4], 2 * pixel_width)
        patch_total = patch_total.reshape(2, pixel_width, D)
    else:
        reduced = []
        for stack, depth in ((dec_stack, DDEC), (enc_stack, D)):
            parts = [
                lax.psum_scatter(g[0], "freq", scatter_dimension=axis, tiled=True)
                for g, axis in stack
            ]
            parts = [lax.psum(part, "dp").astype(F32) for part in parts]
            parts[0] = jnp.stack(
                [parts[0][i * depth : (i + 1) * depth] for i in range(3)], axis=1
            )
            reduced.append(parts)
        dec_totals, enc_totals = reduced
        embed_total = lax.psum(embed_grad, ("dp", "freq")).astype(F32)
        head_total = lax.psum(head_grad, "dp").astype(F32)
        patch_sum = lax.psum(patch_grad, "dp").astype(F32)
        patch_total = jnp.stack(
            [
                patch_sum[:pixel_width],
                jnp.pad(patch_sum[pixel_width:], ((0, pixel_width - rgb_width), (0, 0))),
            ]
        )
    small = [*enc_gain_01, enc_gain_2, *enc_bias_01, enc_bias_2]
    small += [*dec_gain_01, dec_gain_2, *dec_bias_01, dec_bias_2, mask_grad]
    small = sum_small(links, jnp.concatenate(small).reshape(-1, LANES)).reshape(-1)
    enc_end, dec_end = 6 * D, 6 * D + 6 * DDEC
    enc_small = small[:enc_end].reshape(2, 3, D)
    dec_small = small[enc_end:dec_end].reshape(2, 3, DDEC)
    return (
        reconstructions,
        pixel_grad,
        patch_total,
        *enc_totals,
        enc_small[0],
        enc_small[1],
        embed_total,
        small[dec_end:],
        *dec_totals,
        dec_small[0],
        dec_small[1],
        head_total,
    )


def solution(mesh):
    return jax.shard_map(
        local,
        mesh=mesh,
        in_specs=(
            P("dp", None, "freq"),
            P("dp"),
            P("dp", None),
            P("dp"),
            P("dp"),
            P(None, "freq", None),
            P(None, None, "freq"),
            P("freq", None),
            P(None, "freq"),
            P("freq", None),
            P(),
            P(),
            P(),
            P(),
            P(None, None, "freq"),
            P("freq", None),
            P(None, "freq"),
            P("freq", None),
            P(),
            P(),
            P(None, "freq"),
            P("dp", None, "freq"),
        ),
        out_specs=(
            P("dp", None, "freq"),
            P("dp", None, "freq"),
            P(None, "freq", None),
            P(None, None, "freq"),
            P("freq", None),
            P(None, "freq"),
            P("freq", None),
            P(),
            P(),
            P(),
            P(),
            P(None, None, "freq"),
            P("freq", None),
            P(None, "freq"),
            P("freq", None),
            P(),
            P(),
            P(None, "freq"),
        ),
        check_vma=False,
    )
```

time: 2300 us -> 1130 us (0.49)
  waiting for transfers between devices: 1380 us -> 146 us
  Pallas kernels: 0 us -> 471 us
  matrix products: 465 us -> 287 us
  local copies, waits for them, and re-layouts: 217 us -> 78.2 us
  other arithmetic: 176 us -> 96.8 us
  blocking collectives: 42.5 us -> 0 us
  starting transfers between devices: 2.76 us -> 40.8 us
    reduce_scatter x10 -> x0, waiting for transfers between devices: 517 us -> none  [the longest x4 275 us: reduce_rows(): lax.psum_scatter(term_fn(jnp.int32(0), row_total * lax.axis_size('freq'))...]
    pallas_call x0 -> x23, Pallas kernels: none -> 471 us  [the longest x2 261 us: ring_sums(): pl.pallas_call(lambda *refs: ring_kernel(count, *refs), out_shape=shapes...]
    psum x2 -> x0, waiting for transfers between devices: 466 us -> none  [the longest x1 359 us: local(): lax.psum(patch_grad.astype(jnp.bfloat16), 'dp').astype(jnp.float32)]
    all_gather x10 -> x0, waiting for transfers between devices: 393 us -> none  [the longest x5 218 us: gather_rows(): return lax.all_gather(values, 'freq', axis=0, tiled=True)]
    dot_general x48 -> x86, matrix products: 441 us -> 287 us  [the longest x28 102 us: dot_nt(): lax.dot_general(left, right, (((1,), (1,)), ((), ())), preferred_element_...]
    ppermute x0 -> x61, waiting for transfers between devices: none -> 146 us  [the longest x22 113 us: over_x(): return lax.ppermute(values, 'freq', [(0, 1), (1, 0)])]
    convert_element_type x27 -> x13, other arithmetic: 85.2 us -> 17.1 us  [the longest x4 8.2 us: block_backward(): low = grad.astype(BF16)]
    convert_element_type x16 -> x2, local copies, waits for them, and re-layouts: 64.3 us -> 4.9 us  [reduce_rows(): return keep + links.over_x_in_turn(send.astype(BF16)).astype(F32)]
  transfers between devices with their start and end apart: 22 -> 61, of which waited for: 22 -> 16; matrix products, arithmetic and copies ran while one was open for 10% -> 25% of each run, Pallas kernels for 0% -> 18%
where the time goes in v1:
time: 1130 us; the launch traced here: 1120 us
  Pallas kernels  471 us (42%)
  matrix products  287 us (25%)
  waiting for transfers between devices  146 us (13%)
  other arithmetic  96.8 us (9%)
  local copies, waits for them, and re-layouts  78.2 us (7%)
  starting transfers between devices  40.8 us (4%)
    pallas_call x2, Pallas kernels, ring_sums(): pl.pallas_call(lambda *refs: ring_kernel(count, *refs), out_shape=shapes...  261 us
    pallas_call x8, Pallas kernels, attention_call(): pl.pallas_call(kernel, grid_spec=pltpu.PrefetchScalarGridSpec(num_scalar_...  139 us
    ppermute x22, waiting for transfers between devices, over_x(): return lax.ppermute(values, 'freq', [(0, 1), (1, 0)])  113 us
    dot_general x28, matrix products, dot_nt(): lax.dot_general(left, right, (((1,), (1,)), ((), ())), preferred_element_...  102 us
    dot_general x28, matrix products, dot_tn(): lax.dot_general(left, right, (((0,), (0,)), ((), ())), preferred_element_...  90.1 us
    dot_general x24, matrix products, dot(): return jnp.dot(left, right, preferred_element_type=F32)  74 us
    ppermute x39, waiting for transfers between devices, over(): return lax.ppermute(values, 'dp', [(i, i ^ bit) for i in range(16)])  33.1 us
    pallas_call x4, Pallas kernels, join_columns(): pl.pallas_call(lambda *refs: column_kernel(have_blocks, *refs), grid_spec...  32.9 us
  transfers between devices with their start and end apart: 61, of which 16 were waited for; matrix products, arithmetic and copies ran while one was open for 25% of the time, Pallas kernels for 18%

profile of v1, /device:TPU:0, one launch (start us, length us, event | category | flops | bytes accessed | tf_op | source)
XLA Modules:
  0.0 1123.8 jit_solution(11551908385912948896)
XLA Ops:
  0.7 3.7 slice_bitcast_fusion.3
  32.2 5.1 fusion.25
  37.3 3.9 fusion.18
  44.5 20.2 %fusion.149 = f32[4096,512]{1,0:T(8,128)} fusion(bf16[4096,3328]{1,0:T(8,128)(2,1)} %bitcast.385, bf16[512,3328]{1,0:T(8,128)(2,1)S(1)} %copy-done), kind=kOutput, calls=%fused_computation.401 | convolution fusion | flops 13958643712 | bytes 39059456 | tf_op jit(solution)/shard_map/dot_general | solution.py:38
  81.8 3.8 dynamic-slice_convert_fusion
  85.6 18.2 %collective-permute-done.5 = bf16[128,1024]{1,0:T(8,128)(2,1)S(1)} collective-permute-done((bf16[128,1024]{1,0:T(8,128)(2,1)}, bf16[128,1024]{1,0:T(8,128)(2,1)S(1)}, u32[]{:S(2)}, u32[]{:S(2)}) %collective-permute-start.5) | collective-permute-done | bytes 262176 | tf_op jit(solution)/shard_map/ppermute | solution.py:256
  112.8 12.8 %shard_map.349 = bf16[512,512]{1,0:T(8,128)(2,1)S(1)} custom-call(s32[8]{0:T(128)S(1)} %dynamic_slice.136.refs_0_, bf16[512,512]{1,0:T(8,128)(2,1)S(1)} %fusion.29.refs_1_, bf16[512,512]{1,0:T(8,128)(2,1)S(1)} %convolution_convert_fusion.34.refs_2_, bf16[512,512]{1,0:T(8,128)(2,1)S(1)} %convolution_convert_fusion.33.refs_3_), custom_call_target="tpu_custom_call" | custom-call | flops 134217728 | bytes 2097152 | tf_op jit(solution)/shard_map/pallas_call | solution.py:167
  125.6 8.3 collective-permute-done.7
  138.6 13.2 %shard_map.350 = bf16[512,512]{1,0:T(8,128)(2,1)S(1)} custom-call(s32[8]{0:T(128)S(1)} %dynamic_slice.136.refs_0_, bf16[512,512]{1,0:T(8,128)(2,1)S(1)} %fusion.30.refs_1_, bf16[512,512]{1,0:T(8,128)(2,1)S(1)} %convolution_convert_fusion.32.refs_2_, bf16[512,512]{1,0:T(8,128)(2,1)S(1)} %convolution_convert_fusion.31.refs_3_), custom_call_target="tpu_custom_call" | custom-call | flops 134217728 | bytes 2097152 | tf_op jit(solution)/shard_map/pallas_call | solution.py:167
  151.8 6.5 collective-permute-done.10
  161.9 8.7 collective-permute-done.13
  171.6 4.1 collective-permute-done.16
  178.6 3.5 collective-permute-done.19
  187.2 5.8 shard_map.351
  196.3 9.1 collective-permute-done.17
  206.5 5.8 fusion.145
  218.2 4.1 pad_maximum_fusion.w_ref
  222.3 6.0 shard_map.352
  228.4 6.1 fusion.140
  246.5 21.0 %shard_map.353 = bf16[2048,256]{1,0:T(8,128)(2,1)S(1)} custom-call(s32[8]{0:T(128)S(1)} %dynamic_slice.136.refs_0_, bf16[2048,256]{1,0:T(8,128)(2,1)S(1)} %fusion.8.refs_1_, bf16[2048,256]{1,0:T(8,128)(2,1)S(1)} %convolution_convert_fusion.13.refs_2_, bf16[2048,256]{1,0:T(8,128)(2,1)S(1)} %convolution_convert_fusion.12.refs_3_), custom_call_target="tpu_custom_call" | custom-call | flops 2147483648 | bytes 4194304 | tf_op jit(solution)/shard_map/pallas_call | solution.py:167
  275.3 20.6 %shard_map.354 = bf16[2048,256]{1,0:T(8,128)(2,1)S(1)} custom-call(s32[8]{0:T(128)S(1)} %dynamic_slice.136.refs_0_, bf16[2048,256]{1,0:T(8,128)(2,1)S(1)} %fusion.9.refs_1_, bf16[2048,256]{1,0:T(8,128)(2,1)S(1)} %convolution_convert_fusion.11.refs_2_, bf16[2048,256]{1,0:T(8,128)(2,1)S(1)} %convolution_convert_fusion.10.refs_3_), custom_call_target="tpu_custom_call" | custom-call | flops 2147483648 | bytes 4194304 | tf_op jit(solution)/shard_map/pallas_call | solution.py:167
  302.2 7.8 shard_map.355
  310.0 7.8 shard_map.356
  317.8 4.7 fusion.148
  322.5 4.0 fusion.143
  327.4 5.6 multiply_reduce_fusion.1
  333.1 3.5 fusion.131
  345.8 3.4 convolution_convert_fusion.27
  349.2 4.4 fusion.150
  353.6 4.9 multiply_convert_fusion
  358.5 3.5 convolution_convert_fusion.26
  362.1 6.1 multiply_reduce_fusion.2
  376.1 25.1 %shard_map.357 = (bf16[2048,256]{1,0:T(8,128)(2,1)S(1)}, bf16[2048,256]{1,0:T(8,128)(2,1)S(1)}, bf16[2048,256]{1,0:T(8,128)(2,1)S(1)}) custom-call(s32[8]{0:T(128)S(1)} %dynamic_slice.136.refs_0_, bf16[2048,256]{1,0:T(8,128)(2,1)S(1)} %fusion.8.refs_1_, bf16[2048,256]{1,0:T(8,128)(2,1)S(1)} %convolution_convert_fusion.13.refs_2_, ...), custom_call_target="tpu_custom_call" | custom-call | flops 5368709120 | bytes 7340032 | tf_op jit(solution)/shard_map/pallas_call | solution.py:167
  402.9 25.5 %shard_map.358 = (bf16[2048,256]{1,0:T(8,128)(2,1)S(1)}, bf16[2048,256]{1,0:T(8,128)(2,1)S(1)}, bf16[2048,256]{1,0:T(8,128)(2,1)S(1)}) custom-call(s32[8]{0:T(128)S(1)} %dynamic_slice.136.refs_0_, bf16[2048,256]{1,0:T(8,128)(2,1)S(1)} %fusion.9.refs_1_, bf16[2048,256]{1,0:T(8,128)(2,1)S(1)} %convolution_convert_fusion.11.refs_2_, ...), custom_call_target="tpu_custom_call" | custom-call | flops 5368709120 | bytes 7340032 | tf_op jit(solution)/shard_map/pallas_call | solution.py:167
  438.4 3.8 fusion.117
  442.2 8.7 multiply_reduce_fusion.3
  468.6 4.4 convolution_convert_fusion.3
  473.0 4.4 convolution_convert_fusion.4
  482.8 4.4 multiply_convert_fusion.2
  487.2 6.0 multiply_reduce_fusion.14
  499.0 10.4 shard_map.359
  518.6 4.4 convolution_convert_fusion.5
  523.0 4.4 convolution_convert_fusion.6
  535.2 10.2 shard_map.360
  597.9 30.9 %collective-permute-done.48 = bf16[1536,128]{1,0:T(8,128)(2,1)S(1)} collective-permute-done((bf16[1536,128]{1,0:T(8,128)(2,1)S(1)}, bf16[1536,128]{1,0:T(8,128)(2,1)S(1)}, u32[]{:S(2)}, u32[]{:S(2)}) %collective-permute-start.48) | collective-permute-done | bytes 393248 | tf_op jit(solution)/shard_map/ppermute | solution.py:247
  630.9 5.0 fusion.21
  635.9 8.9 add_convert_fusion
  644.8 11.7 %fusion.47 = f32[16,256,1664]{2,1,0:T(8,128)} fusion(bf16[16,64,1664]{2,1,0:T(8,128)(2,1)S(1)} %bitcast.343, s32[16,64]{1,0:T(8,128)S(1)} %copy-done.145), kind=kOutput, calls=%fused_computation.193 | convolution fusion | flops 872677376 | bytes 30674944 | tf_op jit(solution)/shard_map/bsp,bsc->bpc/dot_general | solution.py:720
  656.5 4.1 convolution_convert_fusion.2
  663.5 32.2 %collective-permute-done.59 = bf16[512,512]{1,0:T(8,128)(2,1)S(1)} collective-permute-done((bf16[512,512]{1,0:T(8,128)(2,1)S(1)}, bf16[512,512]{1,0:T(8,128)(2,1)S(1)}, u32[]{:S(2)}, u32[]{:S(2)}) %collective-permute-start.59) | collective-permute-done | bytes 524320 | tf_op jit(solution)/shard_map/ppermute | solution.py:247
  702.7 7.9 collective-permute-done.54
  712.1 8.2 collective-permute-done.33
  725.7 24.0 %convolution_convert_fusion = bf16[4096,3328]{1,0:T(8,128)(2,1)} fusion(bf16[512,3328]{1,0:T(8,128)(2,1)S(1)} %copy-done, bf16[2048,512]{1,0:T(8,128)(2,1)} %copy-done.206, bf16[2048,512]{1,0:T(8,128)(2,1)} %get-tuple-element.160, pred[]{:T(512)S(6)} %eq.37), kind=kOutput, calls=%fused_computation | convolution fusion | flops 13991149568 | bytes 34865152 | tf_op jit(solution)/shard_map/dot_general | solution.py:30
  749.7 28.7 %convolution_convert_fusion.1 = bf16[512,3328]{1,0:T(8,128)(2,1)} fusion(bf16[4096,3328]{1,0:T(8,128)(2,1)} %bitcast.386, bf16[2048,512]{1,0:T(8,128)(2,1)} %copy-done.206, bf16[2048,512]{1,0:T(8,128)(2,1)} %get-tuple-element.160, pred[]{:T(512)S(6)} %eq.37), kind=kOutput, calls=%fused_computation.6 | convolution fusion | flops 13979222016 | bytes 34865152 | tf_op jit(solution)/shard_map/dot_general | solution.py:34
  786.5 4.0 add_add_fusion.7
  791.5 4.3 fusion.12
  797.5 81.7 %shard_map.366 = (bf16[8,192,128]{2,1,0:T(8,128)(2,1)S(1)}, bf16[8,16,512]{2,1,0:T(8,128)(2,1)S(1)}, bf16[8,64,512]{2,1,0:T(8,128)(2,1)S(1)}, bf16[8,64,512]{2,1...) custom-call(bf16[8,192,128]{2,1,0:T(8,128)(2,1)S(1)} %bitcast.317, ...), custom_call_target="tpu_custom_call" | custom-call | flops 3801088 | bytes 11403264 | tf_op jit(solution)/shard_map/pallas_call | solution.py:409
  886.9 4.1 shard_map.371
  893.8 5.3 add_add_fusion.3
  899.1 5.1 add_add_fusion.2
  904.2 179.7 %shard_map.361 = (bf16[8,384,256]{2,1,0:T(8,128)(2,1)S(1)}, bf16[8,32,1024]{2,1,0:T(8,128)(2,1)S(1)}, bf16[8,128,1024]{2,1,0:T(8,128)(2,1)}, bf16[8,128,1024]{2,...) custom-call(bf16[8,384,256]{2,1,0:T(8,128)(2,1)} %bitcast.348, ...), custom_call_target="tpu_custom_call" | custom-call | flops 8781824 | bytes 26345472 | tf_op jit(solution)/shard_map/pallas_call | solution.py:409
  1087.7 6.8 shard_map.364
  1096.1 4.5 shard_map.365
  1101.5 18.9 %shard_map.362 = f32[3328,1024]{1,0:T(8,128)} custom-call(s32[1]{0:T(128)} %bitcast.44.refs_0_, bf16[2432,512]{1,0:T(8,128)(2,1)S(1)} %bitcast.306, bf16[2432,512]{1,0:T(8,128)(2,1)S(1)} %bitcast.307), custom_call_target="tpu_custom_call" | custom-call | bytes 18612224 | tf_op jit(solution)/shard_map/pallas_call | solution.py:453
  (786 shorter events, 285.9 us)
Async XLA Ops:
  7.2 61.9 %collective-permute-start = (bf16[3,1024,128]{2,1,0:T(8,128)(2,1)}, bf16[3,1024,128]{2,1,0:T(8,128)(2,1)}, u32[]{:S(2)}, u32[]{:S(2)}) collective-permute-start(bf16[3,1024,128]{2,1,0:T(8,128)(2,1)} %fusion.55), channel_id=1, source_target_pairs={{0,1},{1,0},{2,3},{3,2},{4,5},{5,4},{6,7},{7,6},{8,9},{9,8},{10,11... | collective-permute-start | bytes 2359304 | tf_op jit(solution)/shard_map/ppermute | solution.py:247
  66.3 119.5 %copy-start.160 = (f32[1,1024]{1,0:T(1,128)}, f32[1,1024]{1,0:T(1,128)S(1)}, u32[]{:S(2)}) copy-start(f32[1,1024]{1,0:T(1,128)S(1)} %get-tuple-element.179) | copy-start | bytes 12292
  69.1 8.1 collective-permute-start.1
  77.2 30.3 %collective-permute-start.2 = (bf16[512,1024]{1,0:T(8,128)(2,1)}, bf16[512,1024]{1,0:T(8,128)(2,1)S(1)}, u32[]{:S(2)}, u32[]{:S(2)}) collective-permute-start(bf16[512,1024]{1,0:T(8,128)(2,1)} %dynamic-slice_convert_fusion.1), channel_id=1, source_target_pairs={{0,1},{1,0},{2,3},{3,2},{4,5},{5,4},{6,7},{7,6},{8,9},{9,8},{10,11... | collective-permute-start | bytes 3145736 | tf_op jit(solution)/shard_map/ppermute | solution.py:247
  79.4 25.6 %collective-permute-start.3 = (bf16[3,1024,128]{2,1,0:T(8,128)(2,1)}, bf16[3,1024,128]{2,1,0:T(8,128)(2,1)S(1)}, u32[]{:S(2)}, u32[]{:S(2)}) collective-permute-start(bf16[3,1024,128]{2,1,0:T(8,128)(2,1)} %collective-permute-done), channel_id=1, source_target_pairs={{0,4},{2,6},{4,0},{6,2},{8,12},{10,14},{12,8},{14,10},{16,20},{18,... | collective-permute-start | bytes 2359304 | tf_op jit(solution)/shard_map/ppermute | solution.py:256
  81.2 22.5 %collective-permute-start.5 = (bf16[128,1024]{1,0:T(8,128)(2,1)}, bf16[128,1024]{1,0:T(8,128)(2,1)S(1)}, u32[]{:S(2)}, u32[]{:S(2)}) collective-permute-start(bf16[128,1024]{1,0:T(8,128)(2,1)} %collective-permute-done.1), channel_id=1, source_target_pairs={{0,4},{2,6},{4,0},{6,2},{8,12},{10,14},{12,8},{14,10},{16,20},{18,... | collective-permute-start | bytes 786440 | tf_op jit(solution)/shard_map/ppermute | solution.py:256
  105.0 54.4 %collective-permute-start.6 = (bf16[256,1024]{1,0:T(8,128)(2,1)S(1)}, bf16[256,1024]{1,0:T(8,128)(2,1)}, u32[]{:S(2)}, u32[]{:S(2)}) collective-permute-start(bf16[256,1024]{1,0:T(8,128)(2,1)S(1)} %maximum_select_fusion.9), channel_id=1, source_target_pairs={{0,2},{2,0},{4,6},{6,4},{8,10},{10,8},{12,14},{14,12},{16,18},{18,... | collective-permute-start | bytes 1572872 | tf_op jit(solution)/shard_map/ppermute | solution.py:256
  107.0 29.3 %collective-permute-start.4 = (bf16[3,1024,256]{2,1,0:T(8,128)(2,1)S(1)}, bf16[3,1024,256]{2,1,0:T(8,128)(2,1)S(1)}, u32[]{:S(2)}, u32[]{:S(2)}) collective-permute-start(bf16[3,1024,256]{2,1,0:T(8,128)(2,1)S(1)} %maximum_select_fusion.5), channel_id=1, source_target_pairs={{0,2},{2,0},{4,6},{6,4},{8,10},{10,8},{12,14},{14,12},{16,18},{18,... | collective-permute-start | bytes 4718600 | tf_op jit(solution)/shard_map/ppermute | solution.py:256
  108.3 25.6 %collective-permute-start.7 = (bf16[1024,512]{1,0:T(8,128)(2,1)}, bf16[1024,512]{1,0:T(8,128)(2,1)}, u32[]{:S(2)}, u32[]{:S(2)}) collective-permute-start(bf16[1024,512]{1,0:T(8,128)(2,1)} %constant_dynamic-slice_fusion.14), channel_id=1, source_target_pairs={{0,1},{1,0},{2,3},{3,2},{4,5},{5,4},{6,7},{7,6},{8,9},{9,8},{10,11... | collective-permute-start | bytes 3145736 | tf_op jit(solution)/shard_map/ppermute | solution.py:247
  133.9 24.5 %collective-permute-start.10 = (bf16[512,1024]{1,0:T(8,128)(2,1)S(1)}, bf16[512,1024]{1,0:T(8,128)(2,1)}, u32[]{:S(2)}, u32[]{:S(2)}) collective-permute-start(bf16[512,1024]{1,0:T(8,128)(2,1)S(1)} %copy-done.117), channel_id=1, source_target_pairs={{0,1},{1,0},{2,3},{3,2},{4,5},{5,4},{6,7},{7,6},{8,9},{9,8},{10,11... | collective-permute-start | bytes 3145736 | tf_op jit(solution)/shard_map/ppermute | solution.py:247
  134.9 41.3 %collective-permute-start.8 = (bf16[1024,512]{1,0:T(8,128)(2,1)}, bf16[1024,512]{1,0:T(8,128)(2,1)S(1)}, u32[]{:S(2)}, u32[]{:S(2)}) collective-permute-start(bf16[1024,512]{1,0:T(8,128)(2,1)} %collective-permute-done.7), channel_id=1, source_target_pairs={{0,4},{2,6},{4,0},{6,2},{8,12},{10,14},{12,8},{14,10},{16,20},{18,... | collective-permute-start | bytes 3145736 | tf_op jit(solution)/shard_map/ppermute | solution.py:256
  158.3 24.7 %collective-permute-start.11 = (bf16[512,1024]{1,0:T(8,128)(2,1)}, bf16[512,1024]{1,0:T(8,128)(2,1)S(1)}, u32[]{:S(2)}, u32[]{:S(2)}) collective-permute-start(bf16[512,1024]{1,0:T(8,128)(2,1)} %collective-permute-done.10), channel_id=1, source_target_pairs={{0,4},{2,6},{4,0},{6,2},{8,12},{10,14},{12,8},{14,10},{16,20},{18,... | collective-permute-start | bytes 3145736 | tf_op jit(solution)/shard_map/ppermute | solution.py:256
  161.3 67.0 %copy-start.53 = (f32[512,1024]{1,0:T(8,128)}, f32[512,1024]{1,0:T(8,128)S(1)}, u32[]{:S(2)}) copy-start(f32[512,1024]{1,0:T(8,128)S(1)} %get-tuple-element.204) | copy-start | bytes 6291460
  161.3 9.3 collective-permute-start.13
  170.7 5.0 collective-permute-start.16
  175.7 6.5 collective-permute-start.19
  178.5 39.4 %collective-permute-start.9 = (bf16[1024,1024]{1,0:T(8,128)(2,1)S(1)}, bf16[1024,1024]{1,0:T(8,128)(2,1)}, u32[]{:S(2)}, u32[]{:S(2)}) collective-permute-start(bf16[1024,1024]{1,0:T(8,128)(2,1)S(1)} %maximum_select_fusion.2), channel_id=1, source_target_pairs={{0,2},{2,0},{4,6},{6,4},{8,10},{10,8},{12,14},{14,12},{16,18},{18,... | collective-permute-start | bytes 6291464 | tf_op jit(solution)/shard_map/ppermute | solution.py:256
  182.1 12.2 %collective-permute-start.20 = (bf16[512,256]{1,0:T(8,128)(2,1)}, bf16[512,256]{1,0:T(8,128)(2,1)S(1)}, u32[]{:S(2)}, u32[]{:S(2)}) collective-permute-start(bf16[512,256]{1,0:T(8,128)(2,1)} %collective-permute-done.19), channel_id=1, source_target_pairs={{0,4},{2,6},{4,0},{6,2},{8,12},{10,14},{12,8},{14,10},{16,20},{18,... | collective-permute-start | bytes 786440 | tf_op jit(solution)/shard_map/ppermute | solution.py:256
  185.7 42.6 %collective-permute-start.12 = (bf16[1024,1024]{1,0:T(8,128)(2,1)S(1)}, bf16[1024,1024]{1,0:T(8,128)(2,1)}, u32[]{:S(2)}, u32[]{:S(2)}) collective-permute-start(bf16[1024,1024]{1,0:T(8,128)(2,1)S(1)} %maximum_select_fusion.3), channel_id=1, source_target_pairs={{0,2},{2,0},{4,6},{6,4},{8,10},{10,8},{12,14},{14,12},{16,18},{18,... | collective-permute-start | bytes 6291464 | tf_op jit(solution)/shard_map/ppermute | solution.py:256
  186.8 18.6 %collective-permute-start.22 = (bf16[256,512]{1,0:T(8,128)(2,1)S(1)}, bf16[256,512]{1,0:T(8,128)(2,1)}, u32[]{:S(2)}, u32[]{:S(2)}) collective-permute-start(bf16[256,512]{1,0:T(8,128)(2,1)S(1)} %copy-done.152), channel_id=1, source_target_pairs={{0,1},{1,0},{2,3},{3,2},{4,5},{5,4},{6,7},{7,6},{8,9},{9,8},{10,11... | collective-permute-start | bytes 786440 | tf_op jit(solution)/shard_map/ppermute | solution.py:247
  193.0 19.3 %collective-permute-start.14 = (bf16[3,512,64]{2,1,0:T(8,128)(2,1)S(1)}, bf16[3,512,64]{2,1,0:T(8,128)(2,1)S(1)}, u32[]{:S(2)}, u32[]{:S(2)}) collective-permute-start(bf16[3,512,64]{2,1,0:T(8,128)(2,1)S(1)} %collective-permute-done.13), channel_id=1, source_target_pairs={{0,4},{2,6},{4,0},{6,2},{8,12},{10,14},{12,8},{14,10},{16,20},{18,... | collective-permute-start | bytes 589832 | tf_op jit(solution)/shard_map/ppermute | solution.py:256
  194.4 11.0 collective-permute-start.17
  205.4 10.9 collective-permute-start.21
  205.4 8.9 collective-permute-start.23
  212.4 83.6 %collective-permute-start.18 = (bf16[128,512]{1,0:T(8,128)(2,1)S(1)}, bf16[128,512]{1,0:T(8,128)(2,1)S(1)}, u32[]{:S(2)}, u32[]{:S(2)}) collective-permute-start(bf16[128,512]{1,0:T(8,128)(2,1)S(1)} %maximum_select_fusion.13), channel_id=1, source_target_pairs={{0,2},{2,0},{4,6},{6,4},{8,10},{10,8},{12,14},{14,12},{16,18},{18,... | collective-permute-start | bytes 393224 | tf_op jit(solution)/shard_map/ppermute | solution.py:256
  214.3 55.9 %collective-permute-start.15 = (bf16[3,512,128]{2,1,0:T(8,128)(2,1)S(1)}, bf16[3,512,128]{2,1,0:T(8,128)(2,1)}, u32[]{:S(2)}, u32[]{:S(2)}) collective-permute-start(bf16[3,512,128]{2,1,0:T(8,128)(2,1)S(1)} %maximum_select_fusion.12), channel_id=1, source_target_pairs={{0,2},{2,0},{4,6},{6,4},{8,10},{10,8},{12,14},{14,12},{16,18},{18,... | collective-permute-start | bytes 1179656 | tf_op jit(solution)/shard_map/ppermute | solution.py:256
  216.3 111.1 %collective-permute-start.26 = (bf16[2048,512]{1,0:T(8,128)(2,1)}, bf16[2048,512]{1,0:T(8,128)(2,1)}, u32[]{:S(2)}, u32[]{:S(2)}) collective-permute-start(bf16[2048,512]{1,0:T(8,128)(2,1)} %dynamic-slice_convert_fusion), channel_id=1, source_target_pairs={{0,1},{1,0},{2,3},{3,2},{4,5},{5,4},{6,7},{7,6},{8,9},{9,8},{10,11... | collective-permute-start | bytes 6291464 | tf_op jit(solution)/shard_map/ppermute | solution.py:247
  217.9 104.6 %collective-permute-start.24 = (bf16[512,512]{1,0:T(8,128)(2,1)}, bf16[512,512]{1,0:T(8,128)(2,1)}, u32[]{:S(2)}, u32[]{:S(2)}) collective-permute-start(bf16[512,512]{1,0:T(8,128)(2,1)} %maximum_select_fusion.11), channel_id=1, source_target_pairs={{0,2},{2,0},{4,6},{6,4},{8,10},{10,8},{12,14},{14,12},{16,18},{18,... | collective-permute-start | bytes 1572872 | tf_op jit(solution)/shard_map/ppermute | solution.py:256
  241.3 54.7 %copy-start.42 = (f32[8,256,512]{2,1,0:T(8,128)}, f32[8,256,512]{2,1,0:T(8,128)S(1)}, u32[]{:S(2)}) copy-start(f32[8,256,512]{2,1,0:T(8,128)S(1)} %get-tuple-element.208) | copy-start | bytes 12582916
  528.2 64.4 %collective-permute-start.56 = (bf16[512,512]{1,0:T(8,128)(2,1)}, bf16[512,512]{1,0:T(8,128)(2,1)}, u32[]{:S(2)}, u32[]{:S(2)}) collective-permute-start(bf16[512,512]{1,0:T(8,128)(2,1)} %slice.278), channel_id=1, source_target_pairs={{0,2},{2,0},{4,6},{6,4},{8,10},{10,8},{12,14},{14,12},{16,18},{18,... | collective-permute-start | bytes 1572872 | tf_op jit(solution)/shard_map/ppermute | solution.py:256
  529.4 131.2 %collective-permute-start.55 = (bf16[512,512]{1,0:T(8,128)(2,1)}, bf16[512,512]{1,0:T(8,128)(2,1)}, u32[]{:S(2)}, u32[]{:S(2)}) collective-permute-start(bf16[512,512]{1,0:T(8,128)(2,1)} %constant_dynamic-slice_fusion.2), channel_id=1, source_target_pairs={{0,2},{2,0},{4,6},{6,4},{8,10},{10,8},{12,14},{14,12},{16,18},{18,... | collective-permute-start | bytes 1572872 | tf_op jit(solution)/shard_map/ppermute | solution.py:256
  530.3 48.0 %collective-permute-start.50 = (bf16[128,512]{1,0:T(8,128)(2,1)}, bf16[128,512]{1,0:T(8,128)(2,1)S(1)}, u32[]{:S(2)}, u32[]{:S(2)}) collective-permute-start(bf16[128,512]{1,0:T(8,128)(2,1)} %slice.274), channel_id=1, source_target_pairs={{0,2},{2,0},{4,6},{6,4},{8,10},{10,8},{12,14},{14,12},{16,18},{18,... | collective-permute-start | bytes 393224 | tf_op jit(solution)/shard_map/ppermute | solution.py:256
  531.2 56.9 %collective-permute-start.49 = (bf16[128,512]{1,0:T(8,128)(2,1)}, bf16[128,512]{1,0:T(8,128)(2,1)}, u32[]{:S(2)}, u32[]{:S(2)}) collective-permute-start(bf16[128,512]{1,0:T(8,128)(2,1)} %constant_dynamic-slice_fusion.4), channel_id=1, source_target_pairs={{0,2},{2,0},{4,6},{6,4},{8,10},{10,8},{12,14},{14,12},{16,18},{18,... | collective-permute-start | bytes 393224 | tf_op jit(solution)/shard_map/ppermute | solution.py:256
  553.2 10.4 collective-permute-start.41
  563.7 1.4 collective-permute-start.42
  565.1 4.1 collective-permute-start.43
  569.1 9.1 collective-permute-start.44
  578.3 12.6 %collective-permute-start.47 = (bf16[1536,128]{1,0:T(8,128)(2,1)}, bf16[1536,128]{1,0:T(8,128)(2,1)}, u32[]{:S(2)}, u32[]{:S(2)}) collective-permute-start(bf16[1536,128]{1,0:T(8,128)(2,1)} %slice.272), channel_id=1, source_target_pairs={{0,2},{2,0},{4,6},{6,4},{8,10},{10,8},{12,14},{14,12},{16,18},{18,... | collective-permute-start | bytes 1179656 | tf_op jit(solution)/shard_map/ppermute | solution.py:256
  578.3 5.7 collective-permute-start.45
  584.0 5.8 collective-permute-start.51
  588.1 6.0 collective-permute-start.53
  589.8 7.0 collective-permute-start.46
  590.9 4.5 collective-permute-start.58
  592.6 3.9 collective-permute-start.32
  594.2 35.6 %collective-permute-start.27 = (bf16[512,1024]{1,0:T(8,128)(2,1)}, bf16[512,1024]{1,0:T(8,128)(2,1)S(1)}, u32[]{:S(2)}, u32[]{:S(2)}) collective-permute-start(bf16[512,1024]{1,0:T(8,128)(2,1)} %add_convert_fusion.5), channel_id=1, source_target_pairs={{0,1},{1,0},{2,3},{3,2},{4,5},{5,4},{6,7},{7,6},{8,9},{9,8},{10,11... | collective-permute-start | bytes 3145736 | tf_op jit(solution)/shard_map/ppermute | solution.py:247
  595.4 33.4 %collective-permute-start.48 = (bf16[1536,128]{1,0:T(8,128)(2,1)S(1)}, bf16[1536,128]{1,0:T(8,128)(2,1)S(1)}, u32[]{:S(2)}, u32[]{:S(2)}) collective-permute-start(bf16[1536,128]{1,0:T(8,128)(2,1)S(1)} %slice_add_fusion.6), channel_id=1, source_target_pairs={{0,1},{1,0},{2,3},{3,2},{4,5},{5,4},{6,7},{7,6},{8,9},{9,8},{10,11... | collective-permute-start | bytes 1179656 | tf_op jit(solution)/shard_map/ppermute | solution.py:247
  596.6 102.9 %collective-permute-start.52 = (bf16[512,512]{1,0:T(8,128)(2,1)}, bf16[512,512]{1,0:T(8,128)(2,1)S(1)}, u32[]{:S(2)}, u32[]{:S(2)}) collective-permute-start(bf16[512,512]{1,0:T(8,128)(2,1)} %constant_dynamic-slice_fusion.3), channel_id=1, source_target_pairs={{0,2},{2,0},{4,6},{6,4},{8,10},{10,8},{12,14},{14,12},{16,18},{18,... | collective-permute-start | bytes 1572872 | tf_op jit(solution)/shard_map/ppermute | solution.py:256
  596.8 126.5 %collective-permute-start.25 = (bf16[2048,512]{1,0:T(8,128)(2,1)S(1)}, bf16[2048,512]{1,0:T(8,128)(2,1)S(1)}, u32[]{:S(2)}, u32[]{:S(2)}) collective-permute-start(bf16[2048,512]{1,0:T(8,128)(2,1)S(1)} %copy-done.95), channel_id=1, source_target_pairs={{0,1},{1,0},{2,3},{3,2},{4,5},{5,4},{6,7},{7,6},{8,9},{9,8},{10,11... | collective-permute-start | bytes 6291464 | tf_op jit(solution)/shard_map/ppermute | solution.py:247
  628.9 92.5 %collective-permute-start.29 = (bf16[3072,256]{1,0:T(8,128)(2,1)S(1)}, bf16[3072,256]{1,0:T(8,128)(2,1)S(1)}, u32[]{:S(2)}, u32[]{:S(2)}) collective-permute-start(bf16[3072,256]{1,0:T(8,128)(2,1)S(1)} %copy-done.106), channel_id=1, source_target_pairs={{0,2},{2,0},{4,6},{6,4},{8,10},{10,8},{12,14},{14,12},{16,18},{18,... | collective-permute-start | bytes 4718600 | tf_op jit(solution)/shard_map/ppermute | solution.py:256
  629.8 69.8 %collective-permute-start.57 = (bf16[512,512]{1,0:T(8,128)(2,1)S(1)}, bf16[512,512]{1,0:T(8,128)(2,1)S(1)}, u32[]{:S(2)}, u32[]{:S(2)}) collective-permute-start(bf16[512,512]{1,0:T(8,128)(2,1)S(1)} %slice_add_fusion.3), channel_id=1, source_target_pairs={{0,1},{1,0},{2,3},{3,2},{4,5},{5,4},{6,7},{7,6},{8,9},{9,8},{10,11... | collective-permute-start | bytes 1572872 | tf_op jit(solution)/shard_map/ppermute | solution.py:247
  660.6 35.1 %collective-permute-start.59 = (bf16[512,512]{1,0:T(8,128)(2,1)S(1)}, bf16[512,512]{1,0:T(8,128)(2,1)S(1)}, u32[]{:S(2)}, u32[]{:S(2)}) collective-permute-start(bf16[512,512]{1,0:T(8,128)(2,1)S(1)} %dynamic-slice_add_fusion.1), channel_id=1, source_target_pairs={{0,1},{1,0},{2,3},{3,2},{4,5},{5,4},{6,7},{7,6},{8,9},{9,8},{10,11... | collective-permute-start | bytes 1572872 | tf_op jit(solution)/shard_map/ppermute | solution.py:247
  695.7 14.9 %collective-permute-start.54 = (bf16[512,512]{1,0:T(8,128)(2,1)S(1)}, bf16[512,512]{1,0:T(8,128)(2,1)S(1)}, u32[]{:S(2)}, u32[]{:S(2)}) collective-permute-start(bf16[512,512]{1,0:T(8,128)(2,1)S(1)} %slice_add_fusion.4), channel_id=1, source_target_pairs={{0,1},{1,0},{2,3},{3,2},{4,5},{5,4},{6,7},{7,6},{8,9},{9,8},{10,11... | collective-permute-start | bytes 1572872 | tf_op jit(solution)/shard_map/ppermute | solution.py:247
  699.5 12.1 %collective-permute-start.31 = (bf16[256,1024]{1,0:T(8,128)(2,1)S(1)}, bf16[256,1024]{1,0:T(8,128)(2,1)S(1)}, u32[]{:S(2)}, u32[]{:S(2)}) collective-permute-start(bf16[256,1024]{1,0:T(8,128)(2,1)S(1)} %copy-done.141), channel_id=1, source_target_pairs={{0,2},{2,0},{4,6},{6,4},{8,10},{10,8},{12,14},{14,12},{16,18},{18,... | collective-permute-start | bytes 1572872 | tf_op jit(solution)/shard_map/ppermute | solution.py:256
  699.6 20.7 %collective-permute-start.33 = (bf16[256,1024]{1,0:T(8,128)(2,1)S(1)}, bf16[256,1024]{1,0:T(8,128)(2,1)S(1)}, u32[]{:S(2)}, u32[]{:S(2)}) collective-permute-start(bf16[256,1024]{1,0:T(8,128)(2,1)S(1)} %slice_add_fusion.5), channel_id=1, source_target_pairs={{0,1},{1,0},{2,3},{3,2},{4,5},{5,4},{6,7},{7,6},{8,9},{9,8},{10,11... | collective-permute-start | bytes 1572872 | tf_op jit(solution)/shard_map/ppermute | solution.py:247
  710.6 74.8 %collective-permute-start.28 = (bf16[3072,256]{1,0:T(8,128)(2,1)}, bf16[3072,256]{1,0:T(8,128)(2,1)}, u32[]{:S(2)}, u32[]{:S(2)}) collective-permute-start(bf16[3072,256]{1,0:T(8,128)(2,1)} %constant_dynamic-slice_fusion.9), channel_id=1, source_target_pairs={{0,2},{2,0},{4,6},{6,4},{8,10},{10,8},{12,14},{14,12},{16,18},{18,... | collective-permute-start | bytes 4718600 | tf_op jit(solution)/shard_map/ppermute | solution.py:256
  711.6 68.3 %collective-permute-start.35 = (bf16[1024,1024]{1,0:T(8,128)(2,1)}, bf16[1024,1024]{1,0:T(8,128)(2,1)}, u32[]{:S(2)}, u32[]{:S(2)}) collective-permute-start(bf16[1024,1024]{1,0:T(8,128)(2,1)} %slice.263), channel_id=1, source_target_pairs={{0,2},{2,0},{4,6},{6,4},{8,10},{10,8},{12,14},{14,12},{16,18},{18,... | collective-permute-start | bytes 6291464 | tf_op jit(solution)/shard_map/ppermute | solution.py:256
  720.3 62.3 %collective-permute-start.38 = (bf16[1024,1024]{1,0:T(8,128)(2,1)}, bf16[1024,1024]{1,0:T(8,128)(2,1)}, u32[]{:S(2)}, u32[]{:S(2)}) collective-permute-start(bf16[1024,1024]{1,0:T(8,128)(2,1)} %slice.265), channel_id=1, source_target_pairs={{0,2},{2,0},{4,6},{6,4},{8,10},{10,8},{12,14},{14,12},{16,18},{18,... | collective-permute-start | bytes 6291464 | tf_op jit(solution)/shard_map/ppermute | solution.py:256
  721.4 69.1 %collective-permute-start.40 = (bf16[2432,512]{1,0:T(8,128)(2,1)}, bf16[2432,512]{1,0:T(8,128)(2,1)}, u32[]{:S(2)}, u32[]{:S(2)}) collective-permute-start(bf16[2432,512]{1,0:T(8,128)(2,1)} %fusion.10), channel_id=1, source_target_pairs={{0,2},{2,0},{4,6},{6,4},{8,10},{10,8},{12,14},{14,12},{16,18},{18,... | collective-permute-start | bytes 7471112 | tf_op jit(solution)/shard_map/ppermute | solution.py:256
  724.6 61.0 %collective-permute-start.30 = (bf16[3072,256]{1,0:T(8,128)(2,1)}, bf16[3072,256]{1,0:T(8,128)(2,1)}, u32[]{:S(2)}, u32[]{:S(2)}) collective-permute-start(bf16[3072,256]{1,0:T(8,128)(2,1)} %slice_add_fusion.2), channel_id=1, source_target_pairs={{0,1},{1,0},{2,3},{3,2},{4,5},{5,4},{6,7},{7,6},{8,9},{9,8},{10,11... | collective-permute-start | bytes 4718600 | tf_op jit(solution)/shard_map/ppermute | solution.py:247
  780.0 112.7 %collective-permute-start.34 = (bf16[1024,1024]{1,0:T(8,128)(2,1)}, bf16[1024,1024]{1,0:T(8,128)(2,1)}, u32[]{:S(2)}, u32[]{:S(2)}) collective-permute-start(bf16[1024,1024]{1,0:T(8,128)(2,1)} %constant_dynamic-slice_fusion.7), channel_id=1, source_target_pairs={{0,2},{2,0},{4,6},{6,4},{8,10},{10,8},{12,14},{14,12},{16,18},{18,... | collective-permute-start | bytes 6291464 | tf_op jit(solution)/shard_map/ppermute | solution.py:256
  782.6 13.1 %collective-permute-start.60 = (bf16[512,1664]{1,0:T(8,128)(2,1)S(1)}, bf16[512,1664]{1,0:T(8,128)(2,1)S(1)}, u32[]{:S(2)}, u32[]{:S(2)}) collective-permute-start(bf16[512,1664]{1,0:T(8,128)(2,1)S(1)} %constant_dynamic-slice_fusion), channel_id=1, source_target_pairs={{0,2},{2,0},{4,6},{6,4},{8,10},{10,8},{12,14},{14,12},{16,18},{18,... | collective-permute-start | bytes 5111816 | tf_op jit(solution)/shard_map/ppermute | solution.py:256
  785.4 113.7 %collective-permute-start.37 = (bf16[1024,1024]{1,0:T(8,128)(2,1)}, bf16[1024,1024]{1,0:T(8,128)(2,1)}, u32[]{:S(2)}, u32[]{:S(2)}) collective-permute-start(bf16[1024,1024]{1,0:T(8,128)(2,1)} %constant_dynamic-slice_fusion.6), channel_id=1, source_target_pairs={{0,2},{2,0},{4,6},{6,4},{8,10},{10,8},{12,14},{14,12},{16,18},{18,... | collective-permute-start | bytes 6291464 | tf_op jit(solution)/shard_map/ppermute | solution.py:256
  785.5 107.1 %collective-permute-start.36 = (bf16[1024,1024]{1,0:T(8,128)(2,1)S(1)}, bf16[1024,1024]{1,0:T(8,128)(2,1)}, u32[]{:S(2)}, u32[]{:S(2)}) collective-permute-start(bf16[1024,1024]{1,0:T(8,128)(2,1)S(1)} %slice_add_fusion.1), channel_id=1, source_target_pairs={{0,1},{1,0},{2,3},{3,2},{4,5},{5,4},{6,7},{7,6},{8,9},{9,8},{10,11... | collective-permute-start | bytes 6291464 | tf_op jit(solution)/shard_map/ppermute | solution.py:247
  790.5 108.6 %collective-permute-start.39 = (bf16[1024,1024]{1,0:T(8,128)(2,1)S(1)}, bf16[1024,1024]{1,0:T(8,128)(2,1)}, u32[]{:S(2)}, u32[]{:S(2)}) collective-permute-start(bf16[1024,1024]{1,0:T(8,128)(2,1)S(1)} %slice_add_fusion), channel_id=1, source_target_pairs={{0,1},{1,0},{2,3},{3,2},{4,5},{5,4},{6,7},{7,6},{8,9},{9,8},{10,11... | collective-permute-start | bytes 6291464 | tf_op jit(solution)/shard_map/ppermute | solution.py:247
  (221 other events, 1837.1 us)

commit v2 on v1

v2 whole, which is shorter than its diff:
```python
import math

import jax
import jax.numpy as jnp
from jax import lax
from jax.experimental import pallas as pl
from jax.experimental.pallas import tpu as pltpu
from jax.sharding import PartitionSpec as P

D = 1024
HDIM = 64
DDEC = 512
DHDIM = 32
RGB_PIX = 768
SIDE = 16
NPATCH = 256
VIS = 64

HIGHEST = lax.Precision.HIGHEST
EPSILON = 1e-06
MASKED = -1e30
BF16 = jnp.bfloat16
F32 = jnp.float32
LANES = 128
VMEM_LIMIT = 48 * 1024 * 1024
RING_VMEM_LIMIT = 58 * 1024 * 1024
MESH = pl.DeviceIdType.MESH


def dot(left, right):
    return jnp.dot(left, right, preferred_element_type=F32)


def dot_tn(left, right):
    return lax.dot_general(left, right, (((0,), (0,)), ((), ())), preferred_element_type=F32)


def dot_nt(left, right):
    return lax.dot_general(left, right, (((1,), (1,)), ((), ())), preferred_element_type=F32)


def normalize(values):
    center = values - jnp.mean(values, -1, keepdims=True)
    rstd = lax.rsqrt(jnp.mean(center * center, -1, keepdims=True) + EPSILON)
    return center * rstd, rstd


def layer_norm(values, scales, shifts):
    return (normalize(values)[0] * scales + shifts).astype(BF16)


def layer_norm_back(grad, values, scales):
    unit, rstd = normalize(values)
    scaled = grad * scales
    mean_grad = jnp.mean(scaled, -1, keepdims=True)
    mean_along = jnp.mean(scaled * unit, -1, keepdims=True)
    grad_in = rstd * (scaled - mean_grad - unit * mean_along)
    return grad_in, jnp.sum(grad * unit, 0), jnp.sum(grad, 0)


def code_tables(ratios, features):
    quarter = features // 4
    index_f = jnp.arange(quarter, dtype=F32)
    frequencies = jnp.exp(index_f * (-math.log(10000.0) / quarter))
    places = jnp.arange(SIDE).astype(F32)
    angle = (places[None, :] * ratios[:, None])[..., None] * frequencies
    return jnp.concatenate([jnp.sin(angle), jnp.cos(angle)], -1)


def slot_codes(slot_ids, ratios, features):
    table = code_tables(ratios, features)
    places = jnp.arange(SIDE)
    row = (slot_ids[..., None] // SIDE == places).astype(F32)
    col = (slot_ids[..., None] % SIDE == places).astype(F32)
    pick = lambda one_hot: jnp.einsum("bsp,bpf->bsf", one_hot, table, precision=HIGHEST)
    return jnp.concatenate([pick(row), pick(col)], -1)


def grid_codes(ratios, features):
    table = code_tables(ratios, features)
    images, _, half = table.shape
    row = jnp.broadcast_to(table[:, :, None, :], (images, SIDE, SIDE, half))
    col = jnp.broadcast_to(table[:, None, :, :], (images, SIDE, SIDE, half))
    return jnp.concatenate([row, col], -1).reshape(images, NPATCH, features)


def head_rows(values, head_size, heads):
    lane = lax.broadcasted_iota(jnp.int32, (1, LANES), 1)
    return jnp.concatenate(
        [jnp.where(lane // head_size == h, values, 0).astype(BF16) for h in heads], 0
    )


def head_parts(values, head_size, seq, merge):
    return [
        values[j * head_size : (j + 1) * head_size, j * seq : (j + 1) * seq] for j in range(merge)
    ]


def masked_scores(keys, queries, valid):
    scores = dot_nt(keys, queries)
    if valid is not None:
        scores = jnp.where(valid > 0.0, scores, MASKED)
    return scores


def attend_rows(head_size, merge, q_ref, k_ref, v_ref, o_ref, valid):
    seq, width = q_ref.shape
    for g in range(width // LANES):
        lanes = slice(g * LANES, (g + 1) * LANES)
        queries, keys, values = q_ref[:, lanes], k_ref[:, lanes], v_ref[:, lanes]
        values_t = jnp.transpose(values)
        parts = []
        for h in range(0, LANES // head_size, merge):
            scores = masked_scores(
                keys, head_rows(queries, head_size, range(h, h + merge)), valid
            )
            top = jnp.max(scores, 0, keepdims=True)
            power = jnp.exp(scores - top)
            total = jnp.sum(power, 0, keepdims=True)
            rows = slice(h * head_size, (h + merge) * head_size)
            mixed = dot(values_t[rows], power.astype(BF16)) * (1.0 / total)
            parts += head_parts(mixed, head_size, seq, merge)
        o_ref[:, lanes] = jnp.transpose(jnp.concatenate(parts, 0)).astype(BF16)


def attend_back_rows(
    head_size, merge, q_ref, k_ref, v_ref, g_ref, dq_ref, dk_ref, dv_ref, valid
):
    seq, width = q_ref.shape
    factor = head_size ** (-0.5)
    for g in range(width // LANES):
        lanes = slice(g * LANES, (g + 1) * LANES)
        queries, keys, values, grads = (
            q_ref[:, lanes],
            k_ref[:, lanes],
            v_ref[:, lanes],
            g_ref[:, lanes],
        )
        keys_t = jnp.transpose(keys)
        parts, dk_sum, dv_sum = [], 0.0, 0.0
        for h in range(0, LANES // head_size, merge):
            own_q = head_rows(queries, head_size, range(h, h + merge))
            own_g = head_rows(grads, head_size, range(h, h + merge))
            scores = masked_scores(keys, own_q, valid)
            top = jnp.max(scores, 0, keepdims=True)
            power = jnp.exp(scores - top)
            weights = power * (1.0 / jnp.sum(power, 0, keepdims=True))
            dv_sum += dot(weights.astype(BF16), own_g)
            grad_weights = dot_nt(values, own_g)
            along = jnp.sum(weights * grad_weights, 0, keepdims=True)
            grad_scores = (weights * (grad_weights - along)).astype(BF16)
            dk_sum += dot(grad_scores, own_q)
            rows = slice(h * head_size, (h + merge) * head_size)
            grad_q = dot(keys_t[rows], grad_scores) * factor
            parts += head_parts(grad_q, head_size, seq, merge)
        dq_ref[:, lanes] = jnp.transpose(jnp.concatenate(parts, 0)).astype(BF16)
        dk_ref[:, lanes] = dk_sum.astype(BF16)
        dv_ref[:, lanes] = dv_sum.astype(BF16)


def valid_rows(counts, seq, merge):
    valid = (jnp.arange(seq)[None, :, None] < counts[:, None, None]).astype(F32)
    return jnp.broadcast_to(valid, (counts.shape[0], seq, merge * seq))


def attention_call(rows_fn, arrays, valid, seq, n_out, head_size, merge, flop_factor):
    rows, width = arrays[0].shape
    images = rows // seq
    block = pl.BlockSpec((seq, width), lambda i: (i, 0))
    out = jax.ShapeDtypeStruct((rows, width), BF16)
    in_specs, masks = [block] * len(arrays), []
    if valid is not None:
        in_specs.append(pl.BlockSpec((None,) + valid.shape[1:], lambda i: (i, 0, 0)))
        masks = [valid]

    def kernel(*refs):
        refs = list(refs)
        mask = refs.pop(len(arrays))[...] if masks else None
        rows_fn(head_size, merge, *refs, mask)

    return pl.pallas_call(
        kernel,
        grid=(images,),
        in_specs=in_specs,
        out_specs=[block] * n_out,
        out_shape=[out] * n_out,
        compiler_params=pltpu.CompilerParams(vmem_limit_bytes=VMEM_LIMIT),
        cost_estimate=pl.CostEstimate(
            flops=flop_factor * rows * seq * width * (LANES // head_size),
            bytes_accessed=(len(arrays) + n_out) * rows * width * 2,
            transcendentals=rows * seq * width // head_size,
        ),
    )(*arrays, *masks)


def attend(queries, keys, values, counts, seq, head_size, masked):
    merge = LANES // head_size
    valid = valid_rows(counts, seq, merge) if masked else None
    arrays = [queries, keys, values]
    return attention_call(attend_rows, arrays, valid, seq, 1, head_size, merge, 4)[0]


def attend_back(queries, keys, values, grads, counts, seq, head_size, masked):
    merge = 1 if masked else LANES // head_size
    valid = valid_rows(counts, seq, merge) if masked else None
    arrays = [queries, keys, values, grads]
    return attention_call(attend_back_rows, arrays, valid, seq, 3, head_size, merge, 10)


def up_kernel(x_ref, w_ref, active_ref, slope_ref):
    pre = dot(x_ref[...], w_ref[...])
    cdf = 0.5 + 0.5 * lax.erf(pre * math.sqrt(0.5))
    density = jnp.exp(-0.5 * pre * pre) * (1.0 / math.sqrt(2.0 * math.pi))
    active_ref[...] = (pre * cdf).astype(BF16)
    slope_ref[...] = (cdf + pre * density).astype(BF16)


def up_projection(rows_in, weight):
    rows, depth = rows_in.shape
    width = weight.shape[1]
    row_block = math.gcd(rows, 512)
    col_block = math.gcd(width, 512)
    out = jax.ShapeDtypeStruct((rows, width), BF16)
    spec = pl.BlockSpec((row_block, col_block), lambda i, j: (i, j))
    return pl.pallas_call(
        up_kernel,
        grid=(rows // row_block, width // col_block),
        in_specs=[
            pl.BlockSpec((row_block, depth), lambda i, j: (i, 0)),
            pl.BlockSpec((depth, col_block), lambda i, j: (0, j)),
        ],
        out_specs=[spec, spec],
        out_shape=[out, out],
        compiler_params=pltpu.CompilerParams(vmem_limit_bytes=VMEM_LIMIT),
        cost_estimate=pl.CostEstimate(
            flops=2 * rows * depth * width,
            bytes_accessed=2 * (rows * depth + depth * width + 2 * rows * width),
            transcendentals=2 * rows * width,
        ),
    )(rows_in, weight)


class Links:
    def __init__(self):
        self.shards = lax.axis_size("freq")
        self.fast = self.shards == 2 and lax.axis_size("dp") == 16
        self.place = lax.axis_index("freq")
        index = lax.axis_index("dp")
        self.core = index % 2
        self.row = (index // 2) % 2
        depth = index // 4
        along = jnp.where(self.row == 0, depth, 7 - depth)
        self.rank = jnp.where(self.core == 0, along, (8 - along) % 8)
        cycle = [z * 4 for z in range(4)] + [z * 4 + 2 for z in range(3, -1, -1)]
        self.ring = []
        for i in range(8):
            self.ring.append((cycle[i], cycle[(i + 1) % 8]))
            self.ring.append((cycle[i] + 1, cycle[(i + 7) % 8] + 1))

    def over_x(self, values):
        return lax.ppermute(values, "freq", [(0, 1), (1, 0)])

    def over(self, bit, values):
        return lax.ppermute(values, "dp", [(i, i ^ bit) for i in range(16)])

    def over_core(self, values):
        return self.over(1, values)

    def over_ring(self, values):
        return lax.ppermute(values, "dp", self.ring)


def halves(values, which, axis):
    size = values.shape[axis] // 2
    return (
        lax.dynamic_slice_in_dim(values, which * size, size, axis),
        lax.dynamic_slice_in_dim(values, (1 - which) * size, size, axis),
    )


def ordered(which, own, other, axis):
    return jnp.where(
        which == 0,
        jnp.concatenate([own, other], axis),
        jnp.concatenate([other, own], axis),
    )


class Fetch:
    STEPS = 4

    def __init__(self, sources, targets, send, recv):
        self.sources, self.targets, self.send, self.recv = sources, targets, send, recv
        index, across = lax.axis_index("dp"), lax.axis_index("freq")
        core, row = index % 2, (index // 2) % 2
        self.quarter = index % 4
        self.next_quarter = self.quarter + 2 - 4 * row
        self.facing = (index, 1 - across)
        self.beside = (index + 2 - 4 * row, across)
        self.twin = (index + 1 - 2 * core, across)

    def greet(self):
        barrier = pltpu.get_barrier_semaphore()
        for partner in (self.facing, self.beside, self.twin):
            pl.semaphore_signal(barrier, inc=1, device_id=partner, device_id_type=MESH)
        pl.semaphore_wait(barrier, 3)

    def view(self, ref, quarter):
        rows = ref.shape[-2] // 4
        place = pl.ds(pl.multiple_of(quarter * rows, 16), rows)
        return ref.at[:, place] if len(ref.shape) == 3 else ref.at[place]

    def copy(self, i, step):
        quarter = self.next_quarter if step == 3 else self.quarter
        target = self.view(self.targets[i], quarter)
        return pltpu.make_async_remote_copy(
            src_ref=self.view(self.sources[i], quarter) if step == 0 else target,
            dst_ref=target,
            send_sem=self.send.at[step, i],
            recv_sem=self.recv.at[step, i],
            device_id=(self.facing, self.beside, self.twin, self.twin)[step],
            device_id_type=MESH,
        )

    def start(self, items):
        for i in items:
            self.copy(i, 0).start()

    def pass_on(self, items):
        for i in items:
            self.copy(i, 0).wait_recv()
            self.copy(i, 1).start()
            self.copy(i, 2).start()

    def pass_on_last(self, items):
        for i in items:
            self.copy(i, 1).wait_recv()
            self.copy(i, 3).start()

    def finish(self):
        for i in range(len(self.sources)):
            for step in range(self.STEPS):
                self.copy(i, step).wait_send()
                if step >= 2:
                    self.copy(i, step).wait_recv()


def head_start_kernel(rows_ref, qkv_ref, out_ref, cot_ref, head_ref, *refs):
    got_ref, new_qkv, new_out, partial_ref, tiles, sums = refs[:6]
    send, recv, row_send, row_recv, tile_sem, sum_sem = refs[6:]
    fetch = Fetch([qkv_ref, out_ref], [new_qkv, new_out], send, recv)
    fetch.greet()
    rows_copy = pltpu.make_async_remote_copy(
        src_ref=rows_ref,
        dst_ref=got_ref,
        send_sem=row_send,
        recv_sem=row_recv,
        device_id=fetch.facing,
        device_id_type=MESH,
    )
    fetch.start([0, 1])
    tile = tiles.shape[1]
    count = cot_ref.shape[0] // tile

    def load(i, slot):
        return pltpu.make_async_copy(
            cot_ref.at[pl.ds(i * tile, tile)], tiles.at[slot], tile_sem.at[slot]
        )

    def store(i, slot):
        return pltpu.make_async_copy(
            sums.at[slot], partial_ref.at[pl.ds(i * tile, tile)], sum_sem.at[slot]
        )

    load(0, 0).start()
    load(1, 1).start()

    def body(pair, carry):
        for slot in range(2):
            i = pair * 2 + slot
            load(i, slot).wait()

            @pl.when(pair > 0)
            def _():
                store(i - 2, slot).wait()

            sums[slot] = dot_nt(tiles[slot], head_ref[...]).astype(BF16)
            store(i, slot).start()

            @pl.when(pair < count // 2 - 1)
            def _():
                load(i + 2, slot).start()

        return carry

    lax.fori_loop(0, count // 2, body, 0)
    for slot in range(2):
        store(count - 2 + slot, slot).wait()
    fetch.pass_on([0, 1])
    rows_copy.start()
    fetch.pass_on_last([0, 1])
    fetch.finish()
    rows_copy.wait()


def head_start(rows, weight_qkv, weight_out, cotangent, head_weight):
    hbm, vmem = pl.BlockSpec(memory_space=pl.ANY), pl.BlockSpec(memory_space=pltpu.VMEM)
    sem, shape = pltpu.SemaphoreType.DMA, lambda a: jax.ShapeDtypeStruct(a.shape, a.dtype)
    count, columns = cotangent.shape
    width = head_weight.shape[0]
    tile = 256
    return pl.pallas_call(
        head_start_kernel,
        out_shape=[
            shape(rows),
            shape(weight_qkv),
            shape(weight_out),
            jax.ShapeDtypeStruct((count, width), BF16),
        ],
        in_specs=[hbm] * 4 + [vmem],
        out_specs=[hbm] * 4,
        scratch_shapes=[
            pltpu.VMEM((2, tile, columns), BF16),
            pltpu.VMEM((2, tile, width), BF16),
            sem((4, 2)),
            sem((4, 2)),
            sem,
            sem,
            sem((2,)),
            sem((2,)),
        ],
        compiler_params=pltpu.CompilerParams(
            collective_id=2, has_side_effects=True, vmem_limit_bytes=VMEM_LIMIT
        ),
        cost_estimate=pl.CostEstimate(
            flops=2 * count * columns * width,
            bytes_accessed=2 * count * columns,
            transcendentals=0,
        ),
    )(rows, weight_qkv, weight_out, cotangent, head_weight)


def attend_fetch_kernel(head_size, merge, steps, *refs):
    own, other, valid_ref, sources = refs[:3], refs[3:6], refs[6], refs[7:13]
    own_out, other_out, targets = refs[13], refs[14], refs[15:21]
    send, recv = refs[21:]
    fetch = Fetch(sources, targets, send, recv)

    @pl.when(pl.program_id(0) == 0)
    def _():
        fetch.greet()
        fetch.start([0])

    valid = valid_ref[...]
    attend_rows(head_size, merge, *own, own_out, valid)
    attend_rows(head_size, merge, *other, other_out, valid)

    @pl.when(pl.program_id(0) == steps - 1)
    def _():
        rest = list(range(2, 6))
        fetch.pass_on([0])
        fetch.start([1])
        fetch.pass_on([1])
        fetch.start(rest)
        fetch.pass_on_last([0, 1])
        fetch.pass_on(rest)
        fetch.pass_on_last(rest)
        fetch.finish()


def attend_fetch(own, other, counts, seq, head_size, weights):
    rows, width = own[0].shape
    images, merge = rows // seq, LANES // head_size
    block = pl.BlockSpec((seq, width), lambda i: (i, 0))
    hbm, sem = pl.BlockSpec(memory_space=pl.ANY), pltpu.SemaphoreType.DMA
    valid = valid_rows(counts, seq, merge)
    out = jax.ShapeDtypeStruct((rows, width), BF16)
    return pl.pallas_call(
        lambda *refs: attend_fetch_kernel(head_size, merge, images, *refs),
        grid=(images,),
        out_shape=[out, out] + [jax.ShapeDtypeStruct(w.shape, w.dtype) for w in weights],
        in_specs=[block] * 6
        + [pl.BlockSpec((None,) + valid.shape[1:], lambda i: (i, 0, 0))]
        + [hbm] * len(weights),
        out_specs=[block] * 2 + [hbm] * len(weights),
        scratch_shapes=[sem((4, len(weights)))] * 2,
        compiler_params=pltpu.CompilerParams(
            collective_id=3, has_side_effects=True, vmem_limit_bytes=VMEM_LIMIT
        ),
        cost_estimate=pl.CostEstimate(
            flops=8 * rows * seq * width * merge,
            bytes_accessed=16 * rows * width,
            transcendentals=2 * rows * seq * width // head_size,
        ),
    )(*own, *other, valid, *weights)


def whole_weight(weight, axis):
    return lax.all_gather(weight, "freq", axis=axis, tiled=True)


def core_sum(links, values, axis):
    keep, send = halves(values, links.core, axis)
    return keep + links.over_core(send)


def ring_kernel(shapes, crossing, pairs, *refs):
    count = len(shapes) - len(pairs)
    total = len(shapes)
    every = total + crossing

    def take(number):
        nonlocal refs
        head, refs = refs[:number], refs[number:]
        return head

    arrays, sums = take(every), take(count)
    mine, twins = take(every), take(every)
    held, crossed, first, done = take(total), take(crossing), take(crossing), take(total)
    arrived = take(len(pairs))
    out_send, out_recv, back_send, back_recv, side_send, side_recv, own_sem = take(7)
    x_send, x_recv, end_send, end_recv, load_sem, core_send, core_recv = take(7)
    index, across = lax.axis_index("dp"), lax.axis_index("freq")
    core, row, depth = index % 2, (index // 2) % 2, index // 4
    along = depth * (1 - row) + (7 - depth) * row
    rank = (along * (1 - core) + (8 - along) * core) % 8
    twin_rank = (8 - rank) % 8

    def device(spot):
        spot = spot % 8
        side = spot // 4
        return (spot * (1 - side) + (7 - spot) * side) * 4 + side * 2 + core

    way = 1 - 2 * core
    after, before = (device(along + way + 8), across), (device(along - way + 8), across)
    twin, facing = (index + 1 - 2 * core, across), (index, 1 - across)
    barrier = pltpu.get_barrier_semaphore()
    for partner in (after, before, twin, facing):
        pl.semaphore_signal(barrier, inc=1, device_id=partner, device_id_type=MESH)
    pl.semaphore_wait(barrier, 4)

    def copy(src, dst, send, recv, partner):
        return pltpu.make_async_remote_copy(
            src_ref=src,
            dst_ref=dst,
            send_sem=send,
            recv_sem=recv,
            device_id=partner,
            device_id_type=MESH,
        )

    def chunk(ref, half, place):
        if ref.shape[0] == 16:
            return ref.at[half * 8 + place]
        width = ref.shape[2] // 2
        return ref.at[place, :, pl.ds(pl.multiple_of(half * width, 128), width)]

    def load(i, step):
        place = (rank + 8 - step) % 8
        return pltpu.make_async_copy(
            chunk(arrays[i], core, place), mine[i].at[step], load_sem.at[step, i]
        )

    def coreward(i, step):
        place = (twin_rank + 8 - step) % 8
        return copy(
            chunk(arrays[i], 1 - core, place),
            twins[i].at[step % 4],
            core_send.at[step, i],
            core_recv.at[step, i],
            twin,
        )

    def core_sum(i, step, more):
        load(i, step).wait()
        coreward(i, step).wait_recv()
        value = mine[i][step] + twins[i][step % 4]
        mine[i][step] = value
        if more:
            coreward(i, step + 2).start()
        return value

    def facingward(i, step):
        return copy(
            mine[total + i].at[step],
            crossed[i].at[step % 4],
            x_send.at[step, i],
            x_recv.at[step, i],
            facing,
        )

    def cross(i, step, more):
        core_sum(total + i, step, more)
        facingward(i, step).start()

    def own(i, step, more, later):
        value = core_sum(i, step, more)
        if i >= crossing:
            return value
        facingward(i, step).wait_recv()
        value = value + crossed[i][step % 4]
        if more:
            mine[i][step] = value
            cross(i, step + 2, later)
        return value

    def outward(i, step, src):
        return copy(src, held[i].at[step], out_send.at[step, i], out_recv.at[step, i], after)

    def backward(i, step, place, src):
        return copy(
            src,
            chunk(sums[i], core, place),
            back_send.at[step, i],
            back_recv.at[step, i],
            after,
        )

    def sideward(i, step, place, src):
        return copy(
            src, chunk(sums[i], core, place), side_send.at[step, i], side_recv.at[step, i], twin
        )

    def keep(i, place):
        return pltpu.make_async_copy(done[i], chunk(sums[i], core, place), own_sem.at[i])

    def lastward(j):
        return copy(done[count + j], arrived[j], end_send.at[j], end_recv.at[j], facing)

    order = list(range(crossing, total)) + list(range(crossing))
    crossers = list(range(total, every))
    for step in range(8):
        for i in crossers + order:
            load(i, step).start()
            if step < 2:
                coreward(i, step).start()
    for step in range(2):
        for i in range(crossing):
            cross(i, step, True)
    for i in order:
        first_ref = mine[i].at[0] if i >= crossing else first[i]
        value = own(i, 0, True, True)
        if i < crossing:
            first[i][...] = value
        outward(i, 0, first_ref).start()

    def out_step(more, later):
        def body(step, carry):
            for i in order:
                outward(i, step, held[i].at[step]).wait_recv()
                held[i][step] = held[i][step] + own(i, step + 1, more, later)
                outward(i, step + 1, held[i].at[step]).start()
            return carry

        return body

    lax.fori_loop(0, 3, out_step(True, True), 0)
    lax.fori_loop(3, 5, out_step(True, False), 0)
    lax.fori_loop(5, 6, out_step(False, False), 0)
    place = (rank + 1) % 8
    for i in range(count, total):
        outward(i, 6, held[i].at[6]).wait_recv()
        done[i][...] = held[i][6] + own(i, 7, False, False)
        lastward(i - count).start()
    for i in order:
        if i >= count:
            continue
        outward(i, 6, held[i].at[6]).wait_recv()
        value = held[i][6] + own(i, 7, False, False)
        if i in pairs:
            lastward(pairs.index(i)).wait_recv()
            value = value + arrived[pairs.index(i)][...]
        done[i][...] = value
        backward(i, 0, place, done[i]).start()
        sideward(i, 0, place, done[i]).start()
        keep(i, place).start()

    def back_step(step, carry):
        place = (rank + 8 - step) % 8
        for i in range(count):
            ref = chunk(sums[i], core, place)
            backward(i, step, place, ref).wait_recv()
            backward(i, step + 1, place, ref).start()
            sideward(i, step + 1, place, ref).start()
        return carry

    lax.fori_loop(0, 6, back_step, 0)
    place = (rank + 2) % 8
    for i in range(count):
        ref = chunk(sums[i], core, place)
        backward(i, 6, place, ref).wait_recv()
        sideward(i, 7, place, ref).start()

    def end_step(step, carry):
        for i in range(total):
            outward(i, step, held[i].at[step]).wait_send()
        for i in range(count):
            backward(i, step, step, chunk(sums[i], core, step)).wait_send()
            sideward(i, step, step, chunk(sums[i], core, step)).wait_send()
            sideward(i, step, step, chunk(sums[i], core, step)).wait_recv()
        for i in range(crossing):
            facingward(i, step).wait_send()
        for i in range(every):
            coreward(i, step).wait_send()
        return carry

    lax.fori_loop(0, 7, end_step, 0)
    for i in range(count):
        sideward(i, 7, 7, chunk(sums[i], core, 7)).wait_send()
        sideward(i, 7, 7, chunk(sums[i], core, 7)).wait_recv()
        keep(i, 7).wait()
    for i in range(crossing):
        facingward(i, 7).wait_send()
    for i in range(every):
        coreward(i, 7).wait_send()
    for j in range(len(pairs)):
        lastward(j).wait_send()


def ring_sums(grads, cross, extra, columns):
    count, crossing, pairs = len(grads), len(cross), sorted(extra)
    total = count + len(pairs)
    arrays = []
    for i, grad in enumerate(list(grads) + [extra[i] for i in pairs] + list(cross)):
        pieces = 8 if i in columns else 16
        arrays.append(grad.reshape(pieces, grad.shape[0] // pieces, grad.shape[1]))
    shapes = [
        (a.shape[1], a.shape[2] // 2 if i in columns else a.shape[2])
        for i, a in enumerate(arrays)
    ]
    hbm, sem = pl.BlockSpec(memory_space=pl.ANY), pltpu.SemaphoreType.DMA
    slots = lambda number, of: [pltpu.VMEM((number,) + shape, BF16) for shape in of]
    one = lambda of: [pltpu.VMEM(shape, BF16) for shape in of]
    every = total + crossing
    scratch = slots(8, shapes) + slots(4, shapes) + slots(7, shapes[:total])
    scratch += slots(4, shapes[total:]) + one(shapes[total:]) + one(shapes[:total])
    scratch += one(shapes[count:total])
    scratch += [sem((7, total))] * 2 + [sem((7, count))] * 2 + [sem((8, count))] * 2 + [sem((count,))]
    scratch += [sem((8, crossing))] * 2 + [sem((len(pairs),))] * 2 + [sem((8, every))] * 3
    outs = pl.pallas_call(
        lambda *refs: ring_kernel(shapes[:total], crossing, pairs, *refs),
        out_shape=[jax.ShapeDtypeStruct(a.shape, BF16) for a in arrays[:count]],
        in_specs=[hbm] * every,
        out_specs=[hbm] * count,
        scratch_shapes=scratch,
        compiler_params=pltpu.CompilerParams(
            collective_id=1, has_side_effects=True, vmem_limit_bytes=RING_VMEM_LIMIT
        ),
        cost_estimate=pl.CostEstimate(
            flops=2 * sum(g.size for g in grads),
            bytes_accessed=6 * sum(g.size for g in grads),
            transcendentals=0,
        ),
    )(*arrays)
    return [o.reshape(g.shape) for o, g in zip(outs, grads)]


def unstack_qkv(total):
    depth = total.shape[0] // 3
    return jnp.stack([total[i * depth : (i + 1) * depth] for i in range(3)], axis=1)


def sum_small(links, values):
    if links.fast:
        values = values + links.over_x(values)
        for bit in (1, 2, 4, 8):
            values = values + links.over(bit, values)
        return values
    return lax.psum(values, ("dp", "freq"))


def own_images(links, values):
    count = values.shape[0] // links.shards
    return lax.dynamic_slice_in_dim(values, links.place * count, count, 0)


def reduce_rows(links, partial):
    if links.fast:
        keep, send = halves(partial, links.place, 0)
        return keep + links.over_x(send.astype(BF16)).astype(F32)
    return lax.psum_scatter(
        partial.astype(BF16), "freq", scatter_dimension=0, tiled=True
    ).astype(F32)


def gather_rows(links, values):
    if links.fast:
        return ordered(links.place, values, links.over_x(values), 0)
    return lax.all_gather(values, "freq", axis=0, tiled=True)


def block_forward(stream, gains, biases, attention, mlp, attend_all, head_size):
    normed = layer_norm(stream, gains[0], biases[0])
    middle = stream
    heads = []
    for weight_qkv, _ in attention:
        queries = (dot(normed, weight_qkv[0]) * head_size ** (-0.5)).astype(BF16)
        keys = dot(normed, weight_qkv[1]).astype(BF16)
        values = dot(normed, weight_qkv[2]).astype(BF16)
        heads.append((queries, keys, values))
    mixed = attend_all(heads)
    heads = [(*head, mix) for head, mix in zip(heads, mixed)]
    for (_, weight_out), mix in zip(attention, mixed):
        middle = middle + dot(mix, weight_out)
    normed_mid = layer_norm(middle, gains[1], biases[1])
    result = middle
    units = []
    for weight_up, weight_down in mlp():
        active, slope = up_projection(normed_mid, weight_up)
        result = result + dot(active, weight_down)
        units.append((active, slope))
    return result, (stream, normed, heads, middle, normed_mid, units)


def block_backward(
    grad, gains, attention, mlp, counts, seq, head_size, masked, saved
):
    stream, normed, heads, middle, normed_mid, units = saved
    low = grad.astype(BF16)
    down_grads, up_grads, grad_normed = [], [], 0.0
    for (weight_up, weight_down), (active, slope) in zip(mlp, units):
        grad_pre = (dot_nt(low, weight_down) * slope.astype(F32)).astype(BF16)
        grad_normed = grad_normed + dot_nt(grad_pre, weight_up)
        down_grads.append(dot_tn(active, low).astype(BF16))
        up_grads.append(dot_tn(normed_mid, grad_pre).astype(BF16))
    grad_in, mid_gain, mid_bias = layer_norm_back(grad_normed, middle, gains[1])
    grad = grad + grad_in
    low = grad.astype(BF16)
    out_grads, qkv_grads, grad_normed = [], [], 0.0
    for (weight_qkv, weight_out), (queries, keys, values, mixed) in zip(attention, heads):
        grad_mixed = dot_nt(low, weight_out).astype(BF16)
        grads = attend_back(queries, keys, values, grad_mixed, counts, seq, head_size, masked)
        for i in range(3):
            grad_normed = grad_normed + dot_nt(grads[i], weight_qkv[i])
        out_grads.append(dot_tn(mixed, low).astype(BF16))
        qkv_grads.append([dot_tn(normed, grads[i]).astype(BF16) for i in range(3)])
    grad_in, first_gain, first_bias = layer_norm_back(grad_normed, stream, gains[0])
    return (
        grad + grad_in,
        (first_gain, mid_gain),
        (first_bias, mid_bias),
        (qkv_grads, out_grads, up_grads, down_grads),
    )


def local(
    pixels,
    band_group,
    mask_order,
    visible_count,
    scale_id,
    patch_weight,
    enc_qkv,
    enc_out,
    enc_up,
    enc_down,
    enc_gains,
    enc_biases,
    dec_embed,
    mask_token,
    dec_qkv,
    dec_out,
    dec_up,
    dec_down,
    dec_gains,
    dec_biases,
    head_weight,
    recon_cotangent,
):
    links = Links()
    images, _, pixel_width = pixels.shape
    own = images // links.shards
    own_slots = own * VIS
    rgb_width = min(RGB_PIX, pixel_width)

    slot_ids = mask_order[:, :VIS]
    one_hot = slot_ids[:, :, None] == jnp.arange(NPATCH)[None, None, :]
    picked = jnp.einsum(
        "bsp,bpc->bsc", one_hot.astype(BF16), pixels, preferred_element_type=F32
    ).astype(BF16)
    multi = (band_group == 0)[:, None, None]
    zero = jnp.zeros((), BF16)
    rgb_valid = links.place * pixel_width + jnp.arange(rgb_width) < RGB_PIX
    picked_multi = jnp.where(multi, picked, zero).reshape(images * VIS, pixel_width)
    picked_rgb = jnp.where(~multi & rgb_valid, picked[:, :, :rgb_width], zero)
    picked_rgb = picked_rgb.reshape(images * VIS, rgb_width)
    patch_rgb = patch_weight[1, :rgb_width]
    partial = dot(picked_multi, patch_weight[0]) + dot(picked_rgb, patch_rgb)
    stacked = lambda weight: jnp.stack([weight[:, i] for i in range(3)])
    enc_attention = [(stacked(enc_qkv), enc_out)]
    enc_mlp = [(enc_up, enc_down)]
    dec_attention = [(stacked(dec_qkv), dec_out)]
    dec_mlp = [(dec_up, dec_down)]
    cotangent = recon_cotangent.reshape(images * NPATCH, -1)
    if links.fast:
        keep, send = halves(partial, links.place, 0)
        got, *others, grad_partial = head_start(
            send.astype(BF16), *enc_attention[0], cotangent, head_weight
        )
        embedded = keep + got.astype(F32)
        enc_attention.append(tuple(others))
        grad_final = None
        embedded, mask_order, scale_id = lax.optimization_barrier((embedded, mask_order, scale_id))
        slot_ids = mask_order[:, :VIS]
    else:
        embedded = reduce_rows(links, partial)
        grad_final = reduce_rows(links, dot_nt(cotangent, head_weight))
        enc_attention = [tuple(map(whole_weight, enc_attention[0], (2, 0)))]
        enc_mlp = [tuple(map(whole_weight, enc_mlp[0], (1, 0)))]
        dec_attention = [tuple(map(whole_weight, dec_attention[0], (2, 0)))]
        dec_mlp = [tuple(map(whole_weight, dec_mlp[0], (1, 0)))]

    my_slots = own_images(links, slot_ids)
    my_count = own_images(links, visible_count)
    ratios = jnp.exp2(own_images(links, scale_id).astype(F32) - 1.0)
    stream = embedded + slot_codes(my_slots, ratios, D).reshape(own_slots, D)

    def encoder_attention(heads):
        if not links.fast:
            return [attend(*head, my_count, VIS, HDIM, True) for head in heads]
        weights = (*enc_mlp[0], *dec_attention[0], *dec_mlp[0])
        nonlocal grad_final
        own_mix, other_mix, *others = attend_fetch(*heads, my_count, VIS, HDIM, weights)
        keep, send = halves(lax.optimization_barrier((grad_partial, own_mix))[0], links.place, 0)
        grad_final = keep.astype(F32) + links.over_x(send).astype(F32)
        enc_mlp.append(tuple(others[:2]))
        dec_attention.append(tuple(others[2:4]))
        dec_mlp.append(tuple(others[4:]))
        return own_mix, other_mix

    stream, enc_saved = block_forward(
        stream, enc_gains, enc_biases, enc_attention, lambda: enc_mlp, encoder_attention, HDIM
    )
    latent = layer_norm(stream, enc_gains[2], enc_biases[2])
    lifted = dot(latent, dec_embed)

    live = jnp.arange(VIS)[None, :] < my_count[:, None]
    select = (my_slots[:, :, None] == jnp.arange(NPATCH)[None, None, :]) & live[:, :, None]
    hidden = 1.0 - jnp.sum(select.astype(F32), axis=1)[:, :, None]
    decoded = (
        jnp.einsum(
            "bsp,bse->bpe",
            select.astype(F32),
            lifted.reshape(own, VIS, DDEC),
            precision=HIGHEST,
        )
        + hidden * mask_token
        + grid_codes(ratios, DDEC)
    ).reshape(own * NPATCH, DDEC)
    decoder_attention = lambda heads: [
        attend(*head, my_count, NPATCH, DHDIM, False) for head in heads
    ]
    decoded, dec_saved = block_forward(
        decoded, dec_gains, dec_biases, dec_attention, lambda: dec_mlp, decoder_attention, DHDIM
    )
    final_own = layer_norm(decoded, dec_gains[2], dec_biases[2])

    final_all = gather_rows(links, final_own)
    reconstructions = dot(final_all, head_weight).astype(BF16).reshape(images, NPATCH, -1)
    head_grad = dot_tn(final_all, cotangent).astype(BF16)

    grad_in, dec_gain_2, dec_bias_2 = layer_norm_back(grad_final, decoded, dec_gains[2])
    grad_decoded, dec_gain_01, dec_bias_01, dec_grads = block_backward(
        grad_in, dec_gains, dec_attention, dec_mlp, my_count, NPATCH, DHDIM, False, dec_saved
    )
    grad_grid = grad_decoded.reshape(own, NPATCH, DDEC)
    mask_grad = jnp.sum(hidden * grad_grid, axis=(0, 1))
    grad_lifted = (
        jnp.einsum(
            "bsp,bpe->bse",
            select.astype(BF16),
            grad_grid.astype(BF16),
            preferred_element_type=F32,
        )
        .astype(BF16)
        .reshape(own_slots, DDEC)
    )
    embed_grad = dot_tn(latent, grad_lifted).astype(BF16)
    grad_latent = dot_nt(grad_lifted, dec_embed)

    grad_in, enc_gain_2, enc_bias_2 = layer_norm_back(grad_latent, stream, enc_gains[2])
    grad_stream, enc_gain_01, enc_bias_01, enc_grads = block_backward(
        grad_in, enc_gains, enc_attention, enc_mlp, my_count, VIS, HDIM, True, enc_saved
    )

    grad_embedded = gather_rows(links, grad_stream.astype(BF16))
    patch_grads = [
        dot_tn(picked_multi, grad_embedded).astype(BF16),
        dot_tn(picked_rgb, grad_embedded).astype(BF16),
    ]
    multi_rows = jnp.repeat(band_group == 0, VIS)[:, None]
    back_multi = dot_nt(jnp.where(multi_rows, grad_embedded, zero), patch_weight[0])
    back_rgb = dot_nt(jnp.where(multi_rows, zero, grad_embedded), patch_rgb)
    back_rgb = jnp.where(rgb_valid, back_rgb, 0.0)
    back = back_multi + jnp.pad(back_rgb, ((0, 0), (0, pixel_width - rgb_width)))
    pixel_grad = jnp.einsum(
        "bsp,bsc->bpc",
        one_hot.astype(BF16),
        back.astype(BF16).reshape(images, VIS, pixel_width),
        preferred_element_type=F32,
    )

    dec_qkv_grads, dec_out_grads, dec_up_grads, dec_down_grads = dec_grads
    enc_qkv_grads, enc_out_grads, enc_up_grads, enc_down_grads = enc_grads
    stacked_qkv = lambda grads: [jnp.concatenate(g, 0) for g in grads]
    enc_stack = [
        (stacked_qkv(enc_qkv_grads), 1),
        (enc_out_grads, 0),
        (enc_up_grads, 1),
        (enc_down_grads, 0),
    ]
    dec_stack = [
        (stacked_qkv(dec_qkv_grads), 1),
        (dec_out_grads, 0),
        (dec_up_grads, 1),
        (dec_down_grads, 0),
    ]
    patch_grad = jnp.concatenate(patch_grads, 0)
    if links.fast:
        stacks = [grads for grads, _ in enc_stack[:3] + dec_stack]
        enc_last = enc_stack[3][0]
        late = [grads[0] for grads in stacks] + [embed_grad, enc_last[0], head_grad, patch_grad]
        late = ring_sums(
            late, [grads[1] for grads in stacks] + [embed_grad], {8: enc_last[1]}, {10}
        )
        late = [total.astype(F32) for total in late]
        enc_totals = [unstack_qkv(late[0]), late[1], late[2], late[8]]
        dec_totals = [unstack_qkv(late[3])] + late[4:7]
        embed_total, head_total = late[7], late[9]
        patch_total = jnp.pad(late[10], ((0, pixel_width - rgb_width), (0, 0)))
        patch_total = patch_total.reshape(2, pixel_width, D)
    else:
        reduced = []
        for stack in (dec_stack, enc_stack):
            parts = [
                lax.psum_scatter(g[0], "freq", scatter_dimension=axis, tiled=True)
                for g, axis in stack
            ]
            parts = [lax.psum(part, "dp").astype(F32) for part in parts]
            parts[0] = unstack_qkv(parts[0])
            reduced.append(parts)
        dec_totals, enc_totals = reduced
        embed_total = lax.psum(embed_grad, ("dp", "freq")).astype(F32)
        head_total = lax.psum(head_grad, "dp").astype(F32)
        patch_sum = lax.psum(patch_grad, "dp").astype(F32)
        patch_total = jnp.stack(
            [
                patch_sum[:pixel_width],
                jnp.pad(patch_sum[pixel_width:], ((0, pixel_width - rgb_width), (0, 0))),
            ]
        )
    small = [*enc_gain_01, enc_gain_2, *enc_bias_01, enc_bias_2]
    small += [*dec_gain_01, dec_gain_2, *dec_bias_01, dec_bias_2, mask_grad]
    small = sum_small(links, jnp.concatenate(small).reshape(-1, LANES)).reshape(-1)
    enc_end, dec_end = 6 * D, 6 * D + 6 * DDEC
    enc_small = small[:enc_end].reshape(2, 3, D)
    dec_small = small[enc_end:dec_end].reshape(2, 3, DDEC)
    return (
        reconstructions,
        pixel_grad,
        patch_total,
        *enc_totals,
        enc_small[0],
        enc_small[1],
        embed_total,
        small[dec_end:],
        *dec_totals,
        dec_small[0],
        dec_small[1],
        head_total,
    )


def solution(mesh):
    return jax.shard_map(
        local,
        mesh=mesh,
        in_specs=(
            P("dp", None, "freq"),
            P("dp"),
            P("dp", None),
            P("dp"),
            P("dp"),
            P(None, "freq", None),
            P(None, None, "freq"),
            P("freq", None),
            P(None, "freq"),
            P("freq", None),
            P(),
            P(),
            P(),
            P(),
            P(None, None, "freq"),
            P("freq", None),
            P(None, "freq"),
            P("freq", None),
            P(),
            P(),
            P(None, "freq"),
            P("dp", None, "freq"),
        ),
        out_specs=(
            P("dp", None, "freq"),
            P("dp", None, "freq"),
            P(None, "freq", None),
            P(None, None, "freq"),
            P("freq", None),
            P(None, "freq"),
            P("freq", None),
            P(),
            P(),
            P(),
            P(),
            P(None, None, "freq"),
            P("freq", None),
            P(None, "freq"),
            P("freq", None),
            P(),
            P(),
            P(None, "freq"),
        ),
        check_vma=False,
    )
```

time: 1130 us -> 972 us (0.86)
  waiting for transfers between devices: 146 us -> 43.9 us
  Pallas kernels: 471 us -> 532 us
  local copies, waits for them, and re-layouts: 78.2 us -> 42.1 us
  matrix products: 287 us -> 256 us
  starting transfers between devices: 40.8 us -> 9.84 us
  other arithmetic: 96.8 us -> 78.5 us
    ppermute x22 -> x4, waiting for transfers between devices: 113 us -> 40 us  [over_x(): return lax.ppermute(values, 'freq', [(0, 1), (1, 0)])]
    pallas_call x19 -> x9, Pallas kernels: 444 us -> 503 us  [the longest x1 279 us: ring_sums(): pl.pallas_call(lambda *refs: ring_kernel(shapes[:total], crossing, pairs,...]
    add x20 -> x1, other arithmetic: 36.7 us -> 1.78 us  [local(): embedded = keep + got.astype(F32)]
    dot_general x28 -> x27, matrix products: 102 us -> 67.5 us  [dot_nt(): lax.dot_general(left, right, (((1,), (1,)), ((), ())), preferred_element_...]
    ppermute x39 -> x4, waiting for transfers between devices: 33.1 us -> 3.89 us  [over(): return lax.ppermute(values, 'dp', [(i, i ^ bit) for i in range(16)])]
    convert_element_type x2 -> x10, other arithmetic: 4.46 us -> 25.8 us  [local(): late = [total.astype(F32) for total in late]]
    ppermute x22 -> x4, starting transfers between devices: 20.9 us -> 4.27 us  [over_x(): return lax.ppermute(values, 'freq', [(0, 1), (1, 0)])]
    ppermute x39 -> x4, starting transfers between devices: 19.9 us -> 5.56 us  [over(): return lax.ppermute(values, 'dp', [(i, i ^ bit) for i in range(16)])]
  transfers between devices with their start and end apart: 61 -> 8, of which waited for: 16 -> 5; matrix products, arithmetic and copies ran while one was open for 25% -> 10% of each run, Pallas kernels for 18% -> 5%
where the time goes in v2:
time: 972 us; the launch traced here: 965 us
  Pallas kernels  532 us (55%)
  matrix products  256 us (26%)
  other arithmetic  78.5 us (8%)
  waiting for transfers between devices  43.9 us (5%)
  local copies, waits for them, and re-layouts  42.1 us (4%)
  starting transfers between devices  9.84 us (1%)
    pallas_call x1, Pallas kernels, ring_sums(): pl.pallas_call(lambda *refs: ring_kernel(shapes[:total], crossing, pairs,...  279 us
    dot_general x28, matrix products, dot_tn(): lax.dot_general(left, right, (((0,), (0,)), ((), ())), preferred_element_...  93.2 us
    pallas_call x1, Pallas kernels, attend_fetch(): pl.pallas_call(lambda *refs: attend_fetch_kernel(head_size, merge, images...  91.9 us
    pallas_call x6, Pallas kernels, attention_call(): pl.pallas_call(kernel, grid=(images,), in_specs=in_specs, out_specs=[bloc...  79.7 us
    dot_general x24, matrix products, dot(): return jnp.dot(left, right, preferred_element_type=F32)  71.1 us
    dot_general x27, matrix products, dot_nt(): lax.dot_general(left, right, (((1,), (1,)), ((), ())), preferred_element_...  67.5 us
    pallas_call x1, Pallas kernels, head_start(): pl.pallas_call(head_start_kernel, out_shape=[shape(rows), shape(weight_qk...  52.8 us
    ppermute x4, waiting for transfers between devices, over_x(): return lax.ppermute(values, 'freq', [(0, 1), (1, 0)])  40 us
  transfers between devices with their start and end apart: 8, of which 5 were waited for; matrix products, arithmetic and copies ran while one was open for 10% of the time, Pallas kernels for 5%

profile of v2, /device:TPU:0, one launch (start us, length us, event | category | flops | bytes accessed | tf_op | source)
XLA Modules:
  0.0 965.2 jit_solution(10236785520142817433)
XLA Ops:
  3.9 3.4 slice_bitcast_fusion.5
  7.3 7.2 broadcast_select_fusion
  14.7 5.1 fusion.24
  19.9 4.0 fusion.17
  26.1 52.8 %shard_map.349 = (bf16[512,1024]{1,0:T(8,128)(2,1)S(1)}, bf16[3,1024,512]{2,1,0:T(8,128)(2,1)}, bf16[512,1024]{1,0:T(8,128)(2,1)S(1)}, bf16[4096,512]{1,0:T(8,128)(2,1)}) custom-call(bf16[512,1024]{1,0:T(8,128)(2,1)S(1)} %dynamic-slice_convert_fusion.rows_ref, bf16[3,1024,512]{2,1,0:T(8,128)(2,1)} %pad_maximum_fusion.3.qkv_ref, ...), custom_call_target="tpu_custom_call" | custom-call | flops 13958643712 | bytes 27262976 | tf_op jit(solution)/shard_map/pallas_call | solution.py:413
  96.0 91.9 %shard_map.350 = (bf16[512,512]{1,0:T(8,128)(2,1)S(1)}, bf16[512,512]{1,0:T(8,128)(2,1)S(1)}, bf16[1024,2048]{1,0:T(8,128)(2,1)}, bf16[2048,1024]{1,0:T(8,128)(2...) custom-call(bf16[512,512]{1,0:T(8,128)(2,1)S(1)} %fusion.28.refs_0_,, ...), custom_call_target="tpu_custom_call" | custom-call | flops 268435456 | bytes 4194304 | tf_op jit(solution)/shard_map/pallas_call | solution.py:479
  191.1 3.1 constant_dynamic-slice_fusion
  199.7 6.6 shard_map.351
  207.7 6.6 shard_map.352
  218.0 2.5 fusion.129
  223.3 3.2 fusion.130
  243.6 9.7 %shard_map.353 = bf16[2048,256]{1,0:T(8,128)(2,1)S(1)} custom-call(bf16[2048,256]{1,0:T(8,128)(2,1)S(1)} %copy-done.46, bf16[2048,256]{1,0:T(8,128)(2,1)S(1)} %copy-done.42, bf16[2048,256]{1,0:T(8,128)(2,1)S(1)} %copy-done.41), custom_call_target="tpu_custom_call" | custom-call | flops 2147483648 | bytes 4194304 | tf_op jit(solution)/shard_map/pallas_call | solution.py:182
  253.3 2.7 fusion.136
  256.0 9.7 %shard_map.354 = bf16[2048,256]{1,0:T(8,128)(2,1)S(1)} custom-call(bf16[2048,256]{1,0:T(8,128)(2,1)S(1)} %copy-done.44, bf16[2048,256]{1,0:T(8,128)(2,1)S(1)} %copy-done.39, bf16[2048,256]{1,0:T(8,128)(2,1)S(1)} %copy-done.38), custom_call_target="tpu_custom_call" | custom-call | flops 2147483648 | bytes 4194304 | tf_op jit(solution)/shard_map/pallas_call | solution.py:182
  265.8 3.3 fusion.131
  271.8 7.8 shard_map.355
  279.6 8.0 shard_map.356
  287.6 5.0 fusion.137
  293.0 2.8 fusion.132
  298.0 4.6 multiply_reduce_fusion.1
  302.5 5.2 fusion.120
  307.7 3.4 convolution_convert_fusion.24
  311.2 3.4 convolution_convert_fusion.26
  314.5 2.4 multiply_convert_fusion.1
  317.0 3.3 convolution_convert_fusion.27
  322.7 2.4 multiply_convert_fusion
  325.2 3.5 convolution_convert_fusion.25
  328.7 4.3 multiply_reduce_fusion.2
  333.0 3.4 fusion.119
  342.7 20.6 %shard_map.357 = (bf16[2048,256]{1,0:T(8,128)(2,1)S(1)}, bf16[2048,256]{1,0:T(8,128)(2,1)S(1)}, bf16[2048,256]{1,0:T(8,128)(2,1)S(1)}) custom-call(bf16[2048,256]{1,0:T(8,128)(2,1)S(1)} %copy-done.47, bf16[2048,256]{1,0:T(8,128)(2,1)S(1)} %copy-done.43, bf16[2048,256]{1,0:T(8,128)(2,1)} %convolution_convert_fusion.12.refs_2_, ...), custom_call_target="tpu_custom_call" | custom-call | flops 5368709120 | bytes 7340032 | tf_op jit(solution)/shard_map/pallas_call | solution.py:182
  363.3 20.8 %shard_map.358 = (bf16[2048,256]{1,0:T(8,128)(2,1)S(1)}, bf16[2048,256]{1,0:T(8,128)(2,1)S(1)}, bf16[2048,256]{1,0:T(8,128)(2,1)S(1)}) custom-call(bf16[2048,256]{1,0:T(8,128)(2,1)S(1)} %copy-done.45, bf16[2048,256]{1,0:T(8,128)(2,1)S(1)} %copy-done.40, bf16[2048,256]{1,0:T(8,128)(2,1)} %convolution_convert_fusion.10.refs_2_, ...), custom_call_target="tpu_custom_call" | custom-call | flops 5368709120 | bytes 7340032 | tf_op jit(solution)/shard_map/pallas_call | solution.py:182
  384.8 2.8 fusion.78
  387.6 2.7 fusion.75
  390.3 2.8 fusion.72
  393.1 2.8 fusion.69
  396.5 8.6 multiply_reduce_fusion.3
  414.0 2.9 multiply_reduce_fusion
  424.7 2.4 multiply_convert_fusion.3
  430.8 3.0 multiply_reduce_fusion.13
  437.0 9.5 shard_map.360
  453.9 9.5 shard_map.359
  468.3 4.4 convolution_convert_fusion.2
  472.7 4.4 convolution_convert_fusion.6
  477.2 4.4 convolution_convert_fusion.3
  481.6 4.8 convolution_convert_fusion.5
  488.1 3.0 multiply_reduce_fusion.14
  499.8 36.2 %collective-permute-done.3 = f32[76,128]{1,0:T(8,128)S(1)} collective-permute-done((f32[76,128]{1,0:T(8,128)S(1)}, f32[76,128]{1,0:T(8,128)S(1)}, u32[]{:S(2)}, u32[]{:S(2)}) %collective-permute-start.3) | collective-permute-done | bytes 38944 | tf_op jit(solution)/shard_map/ppermute | solution.py:262
  545.9 2.7 collective-permute-start.7
  553.9 3.8 collective-permute-done.2
  557.7 6.4 convolution_convert_fusion.4
  564.1 3.6 convolution_convert_fusion.14
  567.8 4.1 fusion.20
  571.8 2.8 pad_maximum_fusion.1
  574.7 5.9 add_convert_fusion
  580.6 11.7 %fusion.49 = f32[16,256,1664]{2,1,0:T(8,128)} fusion(bf16[16,64,1664]{2,1,0:T(8,128)(2,1)S(1)} %bitcast.343, s32[16,64]{1,0:T(8,128)S(1)} %copy-done.110), kind=kOutput, calls=%fused_computation.177 | convolution fusion | flops 872677376 | bytes 30674944 | tf_op jit(solution)/shard_map/bsp,bsc->bpc/dot_general | solution.py:997
  592.2 28.5 %convolution_convert_fusion.1 = bf16[512,3328]{1,0:T(8,128)(2,1)} fusion(bf16[4096,3328]{1,0:T(8,128)(2,1)} %bitcast.405, bf16[2048,512]{1,0:T(8,128)(2,1)} %collective-permute-done, bf16[2048,512]{1,0:T(8,128)(2,1)} %get-tuple-element.154, pred[]{:T(512)S(6)} %eq.30), kind=kOutput, calls=%fused_computation.5 | convolution fusion | flops 13979222016 | bytes 34865152 | tf_op jit(solution)/shard_map/dot_general | solution.py:35
  620.8 278.7 %shard_map.361 = (bf16[16,192,512]{2,1,0:T(8,128)(2,1)}, bf16[16,32,1024]{2,1,0:T(8,128)(2,1)}, bf16[16,64,2048]{2,1,0:T(8,128)(2,1)}, bf16[16,96,256]{2,1,0:T(8...) custom-call(bf16[16,192,512]{2,1,0:T(8,128)(2,1)} %bitcast.339, ...), custom_call_target="tpu_custom_call" | custom-call | flops 25165824 | bytes 75497472 | tf_op jit(solution)/shard_map/pallas_call | solution.py:741
  911.2 3.2 pad.10
  914.4 6.8 convert.16
  921.2 5.5 bitcast_convert_fusion.2
  926.6 4.7 bitcast_convert_fusion.1
  931.4 4.7 bitcast_convert_fusion
  937.3 3.5 pad_maximum_fusion
  940.9 23.9 %convolution_convert_fusion = bf16[4096,3328]{1,0:T(8,128)(2,1)} fusion(bf16[512,3328]{1,0:T(8,128)(2,1)} %head_ref.1, bf16[2048,512]{1,0:T(8,128)(2,1)} %collective-permute-done, bf16[2048,512]{1,0:T(8,128)(2,1)} %get-tuple-element.154, pred[]{:T(512)S(6)} %eq.30), kind=kOutput, calls=%fused_computation | convolution fusion | flops 13991149568 | bytes 34865152 | tf_op jit(solution)/shard_map/dot_general | solution.py:31
  (485 shorter events, 144.7 us)
Async XLA Ops:
  0.7 221.7 %copy-start = (bf16[1024,512]{1,0:T(8,128)(2,1)S(1)}, bf16[1024,512]{1,0:T(8,128)(2,1)}, u32[]{:S(2)}) copy-start(bf16[1024,512]{1,0:T(8,128)(2,1)} %param.34) | copy-start | bytes 3145732
  0.7 6.5 copy-start.130
  2.2 5.2 copy-start.109
  3.0 81.8 %copy-start.111 = (f32[1,1024]{1,0:T(1,128)}, f32[1,1024]{1,0:T(1,128)S(1)}, u32[]{:S(2)}) copy-start(f32[1,1024]{1,0:T(1,128)S(1)} %get-tuple-element.169) | copy-start | bytes 12292
  3.0 196.3 %copy-start.115 = (f32[1,1024]{1,0:T(1,128)}, f32[1,1024]{1,0:T(1,128)S(1)}, u32[]{:S(2)}) copy-start(f32[1,1024]{1,0:T(1,128)S(1)} %get-tuple-element.170) | copy-start | bytes 12292
  14.5 5.3 copy-start.73
  14.5 5.3 slice-start.1
  14.7 5.1 copy-start.86
  14.7 5.1 slice-start.2
  19.9 4.2 copy-start.80
  19.9 4.2 copy-start.81
  85.2 7.4 copy-start.93
  93.6 94.3 %copy-start.117 = (f32[8,64]{1,0:T(8,128)}, f32[8,64]{1,0:T(8,128)S(1)}, u32[]{:S(2)}) copy-start(f32[8,64]{1,0:T(8,128)S(1)} %get-tuple-element.191) | copy-start | bytes 6148
  191.1 4.4 copy-start.16
  191.1 6.3 copy-start.127
  191.1 6.3 copy-start.128
  194.2 102.4 %collective-permute-start.1 = (bf16[2048,512]{1,0:T(8,128)(2,1)}, bf16[2048,512]{1,0:T(8,128)(2,1)}, u32[]{:S(2)}, u32[]{:S(2)}) collective-permute-start(bf16[2048,512]{1,0:T(8,128)(2,1)} %constant_dynamic-slice_fusion), channel_id=1, source_target_pairs={{0,1},{1,0},{2,3},{3,2},{4,5},{5,4},{6,7},{7,6},{8,9},{9,8},{10,11... | collective-permute-start | bytes 6291464 | tf_op jit(solution)/shard_map/ppermute | solution.py:262
  198.9 17.8 %copy-start.64 = (f32[512,1024]{1,0:T(8,128)}, f32[512,1024]{1,0:T(8,128)S(1)}, u32[]{:S(2)}) copy-start(f32[512,1024]{1,0:T(8,128)S(1)} %get-tuple-element.197) | copy-start | bytes 6291460
  198.9 7.4 copy-start.119
  199.3 7.0 copy-start.123
  199.7 7.9 copy-start.23
  207.7 6.6 copy-start.48
  207.7 6.6 copy-start.75
  256.0 9.7 %copy-start.26 = (bf16[256,512]{1,0:T(8,128)(2,1)S(1)}, bf16[256,512]{1,0:T(8,128)(2,1)}, u32[]{:S(2)}) copy-start(bf16[256,512]{1,0:T(8,128)(2,1)} %copy-done.25) | copy-start | bytes 786436
  256.0 9.7 %copy-start.57 = (f32[8,256,512]{2,1,0:T(8,128)S(1)}, f32[8,256,512]{2,1,0:T(8,128)}, u32[]{:S(2)}) copy-start(f32[8,256,512]{2,1,0:T(8,128)} %copy-done.56) | copy-start | bytes 12582916
  271.8 7.8 copy-start.11
  271.8 7.8 copy-start.36
  287.6 5.0 copy-start.63
  287.6 5.0 copy-start.136
  287.6 5.3 copy-start.139
  342.6 20.6 %copy-start.40 = (bf16[2048,256]{1,0:T(8,128)(2,1)S(1)}, bf16[2048,256]{1,0:T(8,128)(2,1)}, u32[]{:S(2)}) copy-start(bf16[2048,256]{1,0:T(8,128)(2,1)} %convolution_convert_fusion.11.refs_1_) | copy-start | bytes 3145732
  342.6 20.6 %copy-start.45 = (bf16[2048,256]{1,0:T(8,128)(2,1)S(1)}, bf16[2048,256]{1,0:T(8,128)(2,1)}, u32[]{:S(2)}) copy-start(bf16[2048,256]{1,0:T(8,128)(2,1)} %fusion.11.refs_0_) | copy-start | bytes 3145732
  363.3 20.8 %copy-start.83 = (bf16[512,3,256]{2,0,1:T(8,128)(2,1)S(1)}, bf16[512,3,256]{2,0,1:T(8,128)(2,1)}, u32[]{:S(2)}) copy-start(bf16[512,3,256]{2,0,1:T(8,128)(2,1)} %param.36) | copy-start | bytes 2359300
  409.6 4.4 copy-start.69
  419.4 4.9 copy-start.99
  424.3 5.3 copy-start.143
  436.0 10.6 %copy-start.94 = (bf16[512,1024]{1,0:T(8,128)(2,1)S(1)}, bf16[512,1024]{1,0:T(8,128)(2,1)}, u32[]{:S(2)}) copy-start(bf16[512,1024]{1,0:T(8,128)(2,1)} %copy-done.93) | copy-start | bytes 3145732
  453.9 10.2 %copy-start.71 = (bf16[1024,3,512]{2,0,1:T(8,128)(2,1)S(1)}, bf16[1024,3,512]{2,0,1:T(8,128)(2,1)}, u32[]{:S(2)}) copy-start(bf16[1024,3,512]{2,0,1:T(8,128)(2,1)} %param.28) | copy-start | bytes 9437188
  468.3 4.4 copy-start.146
  472.7 4.4 copy-start.51
  472.7 4.4 copy-start.100
  477.1 4.4 copy-start.49
  486.4 105.9 %collective-permute-start = (bf16[2048,512]{1,0:T(8,128)(2,1)}, bf16[2048,512]{1,0:T(8,128)(2,1)}, u32[]{:S(2)}, u32[]{:S(2)}) collective-permute-start(bf16[2048,512]{1,0:T(8,128)(2,1)} %get-tuple-element.154), channel_id=1, source_target_pairs={{0,1},{1,0},{2,3},{3,2},{4,5},{5,4},{6,7},{7,6},{8,9},{9,8},{10,11... | collective-permute-start | bytes 6291464 | tf_op jit(solution)/shard_map/ppermute | solution.py:262
  491.3 44.7 %collective-permute-start.3 = (f32[76,128]{1,0:T(8,128)S(1)}, f32[76,128]{1,0:T(8,128)S(1)}, u32[]{:S(2)}, u32[]{:S(2)}) collective-permute-start(f32[76,128]{1,0:T(8,128)S(1)} %bitcast.374), channel_id=1, source_target_pairs={{0,1},{1,0},{2,3},{3,2},{4,5},{5,4},{6,7},{7,6},{8,9},{9,8},{10,11... | collective-permute-start | bytes 116744 | tf_op jit(solution)/shard_map/ppermute | solution.py:262
  493.3 64.4 %collective-permute-start.2 = (bf16[512,1024]{1,0:T(8,128)(2,1)S(1)}, bf16[512,1024]{1,0:T(8,128)(2,1)}, u32[]{:S(2)}, u32[]{:S(2)}) collective-permute-start(bf16[512,1024]{1,0:T(8,128)(2,1)S(1)} %add_convert_fusion.5), channel_id=1, source_target_pairs={{0,1},{1,0},{2,3},{3,2},{4,5},{5,4},{6,7},{7,6},{8,9},{9,8},{10,11... | collective-permute-start | bytes 3145736 | tf_op jit(solution)/shard_map/ppermute | solution.py:262
  498.1 38.0 %copy-start.35 = (bf16[512,512]{1,0:T(8,128)(2,1)S(1)}, bf16[512,512]{1,0:T(8,128)(2,1)}, u32[]{:S(2)}) copy-start(bf16[512,512]{1,0:T(8,128)(2,1)} %copy-done.33) | copy-start | bytes 1572868
  498.1 40.9 %copy-start.32 = (bf16[512,512]{1,0:T(8,128)(2,1)S(1)}, bf16[512,512]{1,0:T(8,128)(2,1)}, u32[]{:S(2)}) copy-start(bf16[512,512]{1,0:T(8,128)(2,1)} %copy-done.31) | copy-start | bytes 1572868
  536.0 7.6 copy-start.104
  536.0 7.6 copy-start.105
  536.0 7.6 copy-start.106
  536.0 1.8 collective-permute-start.4
  537.8 10.8 %copy-start.101 = (bf16[512,256]{1,0:T(8,128)(2,1)S(1)}, bf16[512,256]{1,0:T(8,128)(2,1)}, u32[]{:S(2)}) copy-start(bf16[512,256]{1,0:T(8,128)(2,1)} %convolution_convert_fusion.36) | copy-start | bytes 786436
  537.8 10.8 %copy-start.102 = (bf16[512,256]{1,0:T(8,128)(2,1)S(1)}, bf16[512,256]{1,0:T(8,128)(2,1)}, u32[]{:S(2)}) copy-start(bf16[512,256]{1,0:T(8,128)(2,1)} %convolution_convert_fusion.37) | copy-start | bytes 786436
  537.8 10.8 %copy-start.103 = (bf16[512,256]{1,0:T(8,128)(2,1)S(1)}, bf16[512,256]{1,0:T(8,128)(2,1)}, u32[]{:S(2)}) copy-start(bf16[512,256]{1,0:T(8,128)(2,1)} %convolution_convert_fusion.38) | copy-start | bytes 786436
  537.9 4.1 collective-permute-start.5
  541.9 4.0 collective-permute-start.6
  545.9 4.9 collective-permute-start.7
  553.9 10.2 %copy-start.87 = (bf16[16,64,768]{2,1,0:T(8,128)(2,1)S(1)}, bf16[16,64,768]{2,1,0:T(8,128)(2,1)}, u32[]{:S(2)}) copy-start(bf16[16,64,768]{2,1,0:T(8,128)(2,1)} %copy-done.86) | copy-start | bytes 4718596
  564.1 10.5 %slice-start.3 = ((s8[6815744]{0:T(1024)(128)(4,1)}), s8[4194304]{0:T(1024)(128)(4,1)S(1)}, s32[]{:S(2)}) async-start(s8[6815744]{0:T(1024)(128)(4,1)} %bitcast.408), calls=%async_computation.3 | async-start | bytes 8388608
  567.7 6.9 slice-start.4
  574.7 5.9 copy-start.110
  921.2 5.5 copy-start.79
  926.6 4.8 copy-start.78
  940.9 23.9 %copy-start.1 = (bf16[1024,512]{1,0:T(8,128)(2,1)S(1)}, bf16[1024,512]{1,0:T(8,128)(2,1)}, u32[]{:S(2)}) copy-start(bf16[1024,512]{1,0:T(8,128)(2,1)} %param.34) | copy-start | bytes 3145732
  (96 other events, 234.3 us)

commit v3 on v2

--- a/solution.py
+++ b/solution.py
@@ -22,8 +22,8 @@
 BF16 = jnp.bfloat16
 F32 = jnp.float32
 LANES = 128
-VMEM_LIMIT = 48 * 1024 * 1024
-RING_VMEM_LIMIT = 58 * 1024 * 1024
+MIB = 1024 * 1024
+RING_VMEM_LIMIT = 58 * MIB
 MESH = pl.DeviceIdType.MESH
 
 
@@ -104,7 +104,7 @@
     return scores
 
 
-def attend_rows(head_size, merge, q_ref, k_ref, v_ref, o_ref, valid):
+def attend_rows(head_size, merge, q_ref, k_ref, v_ref, o_ref, p_ref, valid):
     seq, width = q_ref.shape
     for g in range(width // LANES):
         lanes = slice(g * LANES, (g + 1) * LANES)
@@ -117,15 +117,15 @@
             )
             top = jnp.max(scores, 0, keepdims=True)
             power = jnp.exp(scores - top)
-            total = jnp.sum(power, 0, keepdims=True)
+            weights = (power * (1.0 / jnp.sum(power, 0, keepdims=True))).astype(BF16)
+            p_ref[(g * LANES // head_size + h) // merge] = weights
             rows = slice(h * head_size, (h + merge) * head_size)
-            mixed = dot(values_t[rows], power.astype(BF16)) * (1.0 / total)
-            parts += head_parts(mixed, head_size, seq, merge)
+            parts += head_parts(dot(values_t[rows], weights), head_size, seq, merge)
         o_ref[:, lanes] = jnp.transpose(jnp.concatenate(parts, 0)).astype(BF16)
 
 
 def attend_back_rows(
-    head_size, merge, q_ref, k_ref, v_ref, g_ref, dq_ref, dk_ref, dv_ref, valid
+    head_size, merge, q_ref, k_ref, v_ref, p_ref, g_ref, dq_ref, dk_ref, dv_ref
 ):
     seq, width = q_ref.shape
     factor = head_size ** (-0.5)
@@ -142,14 +142,12 @@
         for h in range(0, LANES // head_size, merge):
             own_q = head_rows(queries, head_size, range(h, h + merge))
             own_g = head_rows(grads, head_size, range(h, h + merge))
-            scores = masked_scores(keys, own_q, valid)
-            top = jnp.max(scores, 0, keepdims=True)
-            power = jnp.exp(scores - top)
-            weights = power * (1.0 / jnp.sum(power, 0, keepdims=True))
-            dv_sum += dot(weights.astype(BF16), own_g)
+            weights = p_ref[(g * LANES // head_size + h) // merge]
+            dv_sum += dot(weights, own_g)
             grad_weights = dot_nt(values, own_g)
-            along = jnp.sum(weights * grad_weights, 0, keepdims=True)
-            grad_scores = (weights * (grad_weights - along)).astype(BF16)
+            product = weights.astype(F32) * grad_weights
+            along = jnp.sum(product, 0, keepdims=True)
+            grad_scores = (product - weights.astype(F32) * along).astype(BF16)
             dk_sum += dot(grad_scores, own_q)
             rows = slice(h * head_size, (h + merge) * head_size)
             grad_q = dot(keys_t[rows], grad_scores) * factor
@@ -164,48 +162,66 @@
     return jnp.broadcast_to(valid, (counts.shape[0], seq, merge * seq))
 
 
-def attention_call(rows_fn, arrays, valid, seq, n_out, head_size, merge, flop_factor):
-    rows, width = arrays[0].shape
-    images = rows // seq
-    block = pl.BlockSpec((seq, width), lambda i: (i, 0))
-    out = jax.ShapeDtypeStruct((rows, width), BF16)
-    in_specs, masks = [block] * len(arrays), []
-    if valid is not None:
-        in_specs.append(pl.BlockSpec((None,) + valid.shape[1:], lambda i: (i, 0, 0)))
-        masks = [valid]
+def row_block(seq, width):
+    return pl.BlockSpec((seq, width), lambda i: (i, 0))
+
+
+def weight_block(seq, width, head_size):
+    merge = LANES // head_size
+    return pl.BlockSpec((None, width // LANES, seq, merge * seq), lambda i: (i, 0, 0, 0))
+
+
+def weight_shape(images, seq, width, head_size):
+    merge = LANES // head_size
+    return jax.ShapeDtypeStruct((images, width // LANES, seq, merge * seq), BF16)
+
+
+def attention_cost(rows, seq, width, head_size, shards, products, arrays):
+    merge = LANES // head_size
+    return pl.CostEstimate(
+        flops=2 * shards * products * rows * seq * width * merge,
+        bytes_accessed=2 * shards * rows * (arrays * width + seq * width // head_size),
+        transcendentals=shards * rows * seq * width // head_size,
+    )
+
+
+def attend(queries, keys, values, counts, seq, head_size, masked):
+    rows, width = queries.shape
+    images, merge = rows // seq, LANES // head_size
+    valid = [valid_rows(counts, seq, merge)] if masked else []
 
     def kernel(*refs):
-        refs = list(refs)
-        mask = refs.pop(len(arrays))[...] if masks else None
-        rows_fn(head_size, merge, *refs, mask)
+        mask = refs[3][...] if masked else None
+        attend_rows(head_size, merge, *refs[:3], *refs[3 + len(valid) :], mask)
 
     return pl.pallas_call(
         kernel,
         grid=(images,),
-        in_specs=in_specs,
-        out_specs=[block] * n_out,
-        out_shape=[out] * n_out,
-        compiler_params=pltpu.CompilerParams(vmem_limit_bytes=VMEM_LIMIT),
-        cost_estimate=pl.CostEstimate(
-            flops=flop_factor * rows * seq * width * (LANES // head_size),
-            bytes_accessed=(len(arrays) + n_out) * rows * width * 2,
-            transcendentals=rows * seq * width // head_size,
-        ),
-    )(*arrays, *masks)
-
-
-def attend(queries, keys, values, counts, seq, head_size, masked):
-    merge = LANES // head_size
-    valid = valid_rows(counts, seq, merge) if masked else None
-    arrays = [queries, keys, values]
-    return attention_call(attend_rows, arrays, valid, seq, 1, head_size, merge, 4)[0]
-
-
-def attend_back(queries, keys, values, grads, counts, seq, head_size, masked):
-    merge = 1 if masked else LANES // head_size
-    valid = valid_rows(counts, seq, merge) if masked else None
-    arrays = [queries, keys, values, grads]
-    return attention_call(attend_back_rows, arrays, valid, seq, 3, head_size, merge, 10)
+        in_specs=[row_block(seq, width)] * 3
+        + [pl.BlockSpec((None,) + v.shape[1:], lambda i: (i, 0, 0)) for v in valid],
+        out_specs=[row_block(seq, width), weight_block(seq, width, head_size)],
+        out_shape=[
+            jax.ShapeDtypeStruct((rows, width), BF16),
+            weight_shape(images, seq, width, head_size),
+        ],
+        compiler_params=pltpu.CompilerParams(vmem_limit_bytes=20 * MIB),
+        cost_estimate=attention_cost(rows, seq, width, head_size, 1, 2, 4),
+    )(queries, keys, values, *valid)
+
+
+def attend_back(queries, keys, values, weights, grads, seq, head_size):
+    rows, width = queries.shape
+    images, merge = rows // seq, LANES // head_size
+    return pl.pallas_call(
+        lambda *refs: attend_back_rows(head_size, merge, *refs),
+        grid=(images,),
+        in_specs=[row_block(seq, width)] * 3
+        + [weight_block(seq, width, head_size), row_block(seq, width)],
+        out_specs=[row_block(seq, width)] * 3,
+        out_shape=[jax.ShapeDtypeStruct((rows, width), BF16)] * 3,
+        compiler_params=pltpu.CompilerParams(vmem_limit_bytes=20 * MIB),
+        cost_estimate=attention_cost(rows, seq, width, head_size, 1, 4, 7),
+    )(queries, keys, values, weights, grads)
 
 
 def up_kernel(x_ref, w_ref, active_ref, slope_ref):
@@ -232,13 +248,39 @@
         ],
         out_specs=[spec, spec],
         out_shape=[out, out],
-        compiler_params=pltpu.CompilerParams(vmem_limit_bytes=VMEM_LIMIT),
+        compiler_params=pltpu.CompilerParams(vmem_limit_bytes=20 * MIB),
         cost_estimate=pl.CostEstimate(
             flops=2 * rows * depth * width,
             bytes_accessed=2 * (rows * depth + depth * width + 2 * rows * width),
             transcendentals=2 * rows * width,
         ),
     )(rows_in, weight)
+
+
+def product_kernel(left_ref, right_ref, out_ref):
+    out_ref[...] = dot(left_ref[...], right_ref[...]).astype(BF16)
+
+
+def row_product(left, right):
+    rows, depth = left.shape
+    width = right.shape[1]
+    block = math.gcd(rows, 512)
+    return pl.pallas_call(
+        product_kernel,
+        grid=(rows // block,),
+        in_specs=[
+            pl.BlockSpec((block, depth), lambda i: (i, 0)),
+            pl.BlockSpec((depth, width), lambda i: (0, 0)),
+        ],
+        out_specs=pl.BlockSpec((block, width), lambda i: (i, 0)),
+        out_shape=jax.ShapeDtypeStruct((rows, width), BF16),
+        compiler_params=pltpu.CompilerParams(vmem_limit_bytes=32 * MIB),
+        cost_estimate=pl.CostEstimate(
+            flops=2 * rows * depth * width,
+            bytes_accessed=2 * (rows * depth + depth * width + rows * width),
+            transcendentals=0,
+        ),
+    )(left, right)
 
 
 class Links:
@@ -290,8 +332,9 @@
 class Fetch:
     STEPS = 4
 
-    def __init__(self, sources, targets, send, recv):
+    def __init__(self, sources, targets, items, send, recv):
         self.sources, self.targets, self.send, self.recv = sources, targets, send, recv
+        self.items = items
         index, across = lax.axis_index("dp"), lax.axis_index("freq")
         core, row = index % 2, (index // 2) % 2
         self.quarter = index % 4
@@ -306,16 +349,18 @@
             pl.semaphore_signal(barrier, inc=1, device_id=partner, device_id_type=MESH)
         pl.semaphore_wait(barrier, 3)
 
-    def view(self, ref, quarter):
-        rows = ref.shape[-2] // 4
-        place = pl.ds(pl.multiple_of(quarter * rows, 16), rows)
+    def view(self, ref, quarter, part, parts):
+        rows = ref.shape[-2] // (4 * parts)
+        place = pl.ds(pl.multiple_of((quarter * parts + part) * rows, 16), rows)
         return ref.at[:, place] if len(ref.shape) == 3 else ref.at[place]
 
     def copy(self, i, step):
         quarter = self.next_quarter if step == 3 else self.quarter
-        target = self.view(self.targets[i], quarter)
+        array, part, parts = self.items[i]
+        target = self.view(self.targets[array], quarter, part, parts)
+        source = self.view(self.sources[array], quarter, part, parts)
         return pltpu.make_async_remote_copy(
-            src_ref=self.view(self.sources[i], quarter) if step == 0 else target,
+            src_ref=source if step == 0 else target,
             dst_ref=target,
             send_sem=self.send.at[step, i],
             recv_sem=self.recv.at[step, i],
@@ -339,7 +384,7 @@
             self.copy(i, 3).start()
 
     def finish(self):
-        for i in range(len(self.sources)):
+        for i in range(len(self.items)):
             for step in range(self.STEPS):
                 self.copy(i, step).wait_send()
                 if step >= 2:
@@ -349,7 +394,8 @@
 def head_start_kernel(rows_ref, qkv_ref, out_ref, cot_ref, head_ref, *refs):
     got_ref, new_qkv, new_out, partial_ref, tiles, sums = refs[:6]
     send, recv, row_send, row_recv, tile_sem, sum_sem = refs[6:]
-    fetch = Fetch([qkv_ref, out_ref], [new_qkv, new_out], send, recv)
+    items = [(0, 0, 1), (1, 0, 1)]
+    fetch = Fetch([qkv_ref, out_ref], [new_qkv, new_out], items, send, recv)
     fetch.greet()
     rows_copy = pltpu.make_async_remote_copy(
         src_ref=rows_ref,
@@ -431,7 +477,7 @@
             sem((2,)),
         ],
         compiler_params=pltpu.CompilerParams(
-            collective_id=2, has_side_effects=True, vmem_limit_bytes=VMEM_LIMIT
+            collective_id=2, has_side_effects=True, vmem_limit_bytes=20 * MIB
         ),
         cost_estimate=pl.CostEstimate(
             flops=2 * count * columns * width,
@@ -441,59 +487,116 @@
     )(rows, weight_qkv, weight_out, cotangent, head_weight)
 
 
+ATTEND_ITEMS = [(i, part, 2) for i in range(2) for part in range(2)]
+ATTEND_ITEMS += [(i, 0, 1) for i in range(2, 6)]
+
+
 def attend_fetch_kernel(head_size, merge, steps, *refs):
     own, other, valid_ref, sources = refs[:3], refs[3:6], refs[6], refs[7:13]
-    own_out, other_out, targets = refs[13], refs[14], refs[15:21]
-    send, recv = refs[21:]
-    fetch = Fetch(sources, targets, send, recv)
-
-    @pl.when(pl.program_id(0) == 0)
+    own_out, other_out, targets = refs[13:15], refs[15:17], refs[17:23]
+    send, recv = refs[23:]
+    fetch = Fetch(sources, targets, ATTEND_ITEMS, send, recv)
+    count, step = len(ATTEND_ITEMS), pl.program_id(0)
+
+    @pl.when(step == 0)
     def _():
         fetch.greet()
         fetch.start([0])
 
+    pl.when(step == steps // 2)(lambda: fetch.start([1]))
+
+    @pl.when(step == steps - 2)
+    def _():
+        fetch.pass_on([0])
+        fetch.start([2])
+
     valid = valid_ref[...]
-    attend_rows(head_size, merge, *own, own_out, valid)
-    attend_rows(head_size, merge, *other, other_out, valid)
-
-    @pl.when(pl.program_id(0) == steps - 1)
+    attend_rows(head_size, merge, *own, *own_out, valid)
+    attend_rows(head_size, merge, *other, *other_out, valid)
+
+    @pl.when(step == steps - 1)
     def _():
-        rest = list(range(2, 6))
-        fetch.pass_on([0])
-        fetch.start([1])
-        fetch.pass_on([1])
-        fetch.start(rest)
-        fetch.pass_on_last([0, 1])
-        fetch.pass_on(rest)
-        fetch.pass_on_last(rest)
+        for i in range(1, count):
+            fetch.pass_on([i])
+            fetch.start([i + 2] if i + 2 < count else [])
+            fetch.pass_on_last([i - 1])
+        fetch.pass_on_last([count - 1])
         fetch.finish()
 
 
 def attend_fetch(own, other, counts, seq, head_size, weights):
     rows, width = own[0].shape
     images, merge = rows // seq, LANES // head_size
-    block = pl.BlockSpec((seq, width), lambda i: (i, 0))
+    block = row_block(seq, width)
     hbm, sem = pl.BlockSpec(memory_space=pl.ANY), pltpu.SemaphoreType.DMA
     valid = valid_rows(counts, seq, merge)
-    out = jax.ShapeDtypeStruct((rows, width), BF16)
+    out = [
+        jax.ShapeDtypeStruct((rows, width), BF16),
+        weight_shape(images, seq, width, head_size),
+    ]
     return pl.pallas_call(
         lambda *refs: attend_fetch_kernel(head_size, merge, images, *refs),
         grid=(images,),
-        out_shape=[out, out] + [jax.ShapeDtypeStruct(w.shape, w.dtype) for w in weights],
+        out_shape=out * 2 + [jax.ShapeDtypeStruct(w.shape, w.dtype) for w in weights],
         in_specs=[block] * 6
         + [pl.BlockSpec((None,) + valid.shape[1:], lambda i: (i, 0, 0))]
         + [hbm] * len(weights),
-        out_specs=[block] * 2 + [hbm] * len(weights),
-        scratch_shapes=[sem((4, len(weights)))] * 2,
+        out_specs=[block, weight_block(seq, width, head_size)] * 2 + [hbm] * len(weights),
+        scratch_shapes=[sem((4, len(ATTEND_ITEMS)))] * 2,
         compiler_params=pltpu.CompilerParams(
-            collective_id=3, has_side_effects=True, vmem_limit_bytes=VMEM_LIMIT
+            collective_id=3, has_side_effects=True, vmem_limit_bytes=20 * MIB
         ),
-        cost_estimate=pl.CostEstimate(
-            flops=8 * rows * seq * width * merge,
-            bytes_accessed=16 * rows * width,
-            transcendentals=2 * rows * seq * width // head_size,
+        cost_estimate=attention_cost(rows, seq, width, head_size, 2, 2, 4),
+    )(*own, *other, valid, *weights)
+
+
+def attend_back_swap_kernel(head_size, merge, steps, *refs):
+    own, other, rows_ref = refs[:5], refs[5:10], refs[10]
+    own_out, other_out, got_ref = refs[11:14], refs[14:17], refs[17]
+    send, recv = refs[18:]
+    facing = (lax.axis_index("dp"), 1 - lax.axis_index("freq"))
+    swap = pltpu.make_async_remote_copy(
+        src_ref=rows_ref,
+        dst_ref=got_ref,
+        send_sem=send,
+        recv_sem=recv,
+        device_id=facing,
+        device_id_type=MESH,
+    )
+
+    @pl.when(pl.program_id(0) == 0)
+    def _():
+        barrier = pltpu.get_barrier_semaphore()
+        pl.semaphore_signal(barrier, inc=1, device_id=facing, device_id_type=MESH)
+        pl.semaphore_wait(barrier, 1)
+        swap.start()
+
+    attend_back_rows(head_size, merge, *own, *own_out)
+    attend_back_rows(head_size, merge, *other, *other_out)
+
+    @pl.when(pl.program_id(0) == steps - 1)
+    def _():
+        swap.wait()
+
+
+def attend_back_swap(own, other, seq, head_size, rows_out):
+    rows, width = own[0].shape
+    images, merge = rows // seq, LANES // head_size
+    block = row_block(seq, width)
+    hbm = pl.BlockSpec(memory_space=pl.ANY)
+    out = jax.ShapeDtypeStruct((rows, width), BF16)
+    return pl.pallas_call(
+        lambda *refs: attend_back_swap_kernel(head_size, merge, images, *refs),
+        grid=(images,),
+        out_shape=[out] * 6 + [jax.ShapeDtypeStruct(rows_out.shape, rows_out.dtype)],
+        in_specs=([block] * 3 + [weight_block(seq, width, head_size), block]) * 2 + [hbm],
+        out_specs=[block] * 6 + [hbm],
+        scratch_shapes=[pltpu.SemaphoreType.DMA] * 2,
+        compiler_params=pltpu.CompilerParams(
+            collective_id=4, has_side_effects=True, vmem_limit_bytes=28 * MIB
         ),
-    )(*own, *other, valid, *weights)
+        cost_estimate=attention_cost(rows, seq, width, head_size, 2, 4, 7),
+    )(*own, *other, rows_out)
 
 
 def whole_weight(weight, axis):
@@ -761,15 +864,6 @@
     return jnp.stack([total[i * depth : (i + 1) * depth] for i in range(3)], axis=1)
 
 
-def sum_small(links, values):
-    if links.fast:
-        values = values + links.over_x(values)
-        for bit in (1, 2, 4, 8):
-            values = values + links.over(bit, values)
-        return values
-    return lax.psum(values, ("dp", "freq"))
-
-
 def own_images(links, values):
     count = values.shape[0] // links.shards
     return lax.dynamic_slice_in_dim(values, links.place * count, count, 0)
@@ -800,8 +894,8 @@
         values = dot(normed, weight_qkv[2]).astype(BF16)
         heads.append((queries, keys, values))
     mixed = attend_all(heads)
-    heads = [(*head, mix) for head, mix in zip(heads, mixed)]
-    for (_, weight_out), mix in zip(attention, mixed):
+    heads = [(*head, weights, mix) for head, (mix, weights) in zip(heads, mixed)]
+    for (_, weight_out), (mix, _) in zip(attention, mixed):
         middle = middle + dot(mix, weight_out)
     normed_mid = layer_norm(middle, gains[1], biases[1])
     result = middle
@@ -813,9 +907,7 @@
     return result, (stream, normed, heads, middle, normed_mid, units)
 
 
-def block_backward(
-    grad, gains, attention, mlp, counts, seq, head_size, masked, saved
-):
+def block_backward(grad, gains, attention, mlp, attend_back_all, saved):
     stream, normed, heads, middle, normed_mid, units = saved
     low = grad.astype(BF16)
     down_grads, up_grads, grad_normed = [], [], 0.0
@@ -828,12 +920,14 @@
     grad = grad + grad_in
     low = grad.astype(BF16)
     out_grads, qkv_grads, grad_normed = [], [], 0.0
-    for (weight_qkv, weight_out), (queries, keys, values, mixed) in zip(attention, heads):
-        grad_mixed = dot_nt(low, weight_out).astype(BF16)
-        grads = attend_back(queries, keys, values, grad_mixed, counts, seq, head_size, masked)
+    grad_heads = [
+        (*head[:4], dot_nt(low, weight_out).astype(BF16))
+        for (_, weight_out), head in zip(attention, heads)
+    ]
+    for (weight_qkv, _), head, grads in zip(attention, heads, attend_back_all(grad_heads)):
         for i in range(3):
             grad_normed = grad_normed + dot_nt(grads[i], weight_qkv[i])
-        out_grads.append(dot_tn(mixed, low).astype(BF16))
+        out_grads.append(dot_tn(head[4], low).astype(BF16))
         qkv_grads.append([dot_tn(normed, grads[i]).astype(BF16) for i in range(3)])
     grad_in, first_gain, first_bias = layer_norm_back(grad_normed, stream, gains[0])
     return (
@@ -921,13 +1015,15 @@
             return [attend(*head, my_count, VIS, HDIM, True) for head in heads]
         weights = (*enc_mlp[0], *dec_attention[0], *dec_mlp[0])
         nonlocal grad_final
-        own_mix, other_mix, *others = attend_fetch(*heads, my_count, VIS, HDIM, weights)
+        own_mix, own_weights, other_mix, other_weights, *others = attend_fetch(
+            *heads, my_count, VIS, HDIM, weights
+        )
         keep, send = halves(lax.optimization_barrier((grad_partial, own_mix))[0], links.place, 0)
         grad_final = keep.astype(F32) + links.over_x(send).astype(F32)
         enc_mlp.append(tuple(others[:2]))
         dec_attention.append(tuple(others[2:4]))
         dec_mlp.append(tuple(others[4:]))
-        return own_mix, other_mix
+        return (own_mix, own_weights), (other_mix, other_weights)
 
     stream, enc_saved = block_forward(
         stream, enc_gains, enc_biases, enc_attention, lambda: enc_mlp, encoder_attention, HDIM
@@ -956,14 +1052,30 @@
     )
     final_own = layer_norm(decoded, dec_gains[2], dec_biases[2])
 
-    final_all = gather_rows(links, final_own)
-    reconstructions = dot(final_all, head_weight).astype(BF16).reshape(images, NPATCH, -1)
-    head_grad = dot_tn(final_all, cotangent).astype(BF16)
-
+    final_other = None
+
+    def decoder_attention_back(heads):
+        nonlocal final_other
+        if not links.fast:
+            return [attend_back(*head, NPATCH, DHDIM) for head in heads]
+        *grads, final_other = attend_back_swap(*heads, NPATCH, DHDIM, final_own)
+        return grads[:3], grads[3:]
+
+    encoder_attention_back = lambda heads: [attend_back(*head, VIS, HDIM) for head in heads]
     grad_in, dec_gain_2, dec_bias_2 = layer_norm_back(grad_final, decoded, dec_gains[2])
     grad_decoded, dec_gain_01, dec_bias_01, dec_grads = block_backward(
-        grad_in, dec_gains, dec_attention, dec_mlp, my_count, NPATCH, DHDIM, False, dec_saved
-    )
+        grad_in, dec_gains, dec_attention, dec_mlp, decoder_attention_back, dec_saved
+    )
+
+    if links.fast:
+        final_all = ordered(links.place, final_own, final_other, 0)
+    else:
+        final_all = gather_rows(links, final_own)
+    reconstructions = row_product(final_all, head_weight).reshape(images, NPATCH, -1)
+    head_grad = dot_tn(final_all, cotangent).astype(BF16)
+    grad_decoded, head_grad = lax.optimization_barrier((grad_decoded, head_grad))
+    head_total = lax.psum(head_grad, "dp").astype(F32)
+
     grad_grid = grad_decoded.reshape(own, NPATCH, DDEC)
     mask_grad = jnp.sum(hidden * grad_grid, axis=(0, 1))
     grad_lifted = (
@@ -981,7 +1093,7 @@
 
     grad_in, enc_gain_2, enc_bias_2 = layer_norm_back(grad_latent, stream, enc_gains[2])
     grad_stream, enc_gain_01, enc_bias_01, enc_grads = block_backward(
-        grad_in, enc_gains, enc_attention, enc_mlp, my_count, VIS, HDIM, True, enc_saved
+        grad_in, enc_gains, enc_attention, enc_mlp, encoder_attention_back, enc_saved
     )
 
     grad_embedded = gather_rows(links, grad_stream.astype(BF16))
@@ -1017,18 +1129,32 @@
         (dec_down_grads, 0),
     ]
     patch_grad = jnp.concatenate(patch_grads, 0)
+    small = [*enc_gain_01, enc_gain_2, *enc_bias_01, enc_bias_2]
+    small += [*dec_gain_01, dec_gain_2, *dec_bias_01, dec_bias_2, mask_grad]
+    small = jnp.concatenate(small)
     if links.fast:
-        stacks = [grads for grads, _ in enc_stack[:3] + dec_stack]
-        enc_last = enc_stack[3][0]
-        late = [grads[0] for grads in stacks] + [embed_grad, enc_last[0], head_grad, patch_grad]
+        small_rows = small.shape[0] // DDEC
+        shared_rows = -(-(D + small_rows) // 256) * 256
+        shared = jnp.concatenate([embed_grad, small.reshape(small_rows, DDEC).astype(BF16)], 0)
+        shared = jnp.pad(shared, ((0, shared_rows - D - small_rows), (0, 0)))
+        enc_qkv_pair, enc_out_pair, enc_up_pair, enc_down_pair = [g for g, _ in enc_stack]
+        crossing = [enc_qkv_pair, enc_up_pair] + [g for g, _ in dec_stack]
+        late = [pair[0] for pair in crossing]
+        late += [shared, enc_out_pair[0], enc_down_pair[0], patch_grad]
         late = ring_sums(
-            late, [grads[1] for grads in stacks] + [embed_grad], {8: enc_last[1]}, {10}
-        )
-        late = [total.astype(F32) for total in late]
-        enc_totals = [unstack_qkv(late[0]), late[1], late[2], late[8]]
-        dec_totals = [unstack_qkv(late[3])] + late[4:7]
-        embed_total, head_total = late[7], late[9]
-        patch_total = jnp.pad(late[10], ((0, pixel_width - rgb_width), (0, 0)))
+            late,
+            [pair[1] for pair in crossing] + [shared],
+            {7: enc_out_pair[1], 8: enc_down_pair[1]},
+            {9},
+        )
+        late, patch_total = [total.astype(F32) for total in late[:9]], late[9]
+        enc_totals = [unstack_qkv(late[0]), late[7], late[1], late[8]]
+        dec_totals = [unstack_qkv(late[2])] + late[3:6]
+        embed_total = late[6][:D]
+        small = late[6][D : D + small_rows].reshape(-1)
+        patch_total = lax.pad(
+            patch_total.astype(F32), 0.0, ((0, pixel_width - rgb_width, 0), (0, 0, 0))
+        )
         patch_total = patch_total.reshape(2, pixel_width, D)
     else:
         reduced = []
@@ -1042,7 +1168,7 @@
             reduced.append(parts)
         dec_totals, enc_totals = reduced
         embed_total = lax.psum(embed_grad, ("dp", "freq")).astype(F32)
-        head_total = lax.psum(head_grad, "dp").astype(F32)
+        small = lax.psum(small, ("dp", "freq"))
         patch_sum = lax.psum(patch_grad, "dp").astype(F32)
         patch_total = jnp.stack(
             [
@@ -1050,9 +1176,6 @@
                 jnp.pad(patch_sum[pixel_width:], ((0, pixel_width - rgb_width), (0, 0))),
             ]
         )
-    small = [*enc_gain_01, enc_gain_2, *enc_bias_01, enc_bias_2]
-    small += [*dec_gain_01, dec_gain_2, *dec_bias_01, dec_bias_2, mask_grad]
-    small = sum_small(links, jnp.concatenate(small).reshape(-1, LANES)).reshape(-1)
     enc_end, dec_end = 6 * D, 6 * D + 6 * DDEC
     enc_small = small[:enc_end].reshape(2, 3, D)
     dec_small = small[enc_end:dec_end].reshape(2, 3, DDEC)

time: 972 us -> 949 us (0.976)
  waiting for transfers between devices: 43.9 us -> 0.02 us
  local copies, waits for them, and re-layouts: 42.1 us -> 83.5 us
  matrix products: 256 us -> 222 us
  between operations: 3.38 us -> 16.7 us
    unnamed x317 -> x423, local copies, waits for them, and re-layouts: 23.2 us -> 65.9 us
    ppermute x4 -> x2, waiting for transfers between devices: 40 us -> 0.01 us  [over_x(): return lax.ppermute(values, 'freq', [(0, 1), (1, 0)])]
    dot_general x24 -> x23, matrix products: 71.1 us -> 36.3 us  [dot(): return jnp.dot(left, right, preferred_element_type=F32)]
    pallas_call x6, Pallas kernels: 79.7 us -> 103 us  [the longest x1 49.4 us: attend_back_swap(): pl.pallas_call(lambda *refs: attend_back_swap_kernel(head_size, merge, im...]
    pallas_call x1, Pallas kernels: 91.9 us -> 79.4 us  [attend_fetch(): pl.pallas_call(lambda *refs: attend_fetch_kernel(head_size, merge, images...]
  transfers between devices with their start and end apart: 8 -> 3, of which waited for: 5 -> 0; matrix products, arithmetic and copies ran while one was open for 10% -> 13% of each run, Pallas kernels for 5% -> 36%
where the time goes in v3:
time: 949 us; the launch traced here: 942 us
  Pallas kernels  536 us (56%)
  matrix products  222 us (23%)
  local copies, waits for them, and re-layouts  83.5 us (9%)
  other arithmetic  81.6 us (9%)
  between operations  16.7 us (2%)
    pallas_call x1, Pallas kernels, ring_sums(): pl.pallas_call(lambda *refs: ring_kernel(shapes[:total], crossing, pairs,...  279 us
    dot_general x28, matrix products, dot_tn(): lax.dot_general(left, right, (((0,), (0,)), ((), ())), preferred_element_...  89.8 us
    pallas_call x1, Pallas kernels, attend_fetch(): pl.pallas_call(lambda *refs: attend_fetch_kernel(head_size, merge, images...  79.4 us
    dot_general x27, matrix products, dot_nt(): lax.dot_general(left, right, (((1,), (1,)), ((), ())), preferred_element_...  72 us
    unnamed x423, local copies, waits for them, and re-layouts  65.9 us
    pallas_call x1, Pallas kernels, head_start(): pl.pallas_call(head_start_kernel, out_shape=[shape(rows), shape(weight_qk...  50.7 us
    pallas_call x1, Pallas kernels, attend_back_swap(): pl.pallas_call(lambda *refs: attend_back_swap_kernel(head_size, merge, im...  49.4 us
    dot_general x23, matrix products, dot(): return jnp.dot(left, right, preferred_element_type=F32)  36.3 us
  transfers between devices with their start and end apart: 3, of which 0 were waited for; matrix products, arithmetic and copies ran while one was open for 13% of the time, Pallas kernels for 36%

profile of v3, /device:TPU:0, one launch (start us, length us, event | category | flops | bytes accessed | tf_op | source)
XLA Modules:
  0.0 942.2 jit_solution(4963340138940633940)
XLA Ops:
  8.7 3.4 slice_bitcast_fusion.5
  12.2 7.3 broadcast_select_fusion
  21.9 3.9 fusion.19
  30.9 50.7 %shard_map.349 = (bf16[512,1024]{1,0:T(8,128)(2,1)S(1)}, bf16[3,1024,512]{2,1,0:T(8,128)(2,1)S(1)}, bf16[512,1024]{1,0:T(8,128)(2,1)S(1)}, bf16[4096,512]{1,0:T(8,128)(2,1)S(1)}) custom-call(bf16[512,1024]{1,0:T(8,128)(2,1)S(1)} %dynamic-slice_convert_fusion.rows_ref, bf16[3,1024,512]{2,1,0:T(8,128)(2,1)S(1)} %pad_maximum_fusion.3.qkv_ref, ...), custom_call_target="tpu_custom_call" | custom-call | flops 13958643712 | bytes 27262976 | tf_op jit(solution)/shard_map/pallas_call | solution.py:459
  100.9 79.4 %shard_map.350 = (bf16[512,512]{1,0:T(8,128)(2,1)S(1)}, bf16[8,4,64,128]{3,2,1,0:T(8,128)(2,1)S(1)}, bf16[512,512]{1,0:T(8,128)(2,1)S(1)}, bf16[8,4,64,128]{3,2,...) custom-call(bf16[512,512]{1,0:T(8,128)(2,1)S(1)} %fusion.31.refs_0_,, ...), custom_call_target="tpu_custom_call" | custom-call | flops 268435456 | bytes 5242880 | tf_op jit(solution)/shard_map/pallas_call | solution.py:537
  191.2 3.2 constant_dynamic-slice_fusion
  199.4 5.2 shard_map.351
  204.7 2.4 fusion.135
  208.4 4.8 shard_map.352
  213.2 2.5 fusion.130
  219.1 3.2 fusion.131
  238.8 10.3 %shard_map.353 = (bf16[2048,256]{1,0:T(8,128)(2,1)S(1)}, bf16[8,2,256,1024]{3,2,1,0:T(8,128)(2,1)S(1)}) custom-call(bf16[2048,256]{1,0:T(8,128)(2,1)S(1)} %copy-done.90, bf16[2048,256]{1,0:T(8,128)(2,1)S(1)} %copy-done.81, bf16[2048,256]{1,0:T(8,128)(2,1)S(1)} %copy-done.79), custom_call_target="tpu_custom_call" | custom-call | flops 2147483648 | bytes 12582912 | tf_op jit(solution)/shard_map/pallas_call | solution.py:197
  249.2 3.4 copy-done.96
  255.4 10.3 %shard_map.354 = (bf16[2048,256]{1,0:T(8,128)(2,1)S(1)}, bf16[8,2,256,1024]{3,2,1,0:T(8,128)(2,1)S(1)}) custom-call(bf16[2048,256]{1,0:T(8,128)(2,1)S(1)} %copy-done.88, bf16[2048,256]{1,0:T(8,128)(2,1)S(1)} %copy-done.77, bf16[2048,256]{1,0:T(8,128)(2,1)S(1)} %copy-done.75), custom_call_target="tpu_custom_call" | custom-call | flops 2147483648 | bytes 12582912 | tf_op jit(solution)/shard_map/pallas_call | solution.py:197
  266.7 2.8 copy-done.97
  271.4 7.0 shard_map.355
  282.5 7.2 shard_map.356
  294.6 4.7 fusion.138
  299.6 2.8 fusion.133
  304.6 4.6 multiply_reduce_fusion.1
  309.2 4.4 fusion.121
  313.6 4.5 multiply_convert_fusion
  318.2 2.4 multiply_convert_fusion.1
  320.6 4.5 fusion.139
  326.1 6.1 multiply_reduce_fusion.2
  332.3 3.3 fusion.120
  339.1 49.4 %shard_map.357 = (bf16[2048,256]{1,0:T(8,128)(2,1)S(1)}, bf16[2048,256]{1,0:T(8,128)(2,1)S(1)}, bf16[2048,256]{1,0:T(8,128)(2,1)S(1)}, bf16[2048,256]{1,0:T(8,12...) custom-call(bf16[2048,256]{1,0:T(8,128)(2,1)S(1)} %copy-done.91, ...), custom_call_target="tpu_custom_call" | custom-call | flops 8589934592 | bytes 31457280 | tf_op jit(solution)/shard_map/pallas_call | solution.py:588
  388.6 2.8 fusion.75
  391.3 2.7 fusion.72
  394.1 2.7 fusion.78
  396.8 2.8 fusion.81
  399.6 2.8 fusion.84
  403.0 10.6 %multiply_reduce_fusion.3 = (bf16[512]{0:T(512)(128)(2,1)S(1)}, f32[2048]{0:T(1024)S(1)}, f32[2048]{0:T(1024)S(1)}, bf16[512]{0:T(512)(128)(2,1)S(1)}, bf16[2048,512]{1,0:T(8,128)(2,1)S(1)}, /*index=5*/f32[2048,512]{1,0:T(8,128)}) fusion(f32[8,256,512]{2,1,0:T(8,128)S(1)} %copy-done.108, f32[2048]{0:T(1024)S(1)} %bitcast.367, f32[2048]{0:T(1024)S(1)} %bitcast.365, ...), kind=kOutput, calls=%fused_computation.18 | convolution fusion | flops 554691584 | bytes 32806912 | tf_op jit(solution)/shard_map/dot_general | solution.py:39
  418.7 22.2 %convolution_convert_fusion = bf16[512,3328]{1,0:T(8,128)(2,1)} fusion(bf16[4096,512]{1,0:T(8,128)(2,1)S(1)} %maximum_select_fusion.left_ref, bf16[4096,3328]{1,0:T(8,128)(2,1)} %bitcast.396), kind=kOutput, calls=%fused_computation.4 | convolution fusion | flops 13960347648 | bytes 34865152 | tf_op jit(solution)/shard_map/dot_general | solution.py:35
  442.8 5.7 multiply_add_fusion
  454.2 2.4 multiply_convert_fusion.2
  457.1 2.4 multiply_convert_fusion.3
  459.6 2.4 fusion.140
  462.4 3.1 multiply_reduce_fusion.13
  468.5 8.0 shard_map.360
  481.5 4.4 convolution_convert_fusion.1
  486.0 4.4 convolution_convert_fusion.4
  490.4 4.4 convolution_convert_fusion.2
  504.8 4.4 convolution_convert_fusion.5
  509.3 8.0 shard_map.359
  525.4 3.4 convolution_convert_fusion.24
  530.4 3.4 convolution_convert_fusion.25
  533.8 3.3 convolution_convert_fusion.23
  537.1 3.4 convolution_convert_fusion.26
  560.0 17.3 %shard_map.358 = bf16[4096,3328]{1,0:T(8,128)(2,1)} custom-call(bf16[4096,512]{1,0:T(8,128)(2,1)S(1)} %copy-done.13, bf16[512,3328]{1,0:T(8,128)(2,1)S(1)} %copy-done.69), custom_call_target="tpu_custom_call" | custom-call | flops 13958643712 | bytes 34865152 | tf_op jit(solution)/shard_map/pallas_call | solution.py:268
  577.4 6.0 convolution_convert_fusion.3
  583.4 3.5 convolution_convert_fusion.13
  587.0 2.8 pad_maximum_fusion.1
  589.8 278.6 %shard_map.361 = (bf16[16,192,512]{2,1,0:T(8,128)(2,1)}, bf16[16,64,2048]{2,1,0:T(8,128)(2,1)}, bf16[16,96,256]{2,1,0:T(8,128)(2,1)}, bf16[16,16,512]{2,1,0:T(8,...) custom-call(bf16[16,192,512]{2,1,0:T(8,128)(2,1)} %bitcast.330, ...), custom_call_target="tpu_custom_call" | custom-call | flops 22020096 | bytes 66060288 | tf_op jit(solution)/shard_map/pallas_call | solution.py:844
  875.0 2.8 slice_bitcast_fusion.2
  878.6 6.8 convert.68
  885.5 4.7 bitcast_convert_fusion
  891.4 3.0 bitcast_convert_fusion.4
  899.9 3.4 pad_maximum_fusion
  903.5 3.6 fusion.22
  907.1 6.0 add_convert_fusion
  913.2 4.7 bitcast_convert_fusion.1
  917.9 11.6 %fusion.52 = f32[16,256,1664]{2,1,0:T(8,128)} fusion(bf16[16,64,1664]{2,1,0:T(8,128)(2,1)S(1)} %bitcast.335, s32[16,64]{1,0:T(8,128)S(1)} %copy-done.161), kind=kOutput, calls=%fused_computation.179 | convolution fusion | flops 872677376 | bytes 30674944 | tf_op jit(solution)/shard_map/bsp,bsc->bpc/dot_general | solution.py:1109
  929.6 5.3 convert_element_type.421
  (578 shorter events, 161.6 us)
Async XLA Ops:
  7.2 209.9 %copy-start = (bf16[1024,512]{1,0:T(8,128)(2,1)S(1)}, bf16[1024,512]{1,0:T(8,128)(2,1)}, u32[]{:S(2)}) copy-start(bf16[1024,512]{1,0:T(8,128)(2,1)} %param.34) | copy-start | bytes 3145732
  7.2 922.4 %all-reduce.5.cloned.1.call-start = ((), (), s32[]{:S(2)}) async-start(), calls=%async_computation | async-start | bytes 6815744 | tf_op jit(solution)/shard_map/psum | solution.py:1077
  7.3 4.8 copy-start.188
  12.2 7.5 copy-start.193
  30.9 55.3 %copy-start.135 = (f32[1024,1024]{1,0:T(8,128)S(1)}, f32[1024,1024]{1,0:T(8,128)}, u32[]{:S(2)}) copy-start(f32[1024,1024]{1,0:T(8,128)} %copy-done.134) | copy-start | bytes 12582916
  89.9 107.0 %copy-start.167 = (f32[1,1024]{1,0:T(1,128)}, f32[1,1024]{1,0:T(1,128)S(1)}, u32[]{:S(2)}) copy-start(f32[1,1024]{1,0:T(1,128)S(1)} %get-tuple-element.186) | copy-start | bytes 12292
  89.9 126.7 %copy-start.169 = (f32[1,1024]{1,0:T(1,128)}, f32[1,1024]{1,0:T(1,128)S(1)}, u32[]{:S(2)}) copy-start(f32[1,1024]{1,0:T(1,128)S(1)} %get-tuple-element.184) | copy-start | bytes 12292
  90.6 6.3 copy-start.144
  93.2 5.0 copy-start.26
  93.9 4.3 copy-start.28
  97.8 82.6 %copy-start.24 = (bf16[512,512]{1,0:T(8,128)(2,1)}, bf16[512,512]{1,0:T(8,128)(2,1)S(1)}, u32[]{:S(2)}) copy-start(bf16[512,512]{1,0:T(8,128)(2,1)S(1)} %fusion.31.refs_0_) | copy-start | bytes 1572868
  191.2 4.4 copy-start.40
  191.2 4.4 copy-start.58
  191.2 4.4 copy-start.112
  194.4 108.9 %collective-permute-start = (bf16[2048,512]{1,0:T(8,128)(2,1)}, bf16[2048,512]{1,0:T(8,128)(2,1)}, u32[]{:S(2)}, u32[]{:S(2)}) collective-permute-start(bf16[2048,512]{1,0:T(8,128)(2,1)} %constant_dynamic-slice_fusion), channel_id=1, source_target_pairs={{0,1},{1,0},{2,3},{3,2},{4,5},{5,4},{6,7},{7,6},{8,9},{9,8},{10,11... | collective-permute-start | bytes 6291464 | tf_op jit(solution)/shard_map/ppermute | solution.py:304
  196.5 16.7 %copy-start.116 = (f32[512,1024]{1,0:T(8,128)}, f32[512,1024]{1,0:T(8,128)S(1)}, u32[]{:S(2)}) copy-start(f32[512,1024]{1,0:T(8,128)S(1)} %get-tuple-element.213) | copy-start | bytes 6291460
  196.5 8.1 copy-start.171
  196.8 7.8 copy-start.177
  199.4 7.7 copy-start.44
  199.4 5.3 copy-start.7
  208.4 4.8 copy-start.66
  255.4 10.4 %copy-start.47 = (bf16[256,512]{1,0:T(8,128)(2,1)S(1)}, bf16[256,512]{1,0:T(8,128)(2,1)}, u32[]{:S(2)}) copy-start(bf16[256,512]{1,0:T(8,128)(2,1)} %copy-done.46) | copy-start | bytes 786436
  255.4 10.4 %copy-start.107 = (f32[8,256,512]{2,1,0:T(8,128)S(1)}, f32[8,256,512]{2,1,0:T(8,128)}, u32[]{:S(2)}) copy-start(f32[8,256,512]{2,1,0:T(8,128)} %copy-done.106) | copy-start | bytes 12582916
  271.4 11.1 %copy-start.32 = (bf16[2048,512]{1,0:T(8,128)(2,1)}, bf16[2048,512]{1,0:T(8,128)(2,1)S(1)}, u32[]{:S(2)}) copy-start(bf16[2048,512]{1,0:T(8,128)(2,1)S(1)} %add_convert_fusion.3.x_ref) | copy-start | bytes 6291460
  271.4 11.1 %copy-start.71 = (bf16[512,1024]{1,0:T(8,128)(2,1)S(1)}, bf16[512,1024]{1,0:T(8,128)(2,1)}, u32[]{:S(2)}) copy-start(bf16[512,1024]{1,0:T(8,128)(2,1)} %copy-done.70) | copy-start | bytes 3145732
  294.6 4.7 copy-start.74
  294.6 4.7 copy-start.84
  294.6 5.0 copy-start.115
  309.2 4.4 copy-start.95
  313.6 4.6 copy-start.137
  313.6 4.5 copy-start.93
  320.6 4.6 copy-start.196
  320.6 4.6 copy-start.72
  320.6 5.5 copy-start.198
  339.1 49.4 %copy-start.51 = (bf16[3,512,256]{2,1,0:T(8,128)(2,1)S(1)}, bf16[3,512,256]{2,1,0:T(8,128)(2,1)}, u32[]{:S(2)}) copy-start(bf16[3,512,256]{2,1,0:T(8,128)(2,1)} %copy-done.49) | copy-start | bytes 2359300
  388.6 11.0 %copy-start.4 = (bf16[2048,256]{1,0:T(8,128)(2,1)}, bf16[2048,256]{1,0:T(8,128)(2,1)S(1)}, u32[]{:S(2)}) copy-start(bf16[2048,256]{1,0:T(8,128)(2,1)S(1)} %get-tuple-element.100) | copy-start | bytes 3145732
  467.7 8.8 copy-start.145
  468.5 9.8 %copy-start.18 = (bf16[3,1024,512]{2,1,0:T(8,128)(2,1)S(1)}, bf16[3,1024,512]{2,1,0:T(8,128)(2,1)}, u32[]{:S(2)}) copy-start(bf16[3,1024,512]{2,1,0:T(8,128)(2,1)} %copy-done.16) | copy-start | bytes 9437188
  481.5 4.4 copy-start.99
  486.0 4.4 copy-start.101
  490.4 4.4 copy-start.59
  490.4 6.1 copy-start.56
  504.8 4.5 copy-start.21
  504.8 4.5 copy-start.23
  504.8 4.5 copy-start.25
  504.8 4.5 copy-start.53
  504.8 12.4 %copy-start.123 = (bf16[1024,3,512]{2,0,1:T(8,128)(2,1)S(1)}, bf16[1024,3,512]{2,0,1:T(8,128)(2,1)}, u32[]{:S(2)}) copy-start(bf16[1024,3,512]{2,0,1:T(8,128)(2,1)} %param.28) | copy-start | bytes 9437188
  525.4 4.8 copy-start.87
  546.4 37.0 %copy-start.148 = (bf16[512,1024]{1,0:T(8,128)(2,1)}, bf16[512,1024]{1,0:T(8,128)(2,1)S(1)}, u32[]{:S(2)}) copy-start(bf16[512,1024]{1,0:T(8,128)(2,1)S(1)} %add_convert_fusion.5) | copy-start | bytes 3145732
  546.4 30.9 %collective-permute-start.1 = (bf16[512,1024]{1,0:T(8,128)(2,1)S(1)}, bf16[512,1024]{1,0:T(8,128)(2,1)}, u32[]{:S(2)}, u32[]{:S(2)}) collective-permute-start(bf16[512,1024]{1,0:T(8,128)(2,1)S(1)} %add_convert_fusion.5), channel_id=1, source_target_pairs={{0,1},{1,0},{2,3},{3,2},{4,5},{5,4},{6,7},{7,6},{8,9},{9,8},{10,11... | collective-permute-start | bytes 3145736 | tf_op jit(solution)/shard_map/ppermute | solution.py:304
  550.8 4.1 copy-start.156
  550.8 4.1 copy-start.157
  550.8 4.1 copy-start.158
  553.0 5.3 copy-start.69
  560.0 17.3 %copy-start.125 = (bf16[16,64,1664]{2,1,0:T(8,128)(2,1)S(1)}, bf16[16,64,1664]{2,1,0:T(8,128)(2,1)}, u32[]{:S(2)}) copy-start(bf16[16,64,1664]{2,1,0:T(8,128)(2,1)} %copy-done.124) | copy-start | bytes 10223620
  577.4 6.1 copy-start.140
  868.4 4.4 copy-start.159
  878.6 6.8 copy-start.129
  891.4 4.6 copy-start.141
  894.4 4.2 copy-start.136
  896.0 7.2 slice-start.3
  907.1 6.1 copy-start.128
  913.2 4.8 copy-start.161
  917.9 17.0 %copy-start.1 = (bf16[1024,512]{1,0:T(8,128)(2,1)S(1)}, bf16[1024,512]{1,0:T(8,128)(2,1)}, u32[]{:S(2)}) copy-start(bf16[1024,512]{1,0:T(8,128)(2,1)} %param.34) | copy-start | bytes 3145732
  (144 other events, 339.4 us)
Sparse Core Ops, SparseCore 0:
  549.7 113.6 all-reduce.4
